TPU v7x, 128 devices: a whole 4x4x4 slice. The times are simulated.
128 devices in a mesh: row: 8 (over x_hi, z), col: 16 (over y, x_lo, core).
Axes of the slice: x: 4 (x_hi: 2, x_lo: 2; x = x_hi * 2 + x_lo), y: 4, z: 4, core: 2. Of those that a mesh axis runs over, the one named last changes fastest.
Arguments:
- inputs: bfloat16 [2048, 12288], P('col', 'row'), may hold values from -0.125 to 0.125
- weight: bfloat16 [12288, 49152], P('row', 'col'), may hold values from -0.02734375 to 0.02734375
- grad_out: bfloat16 [2048, 49152], P('row', 'col'), may hold values from -8 to 8
Outputs:
- input_grad: bfloat16 [2048, 12288], P('col', 'row')
- weight_grad: bfloat16 [12288, 49152], P('row', 'col')
All inputs are finite; a program needn't handle non-finite values.
Results may differ from a plain program's by a relative error of at most 0.001.
Values may be sent and summed in bfloat16 or wider, within the bound.
No kernel may reach another device: no remote copies, remote signals or barrier semaphores. Data moves between devices by JAX's collectives and lax.ppermute only.
A program may use at most 128 MiB of HBM per device.

v0:
```python
import jax
import jax.numpy as jnp
from jax import lax
from jax.sharding import PartitionSpec as P


def contract_tokens(left, right):
    return lax.dot_general(
        left, right, (((0,), (0,)), ((), ())), preferred_element_type=jnp.float32
    )


def contract_units(left, right):
    return lax.dot_general(
        left, right, (((1,), (1,)), ((), ())), preferred_element_type=jnp.float32
    )


def local(inputs, weight, grad_out):
    grads = lax.all_gather(grad_out, "row", axis=0, tiled=True)
    acts = lax.all_gather(inputs, "col", axis=0, tiled=True)
    weight_grad = contract_tokens(acts, grads).astype(jnp.bfloat16)
    partial_value = contract_units(grads, weight)
    input_grad = lax.psum_scatter(partial_value, "col", scatter_dimension=0, tiled=True).astype(
        jnp.bfloat16
    )
    return (input_grad, weight_grad)


def solution(mesh):
    placed = (P("col", "row"), P("row", "col"), P("row", "col"))
    return jax.shard_map(
        local,
        mesh=mesh,
        in_specs=placed,
        out_specs=(P("col", "row"), P("row", "col")),
        check_vma=False,
    )
```

profile of v0, /device:TPU:0, one launch (start us, length us, event | category | flops | bytes accessed | tf_op | source)
XLA Modules:
  0.0 351.6 jit_solution(12907540277592048849)
XLA Ops:
  7.2 0.0 all-gather.3.cloned.1.call-start
  7.2 0.7 all-gather.3.cloned.1.call-update
  7.9 0.0 all-gather.5.cloned.1.call-start
  7.9 0.7 all-gather.5.cloned.1.call-update
  8.6 0.0 reduce-scatter.2.cloned.1.call-start
  8.7 149.2 %all-gather.3.cloned.1.call-done = bf16[2048,3072]{1,0:T(8,128)(2,1)} async-done(((bf16[256,3072]{1,0:T(8,128)(2,1)}), bf16[2048,3072]{1,0:T(8,128)(2,1)}) %all-gather.3.cloned.1.call-update) | async-done | bytes 12582928 | tf_op jit(solution)/shard_map/all_gather | solution.py:20
  157.9 26.6 %fusion = f32[2048,1536]{1,0:T(8,128)} fusion(bf16[2048,3072]{1,0:T(8,128)(2,1)} %all-gather.3.cloned.1.call-done, bf16[1536,3072]{1,0:T(8,128)(2,1)} %param.4), kind=kOutput, calls=%fused_computation.1 | convolution fusion | flops 19327352832 | bytes 34603008 | tf_op jit(solution)/shard_map/dot_general | solution.py:14
  184.5 0.0 reduce-scatter.2.cloned.1.call-update
  184.5 15.1 %all-gather.5.cloned.1.call-done = bf16[2048,1536]{1,0:T(8,128)(2,1)} async-done(((bf16[128,1536]{1,0:T(8,128)(2,1)}), bf16[2048,1536]{1,0:T(8,128)(2,1)}) %all-gather.5.cloned.1.call-update) | async-done | bytes 6291472 | tf_op jit(solution)/shard_map/all_gather | solution.py:21
  199.7 25.7 %convolution_convert_fusion = bf16[1536,3072]{1,0:T(8,128)(2,1)} fusion(bf16[2048,1536]{1,0:T(8,128)(2,1)} %all-gather.5.cloned.1.call-done, bf16[2048,3072]{1,0:T(8,128)(2,1)} %all-gather.3.cloned.1.call-done), kind=kOutput, calls=%fused_computation | convolution fusion | flops 19332071424 | bytes 28311552 | tf_op jit(solution)/shard_map/dot_general | solution.py:8
  225.4 117.7 %reduce-scatter.2.cloned.1.call-done = f32[128,1536]{1,0:T(8,128)} async-done(((f32[2048,1536]{1,0:T(8,128)}), f32[128,1536]{1,0:T(8,128)}) %reduce-scatter.2.cloned.1.call-update) | async-done | bytes 786448 | tf_op jit(solution)/shard_map/reduce_scatter | solution.py:24
  343.1 1.9 convert_element_type.6
Async XLA Ops:
  7.2 150.8 %all-gather.3.cloned.1.call-start = ((), (), s32[]{:S(2)}) async-start(), calls=%async_computation.1 | async-start | bytes 14155776 | tf_op jit(solution)/shard_map/all_gather | solution.py:20
  7.9 191.8 %all-gather.5.cloned.1.call-start = ((), (), s32[]{:S(2)}) async-start(), calls=%async_computation.3 | async-start | bytes 6684672 | tf_op jit(solution)/shard_map/all_gather | solution.py:21
  8.6 334.5 %reduce-scatter.2.cloned.1.call-start = ((), (), s32[]{:S(2)}) async-start(), calls=%async_computation.2 | async-start | bytes 13369344 | tf_op jit(solution)/shard_map/reduce_scatter | solution.py:24
Sparse Core Ops, SparseCore 0:
  10.3 147.5 all-gather.2
  159.6 40.0 all-gather.4
  202.1 140.9 reduce-scatter.1
where the time goes:
time: 352 us
  waiting for transfers between devices  283 us (80%)
  matrix products  52.3 us (15%)
  between operations  13.7 us (4%)
    all_gather x1, waiting for transfers between devices, local(): grads = lax.all_gather(grad_out, 'row', axis=0, tiled=True)  149 us
    reduce_scatter x1, waiting for transfers between devices, local(): lax.psum_scatter(partial_value, 'col', scatter_dimension=0, tiled=True)  118 us
    dot_general x1, matrix products, contract_units(): lax.dot_general(left, right, (((1,), (1,)), ((), ())), preferred_element_...  26.6 us
    dot_general x1, matrix products, contract_tokens(): lax.dot_general(left, right, (((0,), (0,)), ((), ())), preferred_element_...  25.7 us
    all_gather x1, waiting for transfers between devices, local(): acts = lax.all_gather(inputs, 'col', axis=0, tiled=True)  15.1 us
  transfers between devices with their start and end apart: 3, of which 3 were waited for; matrix products, arithmetic and copies ran while one was open for 15% of the time, Pallas kernels for 0%

commit v1 on v0

v1 whole, which is shorter than its diff:
```python
import functools

import jax
import jax.numpy as jnp
from jax import lax
from jax.experimental import pallas as pl
from jax.experimental.pallas import tpu as pltpu
from jax.sharding import PartitionSpec as P

BF16 = jnp.bfloat16
F32 = jnp.float32
CHUNKS = (64, 64)
HALF = 128
PLANES, DEPTH = 2, 4
ROWS = PLANES * DEPTH
COLS = 16
MIB = 1 << 20


def row_pairs(move):
    pairs = []
    for plane in range(PLANES):
        for z in range(DEPTH):
            to_plane, to_z = move(plane, z)
            pairs.append((plane * DEPTH + z, to_plane % PLANES * DEPTH + to_z % DEPTH))
    return pairs


UP = row_pairs(lambda p, z: (p, z + 1))
DOWN = row_pairs(lambda p, z: (p, z - 1))
CROSS = row_pairs(lambda p, z: (p + 1, z))
CORE = [(c, c ^ 1) for c in range(COLS)]
BESIDE = [(c, c ^ 2) for c in range(COLS)]
CHIP_GROUPS = [[2 * i + c for i in range(ROWS)] for c in range(2)]
Y_GROUPS = [[i + 4 * y for y in range(4)] for i in range(4)]


def fence(*groups):
    flat, tree = jax.tree.flatten(groups)
    return jax.tree.unflatten(tree, lax.optimization_barrier(flat))


NEAR = ((0, 0), (0, 3), (0, 1), (1, 0))
FAR = ((0, 2), (1, 3), (1, 1), (1, 2))


def pieces_of(sizes, j, offsets):
    size, before = sizes[j], 2 * sizes[j - 1] if j else 0
    places = {
        (0, 0): [(("own", j), half * size) for half in range(2)],
        (1, 0): [(("across", j), half * size) for half in range(2)],
        (0, 3): [(("up", j), before + half * size) for half in range(2)],
        (0, 1): [(("down", j), before + half * size) for half in range(2)],
        (1, 3): [(("up", j + 1), half * size) for half in range(2)],
        (1, 1): [(("down", j + 1), half * size) for half in range(2)],
        (0, 2): [(("far_up", j), 0), (("far_down", j), 0)],
        (1, 2): [(("across_far", j), half * size) for half in range(2)],
    }
    return [places[offset] for offset in offsets]


def send(value, move):
    return lax.ppermute(value, "row", move)


def owner(place, plane, z):
    return (place // DEPTH + plane) % PLANES * DEPTH + (place + z) % DEPTH


def units_kernel(pieces, size, place, *refs):
    blocks, (weight, kept, sent, tokens, held, sems, out_sem) = refs[:-7], refs[-7:]
    core, step = place[1], pl.program_id(0)
    out = pltpu.make_async_copy(held, tokens, out_sem)

    @pl.when(step == 0)
    def _():
        copies = []
        for i, halves in enumerate(pieces):
            for half, (array, first) in enumerate(halves):
                side = (core + half) % 2
                start = (side * len(pieces) + i) * size
                copies.append(
                    pltpu.make_async_copy(
                        blocks[array].at[pl.ds(first, size)],
                        held.at[pl.ds(pl.multiple_of(start, 16), size)],
                        sems.at[len(copies)],
                    )
                )
        for copy in copies:
            copy.start()
        for copy in copies:
            copy.wait()
        out.start()

    total = lax.dot_general(
        held[...], weight[...], (((1,), (1,)), ((), ())), preferred_element_type=F32
    )
    rows = kept.shape[0]
    kept[...] = total[:rows]
    sent[...] = total[rows:]

    @pl.when(step == pl.num_programs(0) - 1)
    def _():
        out.wait()


def contract_units(place, arrays, sizes, j, offsets, weight):
    size, pieces = sizes[j], pieces_of(sizes, j, offsets)
    names = list(dict.fromkeys(name for halves in pieces for name, _ in halves))
    pieces = [[(names.index(name), first) for name, first in halves] for halves in pieces]
    features, units = weight.shape
    rows = len(offsets) * size
    tile = 512
    out = pl.pallas_call(
        functools.partial(units_kernel, pieces, size),
        grid=(features // tile,),
        in_specs=[pl.BlockSpec(memory_space=pltpu.SMEM)]
        + [pl.BlockSpec(memory_space=pl.ANY)] * len(names)
        + [pl.BlockSpec((tile, units), lambda n: (n, 0))],
        out_specs=[pl.BlockSpec((rows, tile), lambda n: (0, n))] * 2
        + [pl.BlockSpec(memory_space=pltpu.HBM)],
        out_shape=[jax.ShapeDtypeStruct((rows, features), F32)] * 2
        + [jax.ShapeDtypeStruct((2 * rows, units), BF16)],
        scratch_shapes=[
            pltpu.VMEM((2 * rows, units), BF16),
            pltpu.SemaphoreType.DMA((2 * len(pieces),)),
            pltpu.SemaphoreType.DMA,
        ],
        compiler_params=pltpu.CompilerParams(vmem_limit_bytes=48 * MIB),
        cost_estimate=pl.CostEstimate(
            flops=4 * rows * units * features,
            bytes_accessed=2 * features * units + 4 * rows * units + 8 * rows * features,
            transcendentals=0,
        ),
        name="units",
    )(place, *[arrays[name] for name in names], weight)
    return [half.reshape(len(offsets), size, features) for half in out[:2]] + [out[2]]


def tokens_kernel(groups, place, *refs):
    blocks, (mine, other, out, held, turned, sems, act_sems) = refs[:-7], refs[-7:]
    row, beside = place[0], place[2]
    tile = out.shape[1]
    columns = pl.ds(pl.multiple_of(pl.program_id(0) * tile, tile), tile)
    counts = [2 * len(offsets) * size for _, size, offsets in groups]
    starts = [sum(counts[:i]) for i in range(len(groups))]

    def copies(i):
        base, size, offsets = groups[i]
        made = [
            pltpu.make_async_copy(blocks[i], held.at[pl.ds(starts[i], counts[i])], sems.at[i])
        ]
        at, n = starts[i], sum(2 * len(g[2]) for g in groups[:i])
        for acts in (mine, other):
            for offset in offsets:
                chip = owner(row, *offset)
                first = chip // 2 * 2 * HALF + (chip + beside) % 2 * HALF + base
                made.append(
                    pltpu.make_async_copy(
                        acts.at[pl.ds(pl.multiple_of(first, 16), size)],
                        turned.at[pl.ds(at, size)],
                        act_sems.at[n],
                    )
                )
                at, n = at + size, n + 1
        return made

    def multiply(first, count):
        rows = pl.ds(first, count)
        return lax.dot_general(
            turned[rows], held[rows, columns], (((0,), (0,)), ((), ())), preferred_element_type=F32
        )

    @pl.when(pl.program_id(0) == 0)
    def _():
        for i in range(len(groups)):
            for copy in copies(i):
                copy.start()
        total = None
        for i in range(len(groups)):
            for copy in copies(i):
                copy.wait()
            part = multiply(starts[i], counts[i])
            total = part if total is None else total + part
        out[...] = total.astype(BF16)

    @pl.when(pl.program_id(0) > 0)
    def _():
        out[...] = multiply(0, held.shape[0]).astype(BF16)


def contract_tokens(place, blocks, groups, mine, other):
    tokens, features = 2 * mine.shape[0], mine.shape[1]
    units = blocks[0].shape[1]
    tile = 512
    return pl.pallas_call(
        functools.partial(tokens_kernel, groups),
        grid=(units // tile,),
        in_specs=[pl.BlockSpec(memory_space=pltpu.SMEM)]
        + [pl.BlockSpec(memory_space=pltpu.HBM)] * (len(blocks) + 2),
        out_specs=pl.BlockSpec((features, tile), lambda n: (0, n)),
        out_shape=jax.ShapeDtypeStruct((features, units), BF16),
        scratch_shapes=[
            pltpu.VMEM((tokens, units), BF16),
            pltpu.VMEM((tokens, features), BF16),
            pltpu.SemaphoreType.DMA((len(groups),)),
            pltpu.SemaphoreType.DMA((sum(2 * len(g[2]) for g in groups),)),
        ],
        compiler_params=pltpu.CompilerParams(vmem_limit_bytes=56 * MIB),
        cost_estimate=pl.CostEstimate(
            flops=2 * tokens * units * features,
            bytes_accessed=2 * (tokens * units + tokens * features + features * units),
            transcendentals=0,
        ),
        name="tokens",
    )(place, *blocks, mine, other)


def chips_kernel(order, near_kept, near_got, far_kept, far_got, out):
    @pl.when(pl.program_id(0) < len(NEAR))
    def _():
        out[...] = near_kept[...] + near_got[...]

    @pl.when(pl.program_id(0) >= len(NEAR))
    def _():
        out[...] = far_kept[...] + far_got[...]


def chip_sums(place, near, far):
    (near_kept, near_sent), (far_kept, far_sent) = near, far
    near_got, far_got = (lax.ppermute(sent, "col", CORE) for sent in (near_sent, far_sent))
    _, size, features = near_kept.shape
    order = jnp.stack([owner(place[0], *offset) for offset in NEAR + FAR])
    block = (1, size, features)
    near = pl.BlockSpec(block, lambda i, order: (jnp.minimum(i, 3), 0, 0))
    far = pl.BlockSpec(block, lambda i, order: (jnp.maximum(i - 4, 0), 0, 0))
    return pl.pallas_call(
        chips_kernel,
        grid_spec=pltpu.PrefetchScalarGridSpec(
            num_scalar_prefetch=1,
            grid=(ROWS,),
            in_specs=[near, near, far, far],
            out_specs=pl.BlockSpec(block, lambda i, order: (order[i], 0, 0)),
        ),
        out_shape=jax.ShapeDtypeStruct((ROWS, size, features), F32),
        compiler_params=pltpu.CompilerParams(vmem_limit_bytes=32 * MIB),
        cost_estimate=pl.CostEstimate(
            flops=ROWS * size * features,
            bytes_accessed=12 * ROWS * size * features,
            transcendentals=0,
        ),
        name="chips",
    )(order, near_kept, near_got, far_kept, far_got)


def gather_along_y(rows):
    copies = jnp.concatenate([rows] * 4)
    return lax.all_to_all(copies, "col", 0, 0, axis_index_groups=Y_GROUPS, tiled=True)


def sum_along_y(chip):
    parts = lax.all_to_all(chip, "col", 0, 0, axis_index_groups=Y_GROUPS, tiled=True)
    return jnp.sum(parts.reshape(4, 2, *chip.shape[1:]), axis=0)


def sum_direct(chip):
    parts = lax.all_to_all(chip, "col", 0, 0, axis_index_groups=CHIP_GROUPS, tiled=True)
    return jnp.sum(parts, axis=0).astype(BF16)


def local(inputs, weight, grad_out):
    row, col = lax.axis_index("row"), lax.axis_index("col")
    place = jnp.stack([row, col % 2, col // 2 % 2]).astype(jnp.int32)
    sizes, count = CHUNKS, len(CHUNKS)
    arrays, base = {}, 0
    for j, size in enumerate(sizes):
        own = [grad_out[half * HALF + base : half * HALF + base + size] for half in range(2)]
        arrays["own", j] = jnp.concatenate(own)
        base += size
    gathered, groups = [], []

    def multiply(j, offsets):
        kept, sent, rows = contract_units(place, arrays, sizes, j, offsets, weight)
        gathered.append(rows)
        groups.append((sum(sizes[:j]), sizes[j], offsets))
        return kept, sent

    near, far = [None] * count, [None] * count
    chips = []
    for k in range(count + 1):
        started, extra = [], ()

        def exchange():
            parts = [arrays["across", k - 1]] if k else []
            if k < count:
                parts.append(arrays["own", k])
            both = jnp.concatenate(parts) if len(parts) > 1 else parts[0]
            arrays["up", k], arrays["down", k] = send(both, UP), send(both, DOWN)
            started.extend([("up", k), ("down", k)])

        if k:
            size = sizes[k - 1]
            first = 2 * sizes[k - 2] if k > 1 else 0
            ready = [
                send(arrays["up", k - 1][first : first + size], UP),
                send(arrays["down", k - 1][first + size : first + 2 * size], DOWN),
            ]
            if k == 1:
                extra = [lax.ppermute(inputs, "col", BESIDE)]
            if k == count:
                exchange()
            if k > 1:
                far[k - 2] = multiply(k - 2, FAR)
                chips.append(chip_sums(place, near[k - 2], far[k - 2]))
            ready, extra, arrays["across", k - 1], near[k - 1], rest = fence(
                ready, extra, arrays["across", k - 1], near[k - 1], [arrays["own", min(k, count - 1)]]
            )
            arrays["own", min(k, count - 1)] = rest[0]
            arrays["far_up", k - 1], arrays["far_down", k - 1] = ready
            arrays["across_far", k - 1] = send(jnp.concatenate(ready), CROSS)
            started.append(("across_far", k - 1))
            near[k - 1] = multiply(k - 1, NEAR)
            if k == 1:
                mine = gather_along_y(jnp.concatenate([inputs, extra[0]]))
        if k < count:
            exchange()
            arrays["across", k] = send(arrays["own", k], CROSS)
            started.append(("across", k))
        held = [arrays[name] for name in started]
        later = [arrays["own", k + 1]] if k + 1 < count else []
        extra = [mine] if k == count else []
        held, later, near, extra = fence(held, later, near, extra)
        arrays.update(zip(started, held))
        if later:
            arrays["own", k + 1] = later[0]
        if extra:
            mine = extra[0]
    far[count - 1] = multiply(count - 1, FAR)
    other = lax.ppermute(mine, "col", CORE)
    chip = chip_sums(place, near[-1], far[-1])
    first = jnp.concatenate([sum_along_y(chip) for chip in chips], axis=1)
    chip, mine, other, first = fence(chip, mine, other, first)
    last = sum_direct(chip)
    beside = place[2]
    own = lax.dynamic_index_in_dim(first, beside, 0, keepdims=False)
    others = lax.dynamic_index_in_dim(first, 1 - beside, 0, keepdims=False)
    sums = [(own + lax.ppermute(others, "col", BESIDE)).astype(BF16), last]
    weight_grad = contract_tokens(place, gathered, groups, mine, other)
    input_grad = jnp.concatenate(sums, axis=0)
    return input_grad, weight_grad


def solution(mesh):
    placed = (P("col", "row"), P("row", "col"), P("row", "col"))
    return jax.shard_map(
        local,
        mesh=mesh,
        in_specs=placed,
        out_specs=(P("col", "row"), P("row", "col")),
        check_vma=False,
    )
```

time: 352 us -> 225 us (0.64)
  waiting for transfers between devices: 283 us -> 72.1 us
  Pallas kernels: 0 us -> 81.5 us
  matrix products: 52.3 us -> 0 us
  starting transfers between devices: 0.11 us -> 43.4 us
  local copies, waits for them, and re-layouts: 0 us -> 20 us
  between operations: 13.7 us -> 0.95 us
  other arithmetic: 1.92 us -> 6.29 us
    all_gather x2 -> x0, waiting for transfers between devices: 164 us -> none  [the longest x1 149 us: local(): grads = lax.all_gather(grad_out, 'row', axis=0, tiled=True)]
    reduce_scatter x1 -> x0, waiting for transfers between devices: 118 us -> none  [local(): lax.psum_scatter(partial_value, 'col', scatter_dimension=0, tiled=True)]
    pallas_call x0 -> x7, Pallas kernels: none -> 81.5 us  [the longest x4 42.1 us: contract_units(): pl.pallas_call(functools.partial(units_kernel, pieces, size), grid=(featu...]
    ppermute x0 -> x21, waiting for transfers between devices: none -> 54.6 us  [the longest x14 32.5 us: send(): return lax.ppermute(value, 'row', move)]
    dot_general x2 -> x0, matrix products: 52.3 us -> none  [the longest x1 26.6 us: contract_units(): lax.dot_general(left, right, (((1,), (1,)), ((), ())), preferred_element_...]
    ppermute x0 -> x21, starting transfers between devices: none -> 30.4 us  [the longest x14 27.1 us: send(): return lax.ppermute(value, 'row', move)]
    all_to_all x0 -> x3, waiting for transfers between devices: none -> 17.5 us  [the longest x1 17.5 us: sum_along_y(): lax.all_to_all(chip, 'col', 0, 0, axis_index_groups=Y_GROUPS, tiled=True)]
    unnamed x0 -> x42, local copies, waits for them, and re-layouts: none -> 13.6 us
  transfers between devices with their start and end apart: 3 -> 24, of which waited for: 3 -> 11; matrix products, arithmetic and copies ran while one was open for 15% -> 7% of each run, Pallas kernels for 0% -> 36%
where the time goes in v1:
time: 225 us; the launch traced here: 224 us
  Pallas kernels  81.5 us (36%)
  waiting for transfers between devices  72.1 us (32%)
  starting transfers between devices  43.4 us (19%)
  local copies, waits for them, and re-layouts  20 us (9%)
  other arithmetic  6.29 us (3%)
    pallas_call x4, Pallas kernels, contract_units(): pl.pallas_call(functools.partial(units_kernel, pieces, size), grid=(featu...  42.1 us
    ppermute x14, waiting for transfers between devices, send(): return lax.ppermute(value, 'row', move)  32.5 us
    pallas_call x1, Pallas kernels, contract_tokens(): pl.pallas_call(functools.partial(tokens_kernel, groups), grid=(units // t...  28.4 us
    ppermute x14, starting transfers between devices, send(): return lax.ppermute(value, 'row', move)  27.1 us
    all_to_all x1, waiting for transfers between devices, sum_along_y(): lax.all_to_all(chip, 'col', 0, 0, axis_index_groups=Y_GROUPS, tiled=True)  17.5 us
    ppermute x1, waiting for transfers between devices, local(): sums = [(own + lax.ppermute(others, 'col', BESIDE)).astype(BF16), last]  14.1 us
    unnamed x42, local copies, waits for them, and re-layouts  13.6 us
    pallas_call x2, Pallas kernels, chip_sums(): pl.pallas_call(chips_kernel, grid_spec=pltpu.PrefetchScalarGridSpec(num_s...  10.9 us
  transfers between devices with their start and end apart: 24, of which 11 were waited for; matrix products, arithmetic and copies ran while one was open for 7% of the time, Pallas kernels for 36%

profile of v1, /device:TPU:0, one launch (start us, length us, event | category | flops | bytes accessed | tf_op | source)
XLA Modules:
  0.0 224.2 jit_solution(4640985854211658640)
XLA Ops:
  0.6 1.5 fusion.1
  2.2 2.1 collective-permute-start
  4.3 2.2 collective-permute-start.1
  6.5 3.0 %collective-permute-start.2 = (bf16[128,3072]{1,0:T(8,128)(2,1)S(1)}, bf16[128,3072]{1,0:T(8,128)(2,1)S(1)}, u32[]{:S(2)}, u32[]{:S(2)}) collective-permute-start(bf16[128,3072]{1,0:T(8,128)(2,1)S(1)} %pad_maximum_fusion.refs_0_), channel_id=1, source_target_pairs={{0,64},{16,80},{32,96},{48,112},{64,0},{80,16},{96,32},{112,48},{1... | collective-permute-start | bytes 2359304 | tf_op jit(solution)/shard_map/ppermute | solution.py:63
  10.2 13.8 %collective-permute-done.refs_1_ = bf16[128,3072]{1,0:T(8,128)(2,1)S(1)} collective-permute-done((bf16[128,3072]{1,0:T(8,128)(2,1)S(1)}, bf16[128,3072]{1,0:T(8,128)(2,1)S(1)}, u32[]{:S(2)}, u32[]{:S(2)}) %collective-permute-start) | collective-permute-done | bytes 786464 | tf_op jit(solution)/shard_map/ppermute | solution.py:63
  23.9 4.5 %collective-permute-done.2.refs_3_ = bf16[128,3072]{1,0:T(8,128)(2,1)S(1)} collective-permute-done((bf16[128,3072]{1,0:T(8,128)(2,1)S(1)}, bf16[128,3072]{1,0:T(8,128)(2,1)S(1)}, u32[]{:S(2)}, u32[]{:S(2)}) %collective-permute-start.2) | collective-permute-done | bytes 786464 | tf_op jit(solution)/shard_map/ppermute | solution.py:63
  28.6 3.3 %collective-permute-start.4 = (bf16[64,3072]{1,0:T(8,128)(2,1)S(1)}, bf16[64,3072]{1,0:T(8,128)(2,1)S(1)}, u32[]{:S(2)}, u32[]{:S(2)}) collective-permute-start(bf16[64,3072]{1,0:T(8,128)(2,1)S(1)} %slice.29), channel_id=1, source_target_pairs={{0,48},{16,0},{32,16},{48,32},{64,112},{80,64},{96,80},{112,96},{1... | collective-permute-start | bytes 1179656 | tf_op jit(solution)/shard_map/ppermute | solution.py:63
  32.7 2.8 %collective-permute-done.5 = bf16[128,1536]{1,0:T(8,128)(2,1)S(1)} collective-permute-done((bf16[128,1536]{1,0:T(8,128)(2,1)S(1)}, bf16[128,1536]{1,0:T(8,128)(2,1)S(1)}, u32[]{:S(2)}, u32[]{:S(2)}) %collective-permute-start.5) | collective-permute-done | bytes 393248 | tf_op jit(solution)/shard_map/ppermute | solution.py:309
  35.5 2.5 %collective-permute-done.3.refs_0_ = bf16[64,3072]{1,0:T(8,128)(2,1)S(1)} collective-permute-done((bf16[64,3072]{1,0:T(8,128)(2,1)S(1)}, bf16[64,3072]{1,0:T(8,128)(2,1)S(1)}, u32[]{:S(2)}, u32[]{:S(2)}) %collective-permute-start.3) | collective-permute-done | bytes 393248 | tf_op jit(solution)/shard_map/ppermute | solution.py:63
  38.0 1.0 constant_dynamic-update-slice_fusion.1
  39.0 1.0 constant_dynamic-update-slice_fusion
  40.2 3.0 %collective-permute-start.8 = (bf16[256,3072]{1,0:T(8,128)(2,1)}, bf16[256,3072]{1,0:T(8,128)(2,1)}, u32[]{:S(2)}, u32[]{:S(2)}) collective-permute-start(bf16[256,3072]{1,0:T(8,128)(2,1)} %constant_dynamic-update-slice_fusion), channel_id=1, source_target_pairs={{0,48},{16,0},{32,16},{48,32},{64,112},{80,64},{96,80},{112,96},{1... | collective-permute-start | bytes 4718600 | tf_op jit(solution)/shard_map/ppermute | solution.py:63
  43.2 3.0 %collective-permute-start.9 = (bf16[128,3072]{1,0:T(8,128)(2,1)S(1)}, bf16[128,3072]{1,0:T(8,128)(2,1)}, u32[]{:S(2)}, u32[]{:S(2)}) collective-permute-start(bf16[128,3072]{1,0:T(8,128)(2,1)S(1)} %pad_maximum_fusion.1.refs_0_), channel_id=1, source_target_pairs={{0,64},{16,80},{32,96},{48,112},{64,0},{80,16},{96,32},{112,48},{1... | collective-permute-start | bytes 2359304 | tf_op jit(solution)/shard_map/ppermute | solution.py:63
  46.2 1.0 pad_maximum_fusion.2
  49.3 0.8 constant_dynamic-update-slice_fusion.6
  53.1 4.7 %all-to-all-start = ((bf16[4,256,1536]{2,1,0:T(8,128)(2,1)}), bf16[4,256,1536]{2,1,0:T(8,128)(2,1)}, u32[]{:S(2)}, u32[]{:S(2)}) async-start(bf16[4,256,1536]{2,1,0:T(8,128)(2,1)} %bitcast.15), calls=%async_computation | async-start | bytes 6291456 | tf_op jit(solution)/shard_map/all_to_all | solution.py:258
  57.9 1.1 copy-done.5
  59.1 1.1 copy-done.9
  60.2 1.1 copy-done.11
  61.3 10.2 %units.4 = (f32[256,1536]{1,0:T(8,128)S(1)}, f32[256,1536]{1,0:T(8,128)}, bf16[512,3072]{1,0:T(8,128)(2,1)}) custom-call(s32[3]{0:T(128)S(1)} %pad_add_fusion.place, bf16[128,3072]{1,0:T(8,128)(2,1)S(1)} %pad_maximum_fusion.refs_0_, bf16[128,3072]{1,0:T(8,128)(2,1)S(1)} %copy-done.9, bf16[128,3072]{1,0:T(8,128)(2,1)S(1)} %copy-done.11, ...), custom_call_target="tpu_custom_call" | custom-call | flops 4831838208 | bytes 15728640 | tf_op jit(solution)/shard_map/units/pallas_call | solution.py:114
  71.6 5.2 %collective-permute-done.6.refs_4_ = bf16[128,3072]{1,0:T(8,128)(2,1)} collective-permute-done((bf16[128,3072]{1,0:T(8,128)(2,1)}, bf16[128,3072]{1,0:T(8,128)(2,1)}, u32[]{:S(2)}, u32[]{:S(2)}) %collective-permute-start.6) | collective-permute-done | bytes 786464 | tf_op jit(solution)/shard_map/ppermute | solution.py:63
  76.9 3.2 %collective-permute-start.11 = (bf16[128,3072]{1,0:T(8,128)(2,1)}, bf16[128,3072]{1,0:T(8,128)(2,1)}, u32[]{:S(2)}, u32[]{:S(2)}) collective-permute-start(bf16[128,3072]{1,0:T(8,128)(2,1)} %collective-permute-done.9.refs_3_), channel_id=1, source_target_pairs={{0,48},{16,0},{32,16},{48,32},{64,112},{80,64},{96,80},{112,96},{1... | collective-permute-start | bytes 2359304 | tf_op jit(solution)/shard_map/ppermute | solution.py:63
  80.1 1.0 slice.30
  81.2 1.0 slice.31
  82.3 3.3 %collective-permute-start.13 = (bf16[64,3072]{1,0:T(8,128)(2,1)S(1)}, bf16[64,3072]{1,0:T(8,128)(2,1)S(1)}, u32[]{:S(2)}, u32[]{:S(2)}) collective-permute-start(bf16[64,3072]{1,0:T(8,128)(2,1)S(1)} %slice.31), channel_id=1, source_target_pairs={{0,48},{16,0},{32,16},{48,32},{64,112},{80,64},{96,80},{112,96},{1... | collective-permute-start | bytes 1179656 | tf_op jit(solution)/shard_map/ppermute | solution.py:63
  85.6 10.8 %units.7 = (f32[256,1536]{1,0:T(8,128)S(1)}, f32[256,1536]{1,0:T(8,128)}, bf16[512,3072]{1,0:T(8,128)(2,1)}) custom-call(s32[3]{0:T(128)S(1)} %pad_add_fusion.place, bf16[64,3072]{1,0:T(8,128)(2,1)S(1)} %collective-permute-done.3.refs_0_, bf16[64,3072]{1,0:T(8,128)(2,1)S(1)} %copy-done.7, bf16[256,3072]{1,0:T(8,128)(2,1)} %collective-permute-done.7.refs_1_.refs_2_, ...), custom_call_target="tpu_custom_call" | custom-call | flops 4831838208 | bytes 15728640 | tf_op jit(solution)/shard_map/units/pallas_call | solution.py:114
  96.5 4.5 %collective-permute-done.12.refs_0_ = bf16[64,3072]{1,0:T(8,128)(2,1)S(1)} collective-permute-done((bf16[64,3072]{1,0:T(8,128)(2,1)S(1)}, bf16[64,3072]{1,0:T(8,128)(2,1)S(1)}, u32[]{:S(2)}, u32[]{:S(2)}) %collective-permute-start.12) | collective-permute-done | bytes 393248 | tf_op jit(solution)/shard_map/ppermute | solution.py:63
  101.0 1.0 pad_maximum_fusion.3
  101.9 3.0 %collective-permute-start.14 = (bf16[128,3072]{1,0:T(8,128)(2,1)}, bf16[128,3072]{1,0:T(8,128)(2,1)}, u32[]{:S(2)}, u32[]{:S(2)}) collective-permute-start(bf16[128,3072]{1,0:T(8,128)(2,1)} %pad_maximum_fusion.3), channel_id=1, source_target_pairs={{0,64},{16,80},{32,96},{48,112},{64,0},{80,16},{96,32},{112,48},{1... | collective-permute-start | bytes 2359304 | tf_op jit(solution)/shard_map/ppermute | solution.py:63
  104.9 9.9 %units.5 = (f32[256,1536]{1,0:T(8,128)S(1)}, f32[256,1536]{1,0:T(8,128)S(1)}, bf16[512,3072]{1,0:T(8,128)(2,1)}) custom-call(s32[3]{0:T(128)S(1)} %pad_add_fusion.place, bf16[128,3072]{1,0:T(8,128)(2,1)S(1)} %pad_maximum_fusion.1.refs_0_, bf16[256,3072]{1,0:T(8,128)(2,1)} %collective-permute-done.7.refs_1_.refs_2_, ...), custom_call_target="tpu_custom_call" | custom-call | flops 4831838208 | bytes 15728640 | tf_op jit(solution)/shard_map/units/pallas_call | solution.py:114
  114.9 1.2 copy-done
  116.0 1.2 copy-done.13
  117.2 2.0 collective-permute-done.14.refs_4_
  119.3 1.4 copy-done.3
  120.7 7.0 %chips.3 = f32[8,64,1536]{2,1,0:T(8,128)} custom-call(s32[8]{0:T(128)S(1)} %stack.56.order, f32[4,64,1536]{2,1,0:T(8,128)S(1)} %bitcast.28, f32[4,64,1536]{2,1,0:T(8,128)} %collective-permute-done.18.near_got, f32[4,64,1536]{2,1,0:T(8,128)S(1)} %bitcast.30, f32[4,64,1536]{2,1,0:T(8,128)} %collective-permute-done.19.far_got), custom_call_target="tpu_custom_call" | custom-call | flops 786432 | bytes 9437184 | tf_op jit(solution)/shard_map/chips/pallas_call | solution.py:237
  127.7 4.7 %all-to-all-start.1 = ((f32[8,64,1536]{2,1,0:T(8,128)}), f32[8,64,1536]{2,1,0:T(8,128)}, u32[]{:S(2)}, u32[]{:S(2)}) async-start(f32[8,64,1536]{2,1,0:T(8,128)} %chips.3), calls=%async_computation.1 | async-start | bytes 6291456 | tf_op jit(solution)/shard_map/all_to_all | solution.py:262
  132.4 11.2 %units.6 = (f32[256,1536]{1,0:T(8,128)S(1)}, f32[256,1536]{1,0:T(8,128)}, bf16[512,3072]{1,0:T(8,128)(2,1)}) custom-call(s32[3]{0:T(128)S(1)} %pad_add_fusion.place, bf16[64,3072]{1,0:T(8,128)(2,1)S(1)} %collective-permute-done.12.refs_0_, bf16[64,3072]{1,0:T(8,128)(2,1)S(1)} %collective-permute-done.13.refs_1_, ...), custom_call_target="tpu_custom_call" | custom-call | flops 4831838208 | bytes 15728640 | tf_op jit(solution)/shard_map/units/pallas_call | solution.py:114
  144.2 4.4 %collective-permute-done.16.far_got = f32[4,64,1536]{2,1,0:T(8,128)S(1)} collective-permute-done((f32[4,64,1536]{2,1,0:T(8,128)}, f32[4,64,1536]{2,1,0:T(8,128)S(1)}, u32[]{:S(2)}, u32[]{:S(2)}) %collective-permute-start.16) | collective-permute-done | bytes 1572896 | tf_op jit(solution)/shard_map/ppermute | solution.py:231
  148.6 0.8 collective-permute-done.15.near_got
  149.4 3.9 %chips.2 = f32[8,64,1536]{2,1,0:T(8,128)} custom-call(s32[8]{0:T(128)S(1)} %stack.56.order, f32[4,64,1536]{2,1,0:T(8,128)S(1)} %bitcast.29, f32[4,64,1536]{2,1,0:T(8,128)S(1)} %collective-permute-done.15.near_got, f32[4,64,1536]{2,1,0:T(8,128)S(1)} %bitcast.31, f32[4,64,1536]{2,1,0:T(8,128)S(1)} %collective-permute-done.16.far_got), custom_call_target="tpu_custom_call" | custom-call | flops 786432 | bytes 9437184 | tf_op jit(solution)/shard_map/chips/pallas_call | solution.py:237
  153.4 17.5 %all-to-all-done.1 = f32[8,64,1536]{2,1,0:T(8,128)} async-done(((f32[8,64,1536]{2,1,0:T(8,128)}), f32[8,64,1536]{2,1,0:T(8,128)}, u32[]{:S(2)}, u32[]{:S(2)}) %all-to-all-start.1) | async-done | bytes 3145760 | tf_op jit(solution)/shard_map/all_to_all | solution.py:262
  170.9 3.1 %reduce_sum.18 = f32[2,64,1536]{2,1,0:T(8,128)} reduce(f32[4,2,64,1536]{3,2,1,0:T(8,128)} %bitcast.21, f32[]{:T(128)} %constant.167.clone.1), dimensions={0}, to_apply=%region_0.1 | reduce | flops 589824 | bytes 3932164 | tf_op jit(solution)/shard_map/reduce_sum | solution.py:263
  174.0 3.6 %all-to-all-start.2 = ((f32[8,64,1536]{2,1,0:T(8,128)}), f32[8,64,1536]{2,1,0:T(8,128)S(1)}, u32[]{:S(2)}, u32[]{:S(2)}) async-start(f32[8,64,1536]{2,1,0:T(8,128)} %chips.2), calls=%async_computation.2 | async-start | bytes 6291456 | tf_op jit(solution)/shard_map/all_to_all | solution.py:267
  177.7 1.0 dynamic-slice_bitcast_fusion
  178.7 2.0 collective-permute-start.20
  180.7 28.4 %tokens.1 = bf16[1536,3072]{1,0:T(8,128)(2,1)} custom-call(s32[3]{0:T(128)} %copy-done.12, bf16[512,3072]{1,0:T(8,128)(2,1)} %get-tuple-element.78.refs_0_, bf16[512,3072]{1,0:T(8,128)(2,1)} %get-tuple-element.79.refs_1_, bf16[512,3072]{1,0:T(8,128)(2,1)} %get-tuple-element.80.refs_2_, bf16[512,3072]{1,0:T(8,128)(2,1)} %get-tuple-element.81.refs_3_, ...), custom_call_target="tpu_custom_call" | custom-call | flops 19327352832 | bytes 28311552 | tf_op jit(solution)/shard_map/tokens/pallas_call | solution.py:196
  209.1 14.1 %collective-permute-done.20 = f32[64,1536]{1,0:T(8,128)S(1)} collective-permute-done((f32[64,1536]{1,0:T(8,128)S(1)}, f32[64,1536]{1,0:T(8,128)S(1)}, u32[]{:S(2)}, u32[]{:S(2)}) %collective-permute-start.20) | collective-permute-done | bytes 393248 | tf_op jit(solution)/shard_map/ppermute | solution.py:347
  223.5 0.8 pad_maximum_fusion.4
  (67 shorter events, 8.4 us)
Async XLA Ops:
  0.6 8.9 %copy-start.15 = (bf16[128,1536]{1,0:T(8,128)(2,1)S(1)}, bf16[128,1536]{1,0:T(8,128)(2,1)}, u32[]{:S(2)}) copy-start(bf16[128,1536]{1,0:T(8,128)(2,1)} %param.3) | copy-start | bytes 1179652
  2.2 21.7 %collective-permute-start = (bf16[128,3072]{1,0:T(8,128)(2,1)S(1)}, bf16[128,3072]{1,0:T(8,128)(2,1)S(1)}, u32[]{:S(2)}, u32[]{:S(2)}) collective-permute-start(bf16[128,3072]{1,0:T(8,128)(2,1)S(1)} %pad_maximum_fusion.refs_0_), channel_id=1, source_target_pairs={{0,16},{16,32},{32,48},{48,0},{64,80},{80,96},{96,112},{112,64},{1... | collective-permute-start | bytes 2359304 | tf_op jit(solution)/shard_map/ppermute | solution.py:63
  4.3 19.7 %collective-permute-start.1 = (bf16[128,3072]{1,0:T(8,128)(2,1)S(1)}, bf16[128,3072]{1,0:T(8,128)(2,1)S(1)}, u32[]{:S(2)}, u32[]{:S(2)}) collective-permute-start(bf16[128,3072]{1,0:T(8,128)(2,1)S(1)} %pad_maximum_fusion.refs_0_), channel_id=1, source_target_pairs={{0,48},{16,0},{32,16},{48,32},{64,112},{80,64},{96,80},{112,96},{1... | collective-permute-start | bytes 2359304 | tf_op jit(solution)/shard_map/ppermute | solution.py:63
  6.5 22.0 %collective-permute-start.2 = (bf16[128,3072]{1,0:T(8,128)(2,1)S(1)}, bf16[128,3072]{1,0:T(8,128)(2,1)S(1)}, u32[]{:S(2)}, u32[]{:S(2)}) collective-permute-start(bf16[128,3072]{1,0:T(8,128)(2,1)S(1)} %pad_maximum_fusion.refs_0_), channel_id=1, source_target_pairs={{0,64},{16,80},{32,96},{48,112},{64,0},{80,16},{96,32},{112,48},{1... | collective-permute-start | bytes 2359304 | tf_op jit(solution)/shard_map/ppermute | solution.py:63
  9.5 26.0 %collective-permute-start.5 = (bf16[128,1536]{1,0:T(8,128)(2,1)S(1)}, bf16[128,1536]{1,0:T(8,128)(2,1)S(1)}, u32[]{:S(2)}, u32[]{:S(2)}) collective-permute-start(bf16[128,1536]{1,0:T(8,128)(2,1)S(1)} %copy-done.15), channel_id=1, source_target_pairs={{0,2},{1,3},{2,0},{3,1},{4,6},{5,7},{6,4},{7,5},{8,10},{9,11},{10,... | collective-permute-start | bytes 1179656 | tf_op jit(solution)/shard_map/ppermute | solution.py:309
  23.9 4.6 %copy-start.8 = (bf16[128,3072]{1,0:T(8,128)(2,1)}, bf16[128,3072]{1,0:T(8,128)(2,1)S(1)}, u32[]{:S(2)}) copy-start(bf16[128,3072]{1,0:T(8,128)(2,1)S(1)} %collective-permute-done.refs_1_) | copy-start | bytes 2359300
  23.9 23.3 %copy-start.10 = (bf16[128,3072]{1,0:T(8,128)(2,1)}, bf16[128,3072]{1,0:T(8,128)(2,1)S(1)}, u32[]{:S(2)}) copy-start(bf16[128,3072]{1,0:T(8,128)(2,1)S(1)} %collective-permute-done.1.refs_2_) | copy-start | bytes 2359300
  28.4 18.8 %copy-start.4 = (bf16[128,3072]{1,0:T(8,128)(2,1)}, bf16[128,3072]{1,0:T(8,128)(2,1)S(1)}, u32[]{:S(2)}) copy-start(bf16[128,3072]{1,0:T(8,128)(2,1)S(1)} %collective-permute-done.2.refs_3_) | copy-start | bytes 2359300
  28.5 9.5 %collective-permute-start.3 = (bf16[64,3072]{1,0:T(8,128)(2,1)S(1)}, bf16[64,3072]{1,0:T(8,128)(2,1)S(1)}, u32[]{:S(2)}, u32[]{:S(2)}) collective-permute-start(bf16[64,3072]{1,0:T(8,128)(2,1)S(1)} %slice.28), channel_id=1, source_target_pairs={{0,16},{16,32},{32,48},{48,0},{64,80},{80,96},{96,112},{112,64},{1... | collective-permute-start | bytes 1179656 | tf_op jit(solution)/shard_map/ppermute | solution.py:63
  28.6 9.4 %collective-permute-start.4 = (bf16[64,3072]{1,0:T(8,128)(2,1)S(1)}, bf16[64,3072]{1,0:T(8,128)(2,1)S(1)}, u32[]{:S(2)}, u32[]{:S(2)}) collective-permute-start(bf16[64,3072]{1,0:T(8,128)(2,1)S(1)} %slice.29), channel_id=1, source_target_pairs={{0,48},{16,0},{32,16},{48,32},{64,112},{80,64},{96,80},{112,96},{1... | collective-permute-start | bytes 1179656 | tf_op jit(solution)/shard_map/ppermute | solution.py:63
  38.0 11.3 %copy-start.6 = (bf16[64,3072]{1,0:T(8,128)(2,1)}, bf16[64,3072]{1,0:T(8,128)(2,1)S(1)}, u32[]{:S(2)}) copy-start(bf16[64,3072]{1,0:T(8,128)(2,1)S(1)} %collective-permute-done.4.refs_1_) | copy-start | bytes 1179652
  40.0 36.9 %collective-permute-start.7 = (bf16[256,3072]{1,0:T(8,128)(2,1)}, bf16[256,3072]{1,0:T(8,128)(2,1)}, u32[]{:S(2)}, u32[]{:S(2)}) collective-permute-start(bf16[256,3072]{1,0:T(8,128)(2,1)} %constant_dynamic-update-slice_fusion), channel_id=1, source_target_pairs={{0,16},{16,32},{32,48},{48,0},{64,80},{80,96},{96,112},{112,64},{1... | collective-permute-start | bytes 4718600 | tf_op jit(solution)/shard_map/ppermute | solution.py:63
  40.2 36.6 %collective-permute-start.8 = (bf16[256,3072]{1,0:T(8,128)(2,1)}, bf16[256,3072]{1,0:T(8,128)(2,1)}, u32[]{:S(2)}, u32[]{:S(2)}) collective-permute-start(bf16[256,3072]{1,0:T(8,128)(2,1)} %constant_dynamic-update-slice_fusion), channel_id=1, source_target_pairs={{0,48},{16,0},{32,16},{48,32},{64,112},{80,64},{96,80},{112,96},{1... | collective-permute-start | bytes 4718600 | tf_op jit(solution)/shard_map/ppermute | solution.py:63
  43.2 33.6 %collective-permute-start.9 = (bf16[128,3072]{1,0:T(8,128)(2,1)S(1)}, bf16[128,3072]{1,0:T(8,128)(2,1)}, u32[]{:S(2)}, u32[]{:S(2)}) collective-permute-start(bf16[128,3072]{1,0:T(8,128)(2,1)S(1)} %pad_maximum_fusion.1.refs_0_), channel_id=1, source_target_pairs={{0,64},{16,80},{32,96},{48,112},{64,0},{80,16},{96,32},{112,48},{1... | collective-permute-start | bytes 2359304 | tf_op jit(solution)/shard_map/ppermute | solution.py:63
  47.2 29.6 %collective-permute-start.6 = (bf16[128,3072]{1,0:T(8,128)(2,1)}, bf16[128,3072]{1,0:T(8,128)(2,1)}, u32[]{:S(2)}, u32[]{:S(2)}) collective-permute-start(bf16[128,3072]{1,0:T(8,128)(2,1)} %pad_maximum_fusion.2), channel_id=1, source_target_pairs={{0,64},{16,80},{32,96},{48,112},{64,0},{80,16},{96,32},{112,48},{1... | collective-permute-start | bytes 2359304 | tf_op jit(solution)/shard_map/ppermute | solution.py:63
  53.1 64.1 %all-to-all-start = ((bf16[4,256,1536]{2,1,0:T(8,128)(2,1)}), bf16[4,256,1536]{2,1,0:T(8,128)(2,1)}, u32[]{:S(2)}, u32[]{:S(2)}) async-start(bf16[4,256,1536]{2,1,0:T(8,128)(2,1)} %bitcast.15), calls=%async_computation | async-start | bytes 6291456 | tf_op jit(solution)/shard_map/all_to_all | solution.py:258
  57.9 1.1 copy-start.5
  59.1 1.1 copy-start.9
  60.2 1.1 copy-start.11
  61.3 71.0 %copy-start.12 = (s32[3]{0:T(128)}, s32[3]{0:T(128)S(1)}, u32[]{:S(2)}) copy-start(s32[3]{0:T(128)S(1)} %pad_add_fusion.place) | copy-start | bytes 40
  61.3 24.2 %copy-start.7 = (bf16[64,3072]{1,0:T(8,128)(2,1)S(1)}, bf16[64,3072]{1,0:T(8,128)(2,1)}, u32[]{:S(2)}) copy-start(bf16[64,3072]{1,0:T(8,128)(2,1)} %copy-done.6) | copy-start | bytes 1179652
  76.8 40.4 %collective-permute-start.10 = (bf16[128,3072]{1,0:T(8,128)(2,1)}, bf16[128,3072]{1,0:T(8,128)(2,1)}, u32[]{:S(2)}, u32[]{:S(2)}) collective-permute-start(bf16[128,3072]{1,0:T(8,128)(2,1)} %collective-permute-done.9.refs_3_), channel_id=1, source_target_pairs={{0,16},{16,32},{32,48},{48,0},{64,80},{80,96},{96,112},{112,64},{1... | collective-permute-start | bytes 2359304 | tf_op jit(solution)/shard_map/ppermute | solution.py:63
  76.9 40.3 %collective-permute-start.11 = (bf16[128,3072]{1,0:T(8,128)(2,1)}, bf16[128,3072]{1,0:T(8,128)(2,1)}, u32[]{:S(2)}, u32[]{:S(2)}) collective-permute-start(bf16[128,3072]{1,0:T(8,128)(2,1)} %collective-permute-done.9.refs_3_), channel_id=1, source_target_pairs={{0,48},{16,0},{32,16},{48,32},{64,112},{80,64},{96,80},{112,96},{1... | collective-permute-start | bytes 2359304 | tf_op jit(solution)/shard_map/ppermute | solution.py:63
  81.2 19.8 %collective-permute-start.12 = (bf16[64,3072]{1,0:T(8,128)(2,1)S(1)}, bf16[64,3072]{1,0:T(8,128)(2,1)S(1)}, u32[]{:S(2)}, u32[]{:S(2)}) collective-permute-start(bf16[64,3072]{1,0:T(8,128)(2,1)S(1)} %slice.30), channel_id=1, source_target_pairs={{0,16},{16,32},{32,48},{48,0},{64,80},{80,96},{96,112},{112,64},{1... | collective-permute-start | bytes 1179656 | tf_op jit(solution)/shard_map/ppermute | solution.py:63
  82.3 18.7 %collective-permute-start.13 = (bf16[64,3072]{1,0:T(8,128)(2,1)S(1)}, bf16[64,3072]{1,0:T(8,128)(2,1)S(1)}, u32[]{:S(2)}, u32[]{:S(2)}) collective-permute-start(bf16[64,3072]{1,0:T(8,128)(2,1)S(1)} %slice.31), channel_id=1, source_target_pairs={{0,48},{16,0},{32,16},{48,32},{64,112},{80,64},{96,80},{112,96},{1... | collective-permute-start | bytes 1179656 | tf_op jit(solution)/shard_map/ppermute | solution.py:63
  96.4 8.6 %copy-start.2 = (f32[256,1536]{1,0:T(8,128)}, f32[256,1536]{1,0:T(8,128)S(1)}, u32[]{:S(2)}) copy-start(f32[256,1536]{1,0:T(8,128)S(1)} %get-tuple-element.74) | copy-start | bytes 4718596
  96.4 22.9 %collective-permute-start.19 = (f32[4,64,1536]{2,1,0:T(8,128)}, f32[4,64,1536]{2,1,0:T(8,128)}, u32[]{:S(2)}, u32[]{:S(2)}) collective-permute-start(f32[4,64,1536]{2,1,0:T(8,128)} %bitcast.20), channel_id=1, source_target_pairs={{0,1},{1,0},{2,3},{3,2},{4,5},{5,4},{6,7},{7,6},{8,9},{9,8},{10,11... | collective-permute-start | bytes 4718600 | tf_op jit(solution)/shard_map/ppermute | solution.py:231
  101.9 17.3 %collective-permute-start.14 = (bf16[128,3072]{1,0:T(8,128)(2,1)}, bf16[128,3072]{1,0:T(8,128)(2,1)}, u32[]{:S(2)}, u32[]{:S(2)}) collective-permute-start(bf16[128,3072]{1,0:T(8,128)(2,1)} %pad_maximum_fusion.3), channel_id=1, source_target_pairs={{0,64},{16,80},{32,96},{48,112},{64,0},{80,16},{96,32},{112,48},{1... | collective-permute-start | bytes 2359304 | tf_op jit(solution)/shard_map/ppermute | solution.py:63
  104.9 14.3 %collective-permute-start.18 = (f32[4,64,1536]{2,1,0:T(8,128)}, f32[4,64,1536]{2,1,0:T(8,128)}, u32[]{:S(2)}, u32[]{:S(2)}) collective-permute-start(f32[4,64,1536]{2,1,0:T(8,128)} %bitcast.12), channel_id=1, source_target_pairs={{0,1},{1,0},{2,3},{3,2},{4,5},{5,4},{6,7},{7,6},{8,9},{9,8},{10,11... | collective-permute-start | bytes 4718600 | tf_op jit(solution)/shard_map/ppermute | solution.py:231
  114.9 1.2 copy-start
  116.0 1.2 copy-start.13
  119.2 54.8 %collective-permute-start.17 = (bf16[1024,1536]{1,0:T(8,128)(2,1)}, bf16[1024,1536]{1,0:T(8,128)(2,1)}, u32[]{:S(2)}, u32[]{:S(2)}) collective-permute-start(bf16[1024,1536]{1,0:T(8,128)(2,1)} %bitcast.16.refs_4_), channel_id=1, source_target_pairs={{0,1},{1,0},{2,3},{3,2},{4,5},{5,4},{6,7},{7,6},{8,9},{9,8},{10,11... | collective-permute-start | bytes 9437192 | tf_op jit(solution)/shard_map/ppermute | solution.py:339
  119.3 1.4 copy-start.3
  127.7 43.2 %all-to-all-start.1 = ((f32[8,64,1536]{2,1,0:T(8,128)}), f32[8,64,1536]{2,1,0:T(8,128)}, u32[]{:S(2)}, u32[]{:S(2)}) async-start(f32[8,64,1536]{2,1,0:T(8,128)} %chips.3), calls=%async_computation.1 | async-start | bytes 6291456 | tf_op jit(solution)/shard_map/all_to_all | solution.py:262
  132.3 11.8 %copy-start.14 = (f32[256,1536]{1,0:T(8,128)S(1)}, f32[256,1536]{1,0:T(8,128)}, u32[]{:S(2)}) copy-start(f32[256,1536]{1,0:T(8,128)} %copy-done.13) | copy-start | bytes 4718596
  132.3 17.1 %copy-start.1 = (f32[256,1536]{1,0:T(8,128)S(1)}, f32[256,1536]{1,0:T(8,128)}, u32[]{:S(2)}) copy-start(f32[256,1536]{1,0:T(8,128)} %copy-done) | copy-start | bytes 4718596
  143.6 5.1 %collective-permute-start.16 = (f32[4,64,1536]{2,1,0:T(8,128)}, f32[4,64,1536]{2,1,0:T(8,128)S(1)}, u32[]{:S(2)}, u32[]{:S(2)}) collective-permute-start(f32[4,64,1536]{2,1,0:T(8,128)} %bitcast.33), channel_id=1, source_target_pairs={{0,1},{1,0},{2,3},{3,2},{4,5},{5,4},{6,7},{7,6},{8,9},{9,8},{10,11... | collective-permute-start | bytes 4718600 | tf_op jit(solution)/shard_map/ppermute | solution.py:231
  144.1 5.3 %collective-permute-start.15 = (f32[4,64,1536]{2,1,0:T(8,128)S(1)}, f32[4,64,1536]{2,1,0:T(8,128)S(1)}, u32[]{:S(2)}, u32[]{:S(2)}) collective-permute-start(f32[4,64,1536]{2,1,0:T(8,128)S(1)} %bitcast.32), channel_id=1, source_target_pairs={{0,1},{1,0},{2,3},{3,2},{4,5},{5,4},{6,7},{7,6},{8,9},{9,8},{10,11... | collective-permute-start | bytes 4718600 | tf_op jit(solution)/shard_map/ppermute | solution.py:231
  174.0 49.2 %all-to-all-start.2 = ((f32[8,64,1536]{2,1,0:T(8,128)}), f32[8,64,1536]{2,1,0:T(8,128)S(1)}, u32[]{:S(2)}, u32[]{:S(2)}) async-start(f32[8,64,1536]{2,1,0:T(8,128)} %chips.2), calls=%async_computation.2 | async-start | bytes 6291456 | tf_op jit(solution)/shard_map/all_to_all | solution.py:267
  178.7 44.5 %collective-permute-start.20 = (f32[64,1536]{1,0:T(8,128)S(1)}, f32[64,1536]{1,0:T(8,128)S(1)}, u32[]{:S(2)}, u32[]{:S(2)}) collective-permute-start(f32[64,1536]{1,0:T(8,128)S(1)} %dynamic-slice_bitcast_fusion), channel_id=1, source_target_pairs={{0,2},{1,3},{2,0},{3,1},{4,6},{5,7},{6,4},{7,5},{8,10},{9,11},{10,... | collective-permute-start | bytes 1179656 | tf_op jit(solution)/shard_map/ppermute | solution.py:347
  180.7 42.5 %copy-start.16 = (f32[2,64,1536]{2,1,0:T(8,128)S(1)}, f32[2,64,1536]{2,1,0:T(8,128)}, u32[]{:S(2)}) copy-start(f32[2,64,1536]{2,1,0:T(8,128)} %reduce_sum.18) | copy-start | bytes 2359300

commit v2 on v1

--- a/solution.py
+++ b/solution.py
@@ -67,74 +67,98 @@
     return (place // DEPTH + plane) % PLANES * DEPTH + (place + z) % DEPTH
 
 
-def units_kernel(pieces, size, place, *refs):
-    blocks, (weight, kept, sent, tokens, held, sems, out_sem) = refs[:-7], refs[-7:]
+def units_kernel(parts, place, *refs):
+    count = len(parts)
+    tokens, (held, sems, out_sems) = refs[-3 - count : -3], refs[-3:]
+    sums = refs[-3 - 3 * count : -3 - count]
+    blocks, weight = refs[: -4 - 3 * count], refs[-4 - 3 * count]
     core, step = place[1], pl.program_id(0)
-    out = pltpu.make_async_copy(held, tokens, out_sem)
+    spans, start = [], 0
+    for size, pieces in parts:
+        spans.append((start, 2 * len(pieces) * size))
+        start += spans[-1][1]
+    outs = [
+        pltpu.make_async_copy(held.at[pl.ds(*span)], rows, out_sems.at[i])
+        for i, (span, rows) in enumerate(zip(spans, tokens))
+    ]
 
     @pl.when(step == 0)
     def _():
         copies = []
-        for i, halves in enumerate(pieces):
-            for half, (array, first) in enumerate(halves):
-                side = (core + half) % 2
-                start = (side * len(pieces) + i) * size
-                copies.append(
-                    pltpu.make_async_copy(
-                        blocks[array].at[pl.ds(first, size)],
-                        held.at[pl.ds(pl.multiple_of(start, 16), size)],
-                        sems.at[len(copies)],
+        for (first_row, _), (size, pieces) in zip(spans, parts):
+            for i, halves in enumerate(pieces):
+                for half, (array, first) in enumerate(halves):
+                    side = (core + half) % 2
+                    start = first_row + (side * len(pieces) + i) * size
+                    copies.append(
+                        pltpu.make_async_copy(
+                            blocks[array].at[pl.ds(first, size)],
+                            held.at[pl.ds(pl.multiple_of(start, 16), size)],
+                            sems.at[len(copies)],
+                        )
                     )
-                )
         for copy in copies:
             copy.start()
         for copy in copies:
             copy.wait()
-        out.start()
+        for out in outs:
+            out.start()
 
     total = lax.dot_general(
         held[...], weight[...], (((1,), (1,)), ((), ())), preferred_element_type=F32
     )
-    rows = kept.shape[0]
-    kept[...] = total[:rows]
-    sent[...] = total[rows:]
+    for i, (first, rows) in enumerate(spans):
+        sums[2 * i][...] = total[first : first + rows // 2]
+        sums[2 * i + 1][...] = total[first + rows // 2 : first + rows]
 
     @pl.when(step == pl.num_programs(0) - 1)
     def _():
-        out.wait()
-
-
-def contract_units(place, arrays, sizes, j, offsets, weight):
-    size, pieces = sizes[j], pieces_of(sizes, j, offsets)
-    names = list(dict.fromkeys(name for halves in pieces for name, _ in halves))
-    pieces = [[(names.index(name), first) for name, first in halves] for halves in pieces]
+        for out in outs:
+            out.wait()
+
+
+def contract_units(place, arrays, sizes, chosen, weight):
+    parts = [(sizes[j], pieces_of(sizes, j, offsets)) for j, offsets in chosen]
+    names = list(
+        dict.fromkeys(name for _, pieces in parts for halves in pieces for name, _ in halves)
+    )
+    parts = [
+        (size, [[(names.index(name), first) for name, first in halves] for halves in pieces])
+        for size, pieces in parts
+    ]
     features, units = weight.shape
-    rows = len(offsets) * size
+    counts = [size * len(pieces) for size, pieces in parts]
+    rows = 2 * sum(counts)
     tile = 512
     out = pl.pallas_call(
-        functools.partial(units_kernel, pieces, size),
+        functools.partial(units_kernel, parts),
         grid=(features // tile,),
         in_specs=[pl.BlockSpec(memory_space=pltpu.SMEM)]
         + [pl.BlockSpec(memory_space=pl.ANY)] * len(names)
         + [pl.BlockSpec((tile, units), lambda n: (n, 0))],
-        out_specs=[pl.BlockSpec((rows, tile), lambda n: (0, n))] * 2
-        + [pl.BlockSpec(memory_space=pltpu.HBM)],
-        out_shape=[jax.ShapeDtypeStruct((rows, features), F32)] * 2
-        + [jax.ShapeDtypeStruct((2 * rows, units), BF16)],
+        out_specs=[pl.BlockSpec((n, tile), lambda n: (0, n)) for n in counts for _ in range(2)]
+        + [pl.BlockSpec(memory_space=pltpu.HBM)] * len(parts),
+        out_shape=[jax.ShapeDtypeStruct((n, features), F32) for n in counts for _ in range(2)]
+        + [jax.ShapeDtypeStruct((2 * n, units), BF16) for n in counts],
         scratch_shapes=[
-            pltpu.VMEM((2 * rows, units), BF16),
-            pltpu.SemaphoreType.DMA((2 * len(pieces),)),
-            pltpu.SemaphoreType.DMA,
+            pltpu.VMEM((rows, units), BF16),
+            pltpu.SemaphoreType.DMA((sum(2 * len(pieces) for _, pieces in parts),)),
+            pltpu.SemaphoreType.DMA((len(parts),)),
         ],
         compiler_params=pltpu.CompilerParams(vmem_limit_bytes=48 * MIB),
         cost_estimate=pl.CostEstimate(
-            flops=4 * rows * units * features,
-            bytes_accessed=2 * features * units + 4 * rows * units + 8 * rows * features,
+            flops=2 * rows * units * features,
+            bytes_accessed=2 * features * units + 4 * rows * units + 4 * rows * features,
             transcendentals=0,
         ),
         name="units",
     )(place, *[arrays[name] for name in names], weight)
-    return [half.reshape(len(offsets), size, features) for half in out[:2]] + [out[2]]
+    made = []
+    for i, (size, pieces) in enumerate(parts):
+        shape = (len(pieces), size, features)
+        kept, sent = (half.reshape(shape) for half in out[2 * i : 2 * i + 2])
+        made.append((kept, sent, out[2 * len(parts) + i]))
+    return made
 
 
 def tokens_kernel(groups, place, *refs):
@@ -216,51 +240,42 @@
     )(place, *blocks, mine, other)
 
 
-def chips_kernel(order, near_kept, near_got, far_kept, far_got, out):
-    @pl.when(pl.program_id(0) < len(NEAR))
-    def _():
-        out[...] = near_kept[...] + near_got[...]
-
-    @pl.when(pl.program_id(0) >= len(NEAR))
-    def _():
-        out[...] = far_kept[...] + far_got[...]
+def chips_kernel(place, near_kept, near_got, far_kept, far_got, out, held, sems):
+    copies = []
+    sums = ((near_kept, near_got), (far_kept, far_got))
+    for i, offset in enumerate(NEAR + FAR):
+        kept, got = sums[i // len(NEAR)]
+        held[i] = kept[i % len(NEAR)] + got[i % len(NEAR)]
+        copies.append(
+            pltpu.make_async_copy(held.at[i], out.at[owner(place[0], *offset)], sems.at[i])
+        )
+        copies[-1].start()
+    for copy in copies:
+        copy.wait()
 
 
 def chip_sums(place, near, far):
     (near_kept, near_sent), (far_kept, far_sent) = near, far
     near_got, far_got = (lax.ppermute(sent, "col", CORE) for sent in (near_sent, far_sent))
-    _, size, features = near_kept.shape
-    order = jnp.stack([owner(place[0], *offset) for offset in NEAR + FAR])
-    block = (1, size, features)
-    near = pl.BlockSpec(block, lambda i, order: (jnp.minimum(i, 3), 0, 0))
-    far = pl.BlockSpec(block, lambda i, order: (jnp.maximum(i - 4, 0), 0, 0))
+    size, features = near_kept.shape[1:]
     return pl.pallas_call(
         chips_kernel,
-        grid_spec=pltpu.PrefetchScalarGridSpec(
-            num_scalar_prefetch=1,
-            grid=(ROWS,),
-            in_specs=[near, near, far, far],
-            out_specs=pl.BlockSpec(block, lambda i, order: (order[i], 0, 0)),
-        ),
+        in_specs=[pl.BlockSpec(memory_space=pltpu.SMEM)]
+        + [pl.BlockSpec(memory_space=pltpu.VMEM)] * 4,
+        out_specs=pl.BlockSpec(memory_space=pl.ANY),
         out_shape=jax.ShapeDtypeStruct((ROWS, size, features), F32),
-        compiler_params=pltpu.CompilerParams(vmem_limit_bytes=32 * MIB),
+        scratch_shapes=[
+            pltpu.VMEM((ROWS, size, features), F32),
+            pltpu.SemaphoreType.DMA((ROWS,)),
+        ],
+        compiler_params=pltpu.CompilerParams(vmem_limit_bytes=24 * MIB),
         cost_estimate=pl.CostEstimate(
             flops=ROWS * size * features,
             bytes_accessed=12 * ROWS * size * features,
             transcendentals=0,
         ),
         name="chips",
-    )(order, near_kept, near_got, far_kept, far_got)
-
-
-def gather_along_y(rows):
-    copies = jnp.concatenate([rows] * 4)
-    return lax.all_to_all(copies, "col", 0, 0, axis_index_groups=Y_GROUPS, tiled=True)
-
-
-def sum_along_y(chip):
-    parts = lax.all_to_all(chip, "col", 0, 0, axis_index_groups=Y_GROUPS, tiled=True)
-    return jnp.sum(parts.reshape(4, 2, *chip.shape[1:]), axis=0)
+    )(place, near_kept, near_got, far_kept, far_got)
 
 
 def sum_direct(chip):
@@ -279,16 +294,17 @@
         base += size
     gathered, groups = [], []
 
-    def multiply(j, offsets):
-        kept, sent, rows = contract_units(place, arrays, sizes, j, offsets, weight)
-        gathered.append(rows)
-        groups.append((sum(sizes[:j]), sizes[j], offsets))
-        return kept, sent
-
-    near, far = [None] * count, [None] * count
-    chips = []
+    def multiply(*chosen):
+        made = contract_units(place, arrays, sizes, chosen, weight)
+        for (j, offsets), (_, _, rows) in zip(chosen, made):
+            gathered.append(rows)
+            groups.append((sum(sizes[:j]), sizes[j], offsets))
+        return [part[:2] for part in made]
+
+    near, far, sums = [None] * count, [None] * count, []
+    beside = lax.ppermute(inputs, "col", BESIDE)
     for k in range(count + 1):
-        started, extra = [], ()
+        started = []
 
         def exchange():
             parts = [arrays["across", k - 1]] if k else []
@@ -298,53 +314,64 @@
             arrays["up", k], arrays["down", k] = send(both, UP), send(both, DOWN)
             started.extend([("up", k), ("down", k)])
 
-        if k:
-            size = sizes[k - 1]
-            first = 2 * sizes[k - 2] if k > 1 else 0
-            ready = [
-                send(arrays["up", k - 1][first : first + size], UP),
-                send(arrays["down", k - 1][first + size : first + 2 * size], DOWN),
-            ]
-            if k == 1:
-                extra = [lax.ppermute(inputs, "col", BESIDE)]
-            if k == count:
-                exchange()
-            if k > 1:
-                far[k - 2] = multiply(k - 2, FAR)
-                chips.append(chip_sums(place, near[k - 2], far[k - 2]))
-            ready, extra, arrays["across", k - 1], near[k - 1], rest = fence(
-                ready, extra, arrays["across", k - 1], near[k - 1], [arrays["own", min(k, count - 1)]]
+        if k == 0:
+            exchange()
+            arrays["across", k] = send(arrays["own", k], CROSS)
+            pair = jnp.concatenate([inputs, beside])
+            copies = jnp.broadcast_to(pair, (4, *pair.shape))
+            arrays["up", k], arrays["down", k], copies, arrays["own", 1] = fence(
+                arrays["up", k], arrays["down", k], copies, arrays["own", 1]
             )
-            arrays["own", min(k, count - 1)] = rest[0]
-            arrays["far_up", k - 1], arrays["far_down", k - 1] = ready
-            arrays["across_far", k - 1] = send(jnp.concatenate(ready), CROSS)
+            mine = lax.all_to_all(copies, "col", 0, 0, axis_index_groups=Y_GROUPS, tiled=True)
+            mine = mine.reshape(-1, mine.shape[-1])
+            continue
+        size = sizes[k - 1]
+        first = 2 * sizes[k - 2] if k > 1 else 0
+        ready = [
+            send(arrays["up", k - 1][first : first + size], UP),
+            send(arrays["down", k - 1][first + size : first + 2 * size], DOWN),
+        ]
+        if k == count:
+            exchange()
+        made = []
+        if k > 1:
+            made = multiply((k - 2, FAR))
+        last = min(k, count - 1)
+        ready, made, arrays["across", k - 1], arrays["own", last] = fence(
+            ready, made, arrays["across", k - 1], arrays["own", last]
+        )
+        if made:
+            far[k - 2] = made[0]
+            made = [chip_sums(place, near[k - 2], far[k - 2])]
+        arrays["far_up", k - 1], arrays["far_down", k - 1] = ready
+        arrays["across_far", k - 1] = send(jnp.concatenate(ready), CROSS)
+        if k < count:
             started.append(("across_far", k - 1))
-            near[k - 1] = multiply(k - 1, NEAR)
-            if k == 1:
-                mine = gather_along_y(jnp.concatenate([inputs, extra[0]]))
+        if k == 1:
+            near[0] = multiply((0, NEAR))[0]
         if k < count:
             exchange()
             arrays["across", k] = send(arrays["own", k], CROSS)
             started.append(("across", k))
+        if k == count:
+            started = []
         held = [arrays[name] for name in started]
         later = [arrays["own", k + 1]] if k + 1 < count else []
-        extra = [mine] if k == count else []
-        held, later, near, extra = fence(held, later, near, extra)
+        extra = [mine] if k == 1 else []
+        held, later, near, extra, made = fence(held, later, near, extra, made)
+        if k == count:
+            near[k - 1] = multiply((k - 1, NEAR))[0]
+        sums += [sum_direct(chip) for chip in made]
         arrays.update(zip(started, held))
         if later:
             arrays["own", k + 1] = later[0]
         if extra:
             mine = extra[0]
-    far[count - 1] = multiply(count - 1, FAR)
-    other = lax.ppermute(mine, "col", CORE)
+            other = lax.ppermute(mine, "col", CORE)
+    far[count - 1] = multiply((count - 1, FAR))[0]
     chip = chip_sums(place, near[-1], far[-1])
-    first = jnp.concatenate([sum_along_y(chip) for chip in chips], axis=1)
-    chip, mine, other, first = fence(chip, mine, other, first)
-    last = sum_direct(chip)
-    beside = place[2]
-    own = lax.dynamic_index_in_dim(first, beside, 0, keepdims=False)
-    others = lax.dynamic_index_in_dim(first, 1 - beside, 0, keepdims=False)
-    sums = [(own + lax.ppermute(others, "col", BESIDE)).astype(BF16), last]
+    chip, mine, other = fence(chip, mine, other)
+    sums.append(sum_direct(chip))
     weight_grad = contract_tokens(place, gathered, groups, mine, other)
     input_grad = jnp.concatenate(sums, axis=0)
     return input_grad, weight_grad

time: 225 us -> 202 us (0.90)
  local copies, waits for them, and re-layouts: 20 us -> 11.7 us
  Pallas kernels: 81.5 us -> 73.9 us
  waiting for transfers between devices: 72.1 us -> 67.8 us
    all_to_all x1 -> x2, waiting for transfers between devices: 0.01 us -> 26.8 us  [sum_direct(): lax.all_to_all(chip, 'col', 0, 0, axis_index_groups=CHIP_GROUPS, tiled=True)]
    all_to_all x2 -> x1, waiting for transfers between devices: 17.5 us -> 0.01 us  [local(): lax.all_to_all(copies, 'col', 0, 0, axis_index_groups=Y_GROUPS, tiled=True)]
    ppermute x2 -> x1, waiting for transfers between devices: 16.9 us -> 7.76 us  [local(): beside = lax.ppermute(inputs, 'col', BESIDE)]
    unnamed x42 -> x25, local copies, waits for them, and re-layouts: 13.6 us -> 4.45 us
    pallas_call x6, Pallas kernels: 53 us -> 45.5 us  [the longest x4 40.9 us: contract_units(): pl.pallas_call(functools.partial(units_kernel, parts), grid=(features //...]
    all_to_all x1 -> x2, starting transfers between devices: 3.65 us -> 8.32 us  [sum_direct(): lax.all_to_all(chip, 'col', 0, 0, axis_index_groups=CHIP_GROUPS, tiled=True)]
    all_to_all x2 -> x1, starting transfers between devices: 9.31 us -> 4.64 us  [local(): lax.all_to_all(copies, 'col', 0, 0, axis_index_groups=Y_GROUPS, tiled=True)]
    reduce_sum x1 -> x0, other arithmetic: 3.11 us -> none  [sum_along_y(): return jnp.sum(parts.reshape(4, 2, *chip.shape[1:]), axis=0)]
  transfers between devices with their start and end apart: 24 -> 23, of which waited for: 11 -> 10; matrix products, arithmetic and copies ran while one was open for 7% -> 5% of each run, Pallas kernels for 36% -> 37%
where the time goes in v2:
time: 202 us
  Pallas kernels  73.9 us (37%)
  waiting for transfers between devices  67.8 us (34%)
  starting transfers between devices  42.1 us (21%)
  local copies, waits for them, and re-layouts  11.7 us (6%)
  other arithmetic  5.28 us (3%)
    pallas_call x4, Pallas kernels, contract_units(): pl.pallas_call(functools.partial(units_kernel, parts), grid=(features //...  40.9 us
    ppermute x14, waiting for transfers between devices, send(): return lax.ppermute(value, 'row', move)  29.6 us
    pallas_call x1, Pallas kernels, contract_tokens(): pl.pallas_call(functools.partial(tokens_kernel, groups), grid=(units // t...  28.3 us
    all_to_all x2, waiting for transfers between devices, sum_direct(): lax.all_to_all(chip, 'col', 0, 0, axis_index_groups=CHIP_GROUPS, tiled=True)  26.8 us
    ppermute x14, starting transfers between devices, send(): return lax.ppermute(value, 'row', move)  26.7 us
    all_to_all x2, starting transfers between devices, sum_direct(): lax.all_to_all(chip, 'col', 0, 0, axis_index_groups=CHIP_GROUPS, tiled=True)  8.32 us
    ppermute x1, waiting for transfers between devices, local(): beside = lax.ppermute(inputs, 'col', BESIDE)  7.76 us
    pallas_call x2, Pallas kernels, chip_sums(): pl.pallas_call(chips_kernel, in_specs=[pl.BlockSpec(memory_space=pltpu.SM...  4.67 us
  transfers between devices with their start and end apart: 23, of which 10 were waited for; matrix products, arithmetic and copies ran while one was open for 5% of the time, Pallas kernels for 37%

profile of v2, /device:TPU:0, one launch (start us, length us, event | category | flops | bytes accessed | tf_op | source)
XLA Modules:
  0.0 201.7 jit_solution(10825133303678387336)
XLA Ops:
  0.6 1.5 fusion
  2.2 2.1 %collective-permute-start = (bf16[128,3072]{1,0:T(8,128)(2,1)S(1)}, bf16[128,3072]{1,0:T(8,128)(2,1)S(1)}, u32[]{:S(2)}, u32[]{:S(2)}) collective-permute-start(bf16[128,3072]{1,0:T(8,128)(2,1)S(1)} %pad_maximum_fusion.refs_0_), channel_id=1, source_target_pairs={{0,16},{16,32},{32,48},{48,0},{64,80},{80,96},{96,112},{112,64},{1... | collective-permute-start | bytes 2359304 | tf_op jit(solution)/shard_map/ppermute | solution.py:63
  4.2 2.2 %collective-permute-start.1 = (bf16[128,3072]{1,0:T(8,128)(2,1)S(1)}, bf16[128,3072]{1,0:T(8,128)(2,1)S(1)}, u32[]{:S(2)}, u32[]{:S(2)}) collective-permute-start(bf16[128,3072]{1,0:T(8,128)(2,1)S(1)} %pad_maximum_fusion.refs_0_), channel_id=1, source_target_pairs={{0,48},{16,0},{32,16},{48,32},{64,112},{80,64},{96,80},{112,96},{1... | collective-permute-start | bytes 2359304 | tf_op jit(solution)/shard_map/ppermute | solution.py:63
  6.4 1.5 collective-permute-start.2
  7.9 2.7 %collective-permute-start.5 = (bf16[128,3072]{1,0:T(8,128)(2,1)S(1)}, bf16[128,3072]{1,0:T(8,128)(2,1)S(1)}, u32[]{:S(2)}, u32[]{:S(2)}) collective-permute-start(bf16[128,3072]{1,0:T(8,128)(2,1)S(1)} %pad_maximum_fusion.refs_0_), channel_id=1, source_target_pairs={{0,64},{16,80},{32,96},{48,112},{64,0},{80,16},{96,32},{112,48},{1... | collective-permute-start | bytes 2359304 | tf_op jit(solution)/shard_map/ppermute | solution.py:63
  10.7 7.8 %collective-permute-done.2 = bf16[128,1536]{1,0:T(8,128)(2,1)S(1)} collective-permute-done((bf16[128,1536]{1,0:T(8,128)(2,1)S(1)}, bf16[128,1536]{1,0:T(8,128)(2,1)S(1)}, u32[]{:S(2)}, u32[]{:S(2)}) %collective-permute-start.2) | collective-permute-done | bytes 393248 | tf_op jit(solution)/shard_map/ppermute | solution.py:305
  18.5 5.4 %collective-permute-done.refs_1_ = bf16[128,3072]{1,0:T(8,128)(2,1)S(1)} collective-permute-done((bf16[128,3072]{1,0:T(8,128)(2,1)S(1)}, bf16[128,3072]{1,0:T(8,128)(2,1)S(1)}, u32[]{:S(2)}, u32[]{:S(2)}) %collective-permute-start) | collective-permute-done | bytes 786464 | tf_op jit(solution)/shard_map/ppermute | solution.py:63
  23.9 2.1 %broadcast_in_dim.3 = bf16[4,256,1536]{2,1,0:T(8,128)(2,1)} broadcast(bf16[256,1536]{1,0:T(8,128)(2,1)S(1)} %pad_maximum_fusion.1), dimensions={1,2} | broadcast | bytes 3932160 | tf_op jit(solution)/shard_map/broadcast_in_dim | solution.py:321
  26.0 0.8 slice.28
  26.7 1.1 collective-permute-start.3
  27.9 2.2 %collective-permute-start.4 = (bf16[64,3072]{1,0:T(8,128)(2,1)S(1)}, bf16[64,3072]{1,0:T(8,128)(2,1)S(1)}, u32[]{:S(2)}, u32[]{:S(2)}) collective-permute-start(bf16[64,3072]{1,0:T(8,128)(2,1)S(1)} %slice.29), channel_id=1, source_target_pairs={{0,48},{16,0},{32,16},{48,32},{64,112},{80,64},{96,80},{112,96},{1... | collective-permute-start | bytes 1179656 | tf_op jit(solution)/shard_map/ppermute | solution.py:63
  30.1 4.6 %all-to-all-start = ((bf16[4,256,1536]{2,1,0:T(8,128)(2,1)}), bf16[4,256,1536]{2,1,0:T(8,128)(2,1)}, u32[]{:S(2)}, u32[]{:S(2)}) async-start(bf16[4,256,1536]{2,1,0:T(8,128)(2,1)} %broadcast_in_dim.3), calls=%async_computation | async-start | bytes 6291456 | tf_op jit(solution)/shard_map/all_to_all | solution.py:325
  34.7 1.3 collective-permute-done.5.refs_3_
  36.1 2.4 %collective-permute-done.3.refs_0_ = bf16[64,3072]{1,0:T(8,128)(2,1)S(1)} collective-permute-done((bf16[64,3072]{1,0:T(8,128)(2,1)}, bf16[64,3072]{1,0:T(8,128)(2,1)S(1)}, u32[]{:S(2)}, u32[]{:S(2)}) %collective-permute-start.3) | collective-permute-done | bytes 393248 | tf_op jit(solution)/shard_map/ppermute | solution.py:63
  38.5 1.0 constant_dynamic-update-slice_fusion.1
  39.5 0.9 constant_dynamic-update-slice_fusion
  40.4 0.7 collective-permute-start.7
  41.1 2.6 %collective-permute-start.8 = (bf16[256,3072]{1,0:T(8,128)(2,1)}, bf16[256,3072]{1,0:T(8,128)(2,1)}, u32[]{:S(2)}, u32[]{:S(2)}) collective-permute-start(bf16[256,3072]{1,0:T(8,128)(2,1)} %constant_dynamic-update-slice_fusion), channel_id=1, source_target_pairs={{0,48},{16,0},{32,16},{48,32},{64,112},{80,64},{96,80},{112,96},{1... | collective-permute-start | bytes 4718600 | tf_op jit(solution)/shard_map/ppermute | solution.py:63
  43.6 0.9 pad_maximum_fusion.3
  44.6 3.0 %collective-permute-start.6 = (bf16[128,3072]{1,0:T(8,128)(2,1)}, bf16[128,3072]{1,0:T(8,128)(2,1)}, u32[]{:S(2)}, u32[]{:S(2)}) collective-permute-start(bf16[128,3072]{1,0:T(8,128)(2,1)} %pad_maximum_fusion.3), channel_id=1, source_target_pairs={{0,64},{16,80},{32,96},{48,112},{64,0},{80,16},{96,32},{112,48},{1... | collective-permute-start | bytes 2359304 | tf_op jit(solution)/shard_map/ppermute | solution.py:63
  47.6 0.5 collective-permute-start.9
  48.2 1.1 copy-done.1
  49.3 1.1 copy-done.7
  50.5 1.1 copy-done.9
  51.6 10.2 %units.4 = (f32[256,1536]{1,0:T(8,128)S(1)}, f32[256,1536]{1,0:T(8,128)}, bf16[512,3072]{1,0:T(8,128)(2,1)}) custom-call(s32[3]{0:T(128)S(1)} %pad_add_fusion.place, bf16[128,3072]{1,0:T(8,128)(2,1)S(1)} %pad_maximum_fusion.refs_0_, bf16[128,3072]{1,0:T(8,128)(2,1)S(1)} %copy-done.7, bf16[128,3072]{1,0:T(8,128)(2,1)S(1)} %copy-done.9, ...), custom_call_target="tpu_custom_call" | custom-call | flops 4831838208 | bytes 18874368 | tf_op jit(solution)/shard_map/units/pallas_call | solution.py:133
  61.8 5.1 %collective-permute-done.6.refs_4_ = bf16[128,3072]{1,0:T(8,128)(2,1)} collective-permute-done((bf16[128,3072]{1,0:T(8,128)(2,1)}, bf16[128,3072]{1,0:T(8,128)(2,1)}, u32[]{:S(2)}, u32[]{:S(2)}) %collective-permute-start.6) | collective-permute-done | bytes 786464 | tf_op jit(solution)/shard_map/ppermute | solution.py:63
  66.9 13.6 %collective-permute-done.9.refs_3_ = bf16[128,3072]{1,0:T(8,128)(2,1)} collective-permute-done((bf16[128,3072]{1,0:T(8,128)(2,1)S(1)}, bf16[128,3072]{1,0:T(8,128)(2,1)}, u32[]{:S(2)}, u32[]{:S(2)}) %collective-permute-start.9) | collective-permute-done | bytes 786464 | tf_op jit(solution)/shard_map/ppermute | solution.py:63
  80.5 1.0 slice.30
  81.6 1.0 slice.31
  82.7 3.3 %collective-permute-start.12 = (bf16[64,3072]{1,0:T(8,128)(2,1)S(1)}, bf16[64,3072]{1,0:T(8,128)(2,1)S(1)}, u32[]{:S(2)}, u32[]{:S(2)}) collective-permute-start(bf16[64,3072]{1,0:T(8,128)(2,1)S(1)} %slice.31), channel_id=1, source_target_pairs={{0,48},{16,0},{32,16},{48,32},{64,112},{80,64},{96,80},{112,96},{1... | collective-permute-start | bytes 1179656 | tf_op jit(solution)/shard_map/ppermute | solution.py:63
  85.9 9.9 %units.5 = (f32[256,1536]{1,0:T(8,128)S(1)}, f32[256,1536]{1,0:T(8,128)S(1)}, bf16[512,3072]{1,0:T(8,128)(2,1)}) custom-call(s32[3]{0:T(128)S(1)} %pad_add_fusion.place, bf16[64,3072]{1,0:T(8,128)(2,1)S(1)} %collective-permute-done.3.refs_0_, bf16[64,3072]{1,0:T(8,128)(2,1)S(1)} %copy-done.3, bf16[256,3072]{1,0:T(8,128)(2,1)} %collective-permute-done.7.refs_2_.refs_1_, ...), custom_call_target="tpu_custom_call" | custom-call | flops 4831838208 | bytes 18874368 | tf_op jit(solution)/shard_map/units/pallas_call | solution.py:133
  95.9 0.6 collective-permute-start.13
  96.5 3.2 %collective-permute-start.16 = (bf16[128,3072]{1,0:T(8,128)(2,1)}, bf16[128,3072]{1,0:T(8,128)(2,1)}, u32[]{:S(2)}, u32[]{:S(2)}) collective-permute-start(bf16[128,3072]{1,0:T(8,128)(2,1)} %collective-permute-done.9.refs_3_), channel_id=1, source_target_pairs={{0,48},{16,0},{32,16},{48,32},{64,112},{80,64},{96,80},{112,96},{1... | collective-permute-start | bytes 2359304 | tf_op jit(solution)/shard_map/ppermute | solution.py:63
  99.7 1.0 pad_maximum_fusion.4
  100.7 3.0 %collective-permute-start.17 = (bf16[128,3072]{1,0:T(8,128)(2,1)}, bf16[128,3072]{1,0:T(8,128)(2,1)}, u32[]{:S(2)}, u32[]{:S(2)}) collective-permute-start(bf16[128,3072]{1,0:T(8,128)(2,1)} %pad_maximum_fusion.4), channel_id=1, source_target_pairs={{0,64},{16,80},{32,96},{48,112},{64,0},{80,16},{96,32},{112,48},{1... | collective-permute-start | bytes 2359304 | tf_op jit(solution)/shard_map/ppermute | solution.py:63
  103.7 2.3 %chips.2 = f32[8,64,1536]{2,1,0:T(8,128)} custom-call(s32[3]{0:T(128)S(1)} %pad_add_fusion.place, f32[4,64,1536]{2,1,0:T(8,128)S(1)} %bitcast.12, f32[4,64,1536]{2,1,0:T(8,128)S(1)} %collective-permute-done.10.near_got, f32[4,64,1536]{2,1,0:T(8,128)S(1)} %bitcast.13, f32[4,64,1536]{2,1,0:T(8,128)S(1)} %collective-permute-done.13.far_got), custom_call_target="tpu_custom_call" | custom-call | flops 786432 | bytes 9437184 | tf_op jit(solution)/shard_map/chips/pallas_call | solution.py:261
  106.0 4.7 %all-to-all-start.1 = ((f32[8,64,1536]{2,1,0:T(8,128)}), f32[8,64,1536]{2,1,0:T(8,128)}, u32[]{:S(2)}, u32[]{:S(2)}) async-start(f32[8,64,1536]{2,1,0:T(8,128)} %chips.2), calls=%async_computation.1 | async-start | bytes 6291456 | tf_op jit(solution)/shard_map/all_to_all | solution.py:282
  110.7 10.0 %units.6 = (f32[256,1536]{1,0:T(8,128)S(1)}, f32[256,1536]{1,0:T(8,128)S(1)}, bf16[512,3072]{1,0:T(8,128)(2,1)}) custom-call(s32[3]{0:T(128)S(1)} %pad_add_fusion.place, bf16[128,3072]{1,0:T(8,128)(2,1)S(1)} %pad_maximum_fusion.2.refs_0_, bf16[256,3072]{1,0:T(8,128)(2,1)} %collective-permute-done.7.refs_2_.refs_1_, ...), custom_call_target="tpu_custom_call" | custom-call | flops 4831838208 | bytes 18874368 | tf_op jit(solution)/shard_map/units/pallas_call | solution.py:133
  121.0 1.8 collective-permute-done.17.refs_4_
  122.8 10.8 %units.7 = (f32[256,1536]{1,0:T(8,128)S(1)}, f32[256,1536]{1,0:T(8,128)}, bf16[512,3072]{1,0:T(8,128)(2,1)}) custom-call(s32[3]{0:T(128)S(1)} %pad_add_fusion.place, bf16[64,3072]{1,0:T(8,128)(2,1)S(1)} %collective-permute-done.11.refs_0_, bf16[64,3072]{1,0:T(8,128)(2,1)S(1)} %copy-done.5, bf16[128,3072]{1,0:T(8,128)(2,1)} %collective-permute-done.15.refs_2_, ...), custom_call_target="tpu_custom_call" | custom-call | flops 4831838208 | bytes 18874368 | tf_op jit(solution)/shard_map/units/pallas_call | solution.py:133
  133.8 3.6 %collective-permute-done.18.far_got = f32[4,64,1536]{2,1,0:T(8,128)S(1)} collective-permute-done((f32[4,64,1536]{2,1,0:T(8,128)}, f32[4,64,1536]{2,1,0:T(8,128)S(1)}, u32[]{:S(2)}, u32[]{:S(2)}) %collective-permute-start.18) | collective-permute-done | bytes 1572896 | tf_op jit(solution)/shard_map/ppermute | solution.py:259
  137.4 2.4 %chips.3 = f32[8,64,1536]{2,1,0:T(8,128)} custom-call(s32[3]{0:T(128)S(1)} %pad_add_fusion.place, f32[4,64,1536]{2,1,0:T(8,128)S(1)} %bitcast.14, f32[4,64,1536]{2,1,0:T(8,128)S(1)} %collective-permute-done.14.near_got, f32[4,64,1536]{2,1,0:T(8,128)S(1)} %bitcast.15, f32[4,64,1536]{2,1,0:T(8,128)S(1)} %collective-permute-done.18.far_got), custom_call_target="tpu_custom_call" | custom-call | flops 786432 | bytes 9437184 | tf_op jit(solution)/shard_map/chips/pallas_call | solution.py:261
  139.7 19.0 %all-to-all-done.1 = f32[8,64,1536]{2,1,0:T(8,128)} async-done(((f32[8,64,1536]{2,1,0:T(8,128)}), f32[8,64,1536]{2,1,0:T(8,128)}, u32[]{:S(2)}, u32[]{:S(2)}) %all-to-all-start.1) | async-done | bytes 3145760 | tf_op jit(solution)/shard_map/all_to_all | solution.py:282
  158.7 3.6 %all-to-all-start.2 = ((f32[8,64,1536]{2,1,0:T(8,128)}), f32[8,64,1536]{2,1,0:T(8,128)S(1)}, u32[]{:S(2)}, u32[]{:S(2)}) async-start(f32[8,64,1536]{2,1,0:T(8,128)} %chips.3), calls=%async_computation.2 | async-start | bytes 6291456 | tf_op jit(solution)/shard_map/all_to_all | solution.py:282
  162.3 28.3 %tokens.1 = bf16[1536,3072]{1,0:T(8,128)(2,1)} custom-call(s32[3]{0:T(128)} %copy-done.10, bf16[512,3072]{1,0:T(8,128)(2,1)} %get-tuple-element.70.refs_0_, bf16[512,3072]{1,0:T(8,128)(2,1)} %get-tuple-element.71.refs_1_, bf16[512,3072]{1,0:T(8,128)(2,1)} %get-tuple-element.72.refs_2_, bf16[512,3072]{1,0:T(8,128)(2,1)} %get-tuple-element.73.refs_3_, ...), custom_call_target="tpu_custom_call" | custom-call | flops 19327352832 | bytes 28311552 | tf_op jit(solution)/shard_map/tokens/pallas_call | solution.py:220
  190.7 2.1 %reduce_sum.18 = bf16[64,1536]{1,0:T(8,128)(2,1)S(1)} reduce(f32[8,64,1536]{2,1,0:T(8,128)} %all-to-all-done.1, f32[]{:T(128)} %constant.38.clone.1), dimensions={0}, to_apply=%region_0.1 | reduce | flops 688128 | bytes 3342340 | tf_op jit(solution)/shard_map/reduce_sum | solution.py:283
  192.8 7.8 %all-to-all-done.2 = f32[8,64,1536]{2,1,0:T(8,128)S(1)} async-done(((f32[8,64,1536]{2,1,0:T(8,128)}), f32[8,64,1536]{2,1,0:T(8,128)S(1)}, u32[]{:S(2)}, u32[]{:S(2)}) %all-to-all-start.2) | async-done | bytes 3145760 | tf_op jit(solution)/shard_map/all_to_all | solution.py:282
  200.9 0.8 pad_maximum_fusion.5
  (46 shorter events, 1.0 us)
Async XLA Ops:
  2.1 4.3 %copy-start.11 = (bf16[128,1536]{1,0:T(8,128)(2,1)S(1)}, bf16[128,1536]{1,0:T(8,128)(2,1)}, u32[]{:S(2)}) copy-start(bf16[128,1536]{1,0:T(8,128)(2,1)} %param.3) | copy-start | bytes 1179652
  2.2 21.7 %collective-permute-start = (bf16[128,3072]{1,0:T(8,128)(2,1)S(1)}, bf16[128,3072]{1,0:T(8,128)(2,1)S(1)}, u32[]{:S(2)}, u32[]{:S(2)}) collective-permute-start(bf16[128,3072]{1,0:T(8,128)(2,1)S(1)} %pad_maximum_fusion.refs_0_), channel_id=1, source_target_pairs={{0,16},{16,32},{32,48},{48,0},{64,80},{80,96},{96,112},{112,64},{1... | collective-permute-start | bytes 2359304 | tf_op jit(solution)/shard_map/ppermute | solution.py:63
  4.2 19.7 %collective-permute-start.1 = (bf16[128,3072]{1,0:T(8,128)(2,1)S(1)}, bf16[128,3072]{1,0:T(8,128)(2,1)S(1)}, u32[]{:S(2)}, u32[]{:S(2)}) collective-permute-start(bf16[128,3072]{1,0:T(8,128)(2,1)S(1)} %pad_maximum_fusion.refs_0_), channel_id=1, source_target_pairs={{0,48},{16,0},{32,16},{48,32},{64,112},{80,64},{96,80},{112,96},{1... | collective-permute-start | bytes 2359304 | tf_op jit(solution)/shard_map/ppermute | solution.py:63
  6.4 12.0 %collective-permute-start.2 = (bf16[128,1536]{1,0:T(8,128)(2,1)S(1)}, bf16[128,1536]{1,0:T(8,128)(2,1)S(1)}, u32[]{:S(2)}, u32[]{:S(2)}) collective-permute-start(bf16[128,1536]{1,0:T(8,128)(2,1)S(1)} %copy-done.11), channel_id=1, source_target_pairs={{0,2},{1,3},{2,0},{3,1},{4,6},{5,7},{6,4},{7,5},{8,10},{9,11},{10,... | collective-permute-start | bytes 1179656 | tf_op jit(solution)/shard_map/ppermute | solution.py:305
  7.9 28.1 %collective-permute-start.5 = (bf16[128,3072]{1,0:T(8,128)(2,1)S(1)}, bf16[128,3072]{1,0:T(8,128)(2,1)S(1)}, u32[]{:S(2)}, u32[]{:S(2)}) collective-permute-start(bf16[128,3072]{1,0:T(8,128)(2,1)S(1)} %pad_maximum_fusion.refs_0_), channel_id=1, source_target_pairs={{0,64},{16,80},{32,96},{48,112},{64,0},{80,16},{96,32},{112,48},{1... | collective-permute-start | bytes 2359304 | tf_op jit(solution)/shard_map/ppermute | solution.py:63
  23.9 2.1 %copy-start.6 = (bf16[128,3072]{1,0:T(8,128)(2,1)}, bf16[128,3072]{1,0:T(8,128)(2,1)S(1)}, u32[]{:S(2)}) copy-start(bf16[128,3072]{1,0:T(8,128)(2,1)S(1)} %collective-permute-done.refs_1_) | copy-start | bytes 2359300
  23.9 4.0 %copy-start.8 = (bf16[128,3072]{1,0:T(8,128)(2,1)}, bf16[128,3072]{1,0:T(8,128)(2,1)S(1)}, u32[]{:S(2)}) copy-start(bf16[128,3072]{1,0:T(8,128)(2,1)S(1)} %collective-permute-done.1.refs_2_) | copy-start | bytes 2359300
  26.7 11.7 %collective-permute-start.3 = (bf16[64,3072]{1,0:T(8,128)(2,1)}, bf16[64,3072]{1,0:T(8,128)(2,1)S(1)}, u32[]{:S(2)}, u32[]{:S(2)}) collective-permute-start(bf16[64,3072]{1,0:T(8,128)(2,1)} %slice.28), channel_id=1, source_target_pairs={{0,16},{16,32},{32,48},{48,0},{64,80},{80,96},{96,112},{112,64},{1... | collective-permute-start | bytes 1179656 | tf_op jit(solution)/shard_map/ppermute | solution.py:63
  27.9 10.6 %collective-permute-start.4 = (bf16[64,3072]{1,0:T(8,128)(2,1)S(1)}, bf16[64,3072]{1,0:T(8,128)(2,1)S(1)}, u32[]{:S(2)}, u32[]{:S(2)}) collective-permute-start(bf16[64,3072]{1,0:T(8,128)(2,1)S(1)} %slice.29), channel_id=1, source_target_pairs={{0,48},{16,0},{32,16},{48,32},{64,112},{80,64},{96,80},{112,96},{1... | collective-permute-start | bytes 1179656 | tf_op jit(solution)/shard_map/ppermute | solution.py:63
  30.1 50.4 %all-to-all-start = ((bf16[4,256,1536]{2,1,0:T(8,128)(2,1)}), bf16[4,256,1536]{2,1,0:T(8,128)(2,1)}, u32[]{:S(2)}, u32[]{:S(2)}) async-start(bf16[4,256,1536]{2,1,0:T(8,128)(2,1)} %broadcast_in_dim.3), calls=%async_computation | async-start | bytes 6291456 | tf_op jit(solution)/shard_map/all_to_all | solution.py:325
  36.1 4.3 %copy-start = (bf16[128,3072]{1,0:T(8,128)(2,1)}, bf16[128,3072]{1,0:T(8,128)(2,1)S(1)}, u32[]{:S(2)}) copy-start(bf16[128,3072]{1,0:T(8,128)(2,1)S(1)} %collective-permute-done.5.refs_3_) | copy-start | bytes 2359300
  38.5 5.2 %copy-start.2 = (bf16[64,3072]{1,0:T(8,128)(2,1)}, bf16[64,3072]{1,0:T(8,128)(2,1)S(1)}, u32[]{:S(2)}) copy-start(bf16[64,3072]{1,0:T(8,128)(2,1)S(1)} %collective-permute-done.4.refs_1_) | copy-start | bytes 1179652
  40.4 40.1 %collective-permute-start.7 = (bf16[256,3072]{1,0:T(8,128)(2,1)}, bf16[256,3072]{1,0:T(8,128)(2,1)}, u32[]{:S(2)}, u32[]{:S(2)}) collective-permute-start(bf16[256,3072]{1,0:T(8,128)(2,1)} %constant_dynamic-update-slice_fusion), channel_id=1, source_target_pairs={{0,16},{16,32},{32,48},{48,0},{64,80},{80,96},{96,112},{112,64},{1... | collective-permute-start | bytes 4718600 | tf_op jit(solution)/shard_map/ppermute | solution.py:63
  41.1 39.5 %collective-permute-start.8 = (bf16[256,3072]{1,0:T(8,128)(2,1)}, bf16[256,3072]{1,0:T(8,128)(2,1)}, u32[]{:S(2)}, u32[]{:S(2)}) collective-permute-start(bf16[256,3072]{1,0:T(8,128)(2,1)} %constant_dynamic-update-slice_fusion), channel_id=1, source_target_pairs={{0,48},{16,0},{32,16},{48,32},{64,112},{80,64},{96,80},{112,96},{1... | collective-permute-start | bytes 4718600 | tf_op jit(solution)/shard_map/ppermute | solution.py:63
  44.6 22.3 %collective-permute-start.6 = (bf16[128,3072]{1,0:T(8,128)(2,1)}, bf16[128,3072]{1,0:T(8,128)(2,1)}, u32[]{:S(2)}, u32[]{:S(2)}) collective-permute-start(bf16[128,3072]{1,0:T(8,128)(2,1)} %pad_maximum_fusion.3), channel_id=1, source_target_pairs={{0,64},{16,80},{32,96},{48,112},{64,0},{80,16},{96,32},{112,48},{1... | collective-permute-start | bytes 2359304 | tf_op jit(solution)/shard_map/ppermute | solution.py:63
  47.6 32.9 %collective-permute-start.9 = (bf16[128,3072]{1,0:T(8,128)(2,1)S(1)}, bf16[128,3072]{1,0:T(8,128)(2,1)}, u32[]{:S(2)}, u32[]{:S(2)}) collective-permute-start(bf16[128,3072]{1,0:T(8,128)(2,1)S(1)} %pad_maximum_fusion.2.refs_0_), channel_id=1, source_target_pairs={{0,64},{16,80},{32,96},{48,112},{64,0},{80,16},{96,32},{112,48},{1... | collective-permute-start | bytes 2359304 | tf_op jit(solution)/shard_map/ppermute | solution.py:63
  48.2 1.1 copy-start.1
  49.3 1.1 copy-start.7
  50.5 1.1 copy-start.9
  51.6 85.8 %copy-start.10 = (s32[3]{0:T(128)}, s32[3]{0:T(128)S(1)}, u32[]{:S(2)}) copy-start(s32[3]{0:T(128)S(1)} %pad_add_fusion.place) | copy-start | bytes 40
  61.8 24.1 %copy-start.3 = (bf16[64,3072]{1,0:T(8,128)(2,1)S(1)}, bf16[64,3072]{1,0:T(8,128)(2,1)}, u32[]{:S(2)}) copy-start(bf16[64,3072]{1,0:T(8,128)(2,1)} %copy-done.2) | copy-start | bytes 1179652
  81.5 14.3 %collective-permute-start.11 = (bf16[64,3072]{1,0:T(8,128)(2,1)S(1)}, bf16[64,3072]{1,0:T(8,128)(2,1)S(1)}, u32[]{:S(2)}, u32[]{:S(2)}) collective-permute-start(bf16[64,3072]{1,0:T(8,128)(2,1)S(1)} %slice.30), channel_id=1, source_target_pairs={{0,16},{16,32},{32,48},{48,0},{64,80},{80,96},{96,112},{112,64},{1... | collective-permute-start | bytes 1179656 | tf_op jit(solution)/shard_map/ppermute | solution.py:63
  82.7 13.2 %collective-permute-start.12 = (bf16[64,3072]{1,0:T(8,128)(2,1)S(1)}, bf16[64,3072]{1,0:T(8,128)(2,1)S(1)}, u32[]{:S(2)}, u32[]{:S(2)}) collective-permute-start(bf16[64,3072]{1,0:T(8,128)(2,1)S(1)} %slice.31), channel_id=1, source_target_pairs={{0,48},{16,0},{32,16},{48,32},{64,112},{80,64},{96,80},{112,96},{1... | collective-permute-start | bytes 1179656 | tf_op jit(solution)/shard_map/ppermute | solution.py:63
  85.9 14.7 %collective-permute-start.10 = (f32[4,64,1536]{2,1,0:T(8,128)}, f32[4,64,1536]{2,1,0:T(8,128)S(1)}, u32[]{:S(2)}, u32[]{:S(2)}) collective-permute-start(f32[4,64,1536]{2,1,0:T(8,128)} %bitcast.18), channel_id=1, source_target_pairs={{0,1},{1,0},{2,3},{3,2},{4,5},{5,4},{6,7},{7,6},{8,9},{9,8},{10,11... | collective-permute-start | bytes 4718600 | tf_op jit(solution)/shard_map/ppermute | solution.py:259
  95.9 7.8 %copy-start.4 = (bf16[64,3072]{1,0:T(8,128)(2,1)}, bf16[64,3072]{1,0:T(8,128)(2,1)S(1)}, u32[]{:S(2)}) copy-start(bf16[64,3072]{1,0:T(8,128)(2,1)S(1)} %collective-permute-done.12.refs_1_) | copy-start | bytes 1179652
  95.9 7.8 %collective-permute-start.13 = (f32[4,64,1536]{2,1,0:T(8,128)S(1)}, f32[4,64,1536]{2,1,0:T(8,128)S(1)}, u32[]{:S(2)}, u32[]{:S(2)}) collective-permute-start(f32[4,64,1536]{2,1,0:T(8,128)S(1)} %bitcast.16), channel_id=1, source_target_pairs={{0,1},{1,0},{2,3},{3,2},{4,5},{5,4},{6,7},{7,6},{8,9},{9,8},{10,11... | collective-permute-start | bytes 4718600 | tf_op jit(solution)/shard_map/ppermute | solution.py:259
  96.5 24.5 %collective-permute-start.15 = (bf16[128,3072]{1,0:T(8,128)(2,1)}, bf16[128,3072]{1,0:T(8,128)(2,1)}, u32[]{:S(2)}, u32[]{:S(2)}) collective-permute-start(bf16[128,3072]{1,0:T(8,128)(2,1)} %collective-permute-done.9.refs_3_), channel_id=1, source_target_pairs={{0,16},{16,32},{32,48},{48,0},{64,80},{80,96},{96,112},{112,64},{1... | collective-permute-start | bytes 2359304 | tf_op jit(solution)/shard_map/ppermute | solution.py:63
  96.5 24.5 %collective-permute-start.16 = (bf16[128,3072]{1,0:T(8,128)(2,1)}, bf16[128,3072]{1,0:T(8,128)(2,1)}, u32[]{:S(2)}, u32[]{:S(2)}) collective-permute-start(bf16[128,3072]{1,0:T(8,128)(2,1)} %collective-permute-done.9.refs_3_), channel_id=1, source_target_pairs={{0,48},{16,0},{32,16},{48,32},{64,112},{80,64},{96,80},{112,96},{1... | collective-permute-start | bytes 2359304 | tf_op jit(solution)/shard_map/ppermute | solution.py:63
  99.7 40.0 %collective-permute-start.19 = (bf16[1024,1536]{1,0:T(8,128)(2,1)}, bf16[1024,1536]{1,0:T(8,128)(2,1)}, u32[]{:S(2)}, u32[]{:S(2)}) collective-permute-start(bf16[1024,1536]{1,0:T(8,128)(2,1)} %bitcast.5.refs_4_), channel_id=1, source_target_pairs={{0,1},{1,0},{2,3},{3,2},{4,5},{5,4},{6,7},{7,6},{8,9},{9,8},{10,11... | collective-permute-start | bytes 9437192 | tf_op jit(solution)/shard_map/ppermute | solution.py:370
  100.7 22.2 %collective-permute-start.17 = (bf16[128,3072]{1,0:T(8,128)(2,1)}, bf16[128,3072]{1,0:T(8,128)(2,1)}, u32[]{:S(2)}, u32[]{:S(2)}) collective-permute-start(bf16[128,3072]{1,0:T(8,128)(2,1)} %pad_maximum_fusion.4), channel_id=1, source_target_pairs={{0,64},{16,80},{32,96},{48,112},{64,0},{80,16},{96,32},{112,48},{1... | collective-permute-start | bytes 2359304 | tf_op jit(solution)/shard_map/ppermute | solution.py:63
  106.0 52.7 %all-to-all-start.1 = ((f32[8,64,1536]{2,1,0:T(8,128)}), f32[8,64,1536]{2,1,0:T(8,128)}, u32[]{:S(2)}, u32[]{:S(2)}) async-start(f32[8,64,1536]{2,1,0:T(8,128)} %chips.2), calls=%async_computation.1 | async-start | bytes 6291456 | tf_op jit(solution)/shard_map/all_to_all | solution.py:282
  110.7 12.1 %copy-start.5 = (bf16[64,3072]{1,0:T(8,128)(2,1)S(1)}, bf16[64,3072]{1,0:T(8,128)(2,1)}, u32[]{:S(2)}) copy-start(bf16[64,3072]{1,0:T(8,128)(2,1)} %copy-done.4) | copy-start | bytes 1179652
  120.7 13.1 %collective-permute-start.14 = (f32[4,64,1536]{2,1,0:T(8,128)S(1)}, f32[4,64,1536]{2,1,0:T(8,128)S(1)}, u32[]{:S(2)}, u32[]{:S(2)}) collective-permute-start(f32[4,64,1536]{2,1,0:T(8,128)S(1)} %bitcast.17), channel_id=1, source_target_pairs={{0,1},{1,0},{2,3},{3,2},{4,5},{5,4},{6,7},{7,6},{8,9},{9,8},{10,11... | collective-permute-start | bytes 4718600 | tf_op jit(solution)/shard_map/ppermute | solution.py:259
  133.6 3.7 %collective-permute-start.18 = (f32[4,64,1536]{2,1,0:T(8,128)}, f32[4,64,1536]{2,1,0:T(8,128)S(1)}, u32[]{:S(2)}, u32[]{:S(2)}) collective-permute-start(f32[4,64,1536]{2,1,0:T(8,128)} %bitcast.19), channel_id=1, source_target_pairs={{0,1},{1,0},{2,3},{3,2},{4,5},{5,4},{6,7},{7,6},{8,9},{9,8},{10,11... | collective-permute-start | bytes 4718600 | tf_op jit(solution)/shard_map/ppermute | solution.py:259
  158.7 42.0 %all-to-all-start.2 = ((f32[8,64,1536]{2,1,0:T(8,128)}), f32[8,64,1536]{2,1,0:T(8,128)S(1)}, u32[]{:S(2)}, u32[]{:S(2)}) async-start(f32[8,64,1536]{2,1,0:T(8,128)} %chips.3), calls=%async_computation.2 | async-start | bytes 6291456 | tf_op jit(solution)/shard_map/all_to_all | solution.py:282

commit v3 on v2

--- a/solution.py
+++ b/solution.py
@@ -56,6 +56,8 @@
         (0, 2): [(("far_up", j), 0), (("far_down", j), 0)],
         (1, 2): [(("across_far", j), half * size) for half in range(2)],
     }
+    if j == len(sizes) - 1:
+        places[1, 2] = [(("last_up", j), 0), (("last_down", j), 0)]
     return [places[offset] for offset in offsets]
 
 
@@ -344,9 +346,12 @@
             far[k - 2] = made[0]
             made = [chip_sums(place, near[k - 2], far[k - 2])]
         arrays["far_up", k - 1], arrays["far_down", k - 1] = ready
-        arrays["across_far", k - 1] = send(jnp.concatenate(ready), CROSS)
         if k < count:
+            arrays["across_far", k - 1] = send(jnp.concatenate(ready), CROSS)
             started.append(("across_far", k - 1))
+        else:
+            arrays["last_up", k - 1] = send(arrays["up", k][:size], UP)
+            arrays["last_down", k - 1] = send(arrays["down", k][size:], DOWN)
         if k == 1:
             near[0] = multiply((0, NEAR))[0]
         if k < count:

time: 202 us -> 197 us (0.975)
  waiting for transfers between devices: 67.8 us -> 57 us
  starting transfers between devices: 42.1 us -> 45.3 us
  local copies, waits for them, and re-layouts: 11.7 us -> 14.3 us
    all_to_all x2, waiting for transfers between devices: 26.8 us -> 8.28 us  [sum_direct(): lax.all_to_all(chip, 'col', 0, 0, axis_index_groups=CHIP_GROUPS, tiled=True)]
    ppermute x14 -> x15, waiting for transfers between devices: 29.6 us -> 37.7 us  [send(): return lax.ppermute(value, 'row', move)]
    all_to_all x2, starting transfers between devices: 8.32 us -> 10.8 us  [sum_direct(): lax.all_to_all(chip, 'col', 0, 0, axis_index_groups=CHIP_GROUPS, tiled=True)]
    unnamed x25 -> x29, local copies, waits for them, and re-layouts: 4.45 us -> 5.93 us
    ppermute x14 -> x15, starting transfers between devices: 26.7 us -> 27.2 us  [send(): return lax.ppermute(value, 'row', move)]
  transfers between devices with their start and end apart: 23 -> 24, of which waited for: 10 -> 9; matrix products, arithmetic and copies ran while one was open for 5% -> 5% of each run, Pallas kernels for 37% -> 38%
where the time goes in v3:
time: 197 us; the launch traced here: 196 us
  Pallas kernels  73.6 us (37%)
  waiting for transfers between devices  57 us (29%)
  starting transfers between devices  45.3 us (23%)
  local copies, waits for them, and re-layouts  14.3 us (7%)
  other arithmetic  4.38 us (2%)
    pallas_call x4, Pallas kernels, contract_units(): pl.pallas_call(functools.partial(units_kernel, parts), grid=(features //...  40.6 us
    ppermute x15, waiting for transfers between devices, send(): return lax.ppermute(value, 'row', move)  37.7 us
    pallas_call x1, Pallas kernels, contract_tokens(): pl.pallas_call(functools.partial(tokens_kernel, groups), grid=(units // t...  28.3 us
    ppermute x15, starting transfers between devices, send(): return lax.ppermute(value, 'row', move)  27.2 us
    all_to_all x2, starting transfers between devices, sum_direct(): lax.all_to_all(chip, 'col', 0, 0, axis_index_groups=CHIP_GROUPS, tiled=True)  10.8 us
    all_to_all x2, waiting for transfers between devices, sum_direct(): lax.all_to_all(chip, 'col', 0, 0, axis_index_groups=CHIP_GROUPS, tiled=True)  8.28 us
    ppermute x1, waiting for transfers between devices, local(): beside = lax.ppermute(inputs, 'col', BESIDE)  7.76 us
    unnamed x29, local copies, waits for them, and re-layouts  5.93 us
  transfers between devices with their start and end apart: 24, of which 9 were waited for; matrix products, arithmetic and copies ran while one was open for 5% of the time, Pallas kernels for 38%

profile of v3, /device:TPU:0, one launch (start us, length us, event | category | flops | bytes accessed | tf_op | source)
XLA Modules:
  0.0 195.6 jit_solution(18406661896642585076)
XLA Ops:
  0.6 1.5 fusion
  2.2 2.1 %collective-permute-start = (bf16[128,3072]{1,0:T(8,128)(2,1)S(1)}, bf16[128,3072]{1,0:T(8,128)(2,1)S(1)}, u32[]{:S(2)}, u32[]{:S(2)}) collective-permute-start(bf16[128,3072]{1,0:T(8,128)(2,1)S(1)} %pad_maximum_fusion.refs_0_), channel_id=1, source_target_pairs={{0,16},{16,32},{32,48},{48,0},{64,80},{80,96},{96,112},{112,64},{1... | collective-permute-start | bytes 2359304 | tf_op jit(solution)/shard_map/ppermute | solution.py:65
  4.2 2.2 %collective-permute-start.1 = (bf16[128,3072]{1,0:T(8,128)(2,1)S(1)}, bf16[128,3072]{1,0:T(8,128)(2,1)S(1)}, u32[]{:S(2)}, u32[]{:S(2)}) collective-permute-start(bf16[128,3072]{1,0:T(8,128)(2,1)S(1)} %pad_maximum_fusion.refs_0_), channel_id=1, source_target_pairs={{0,48},{16,0},{32,16},{48,32},{64,112},{80,64},{96,80},{112,96},{1... | collective-permute-start | bytes 2359304 | tf_op jit(solution)/shard_map/ppermute | solution.py:65
  6.4 1.5 collective-permute-start.2
  7.9 2.7 %collective-permute-start.5 = (bf16[128,3072]{1,0:T(8,128)(2,1)S(1)}, bf16[128,3072]{1,0:T(8,128)(2,1)S(1)}, u32[]{:S(2)}, u32[]{:S(2)}) collective-permute-start(bf16[128,3072]{1,0:T(8,128)(2,1)S(1)} %pad_maximum_fusion.refs_0_), channel_id=1, source_target_pairs={{0,64},{16,80},{32,96},{48,112},{64,0},{80,16},{96,32},{112,48},{1... | collective-permute-start | bytes 2359304 | tf_op jit(solution)/shard_map/ppermute | solution.py:65
  10.7 7.8 %collective-permute-done.2 = bf16[128,1536]{1,0:T(8,128)(2,1)S(1)} collective-permute-done((bf16[128,1536]{1,0:T(8,128)(2,1)S(1)}, bf16[128,1536]{1,0:T(8,128)(2,1)S(1)}, u32[]{:S(2)}, u32[]{:S(2)}) %collective-permute-start.2) | collective-permute-done | bytes 393248 | tf_op jit(solution)/shard_map/ppermute | solution.py:307
  18.5 5.4 %collective-permute-done.refs_1_ = bf16[128,3072]{1,0:T(8,128)(2,1)S(1)} collective-permute-done((bf16[128,3072]{1,0:T(8,128)(2,1)S(1)}, bf16[128,3072]{1,0:T(8,128)(2,1)S(1)}, u32[]{:S(2)}, u32[]{:S(2)}) %collective-permute-start) | collective-permute-done | bytes 786464 | tf_op jit(solution)/shard_map/ppermute | solution.py:65
  23.9 2.1 %broadcast_in_dim.3 = bf16[4,256,1536]{2,1,0:T(8,128)(2,1)} broadcast(bf16[256,1536]{1,0:T(8,128)(2,1)S(1)} %pad_maximum_fusion.1), dimensions={1,2} | broadcast | bytes 3932160 | tf_op jit(solution)/shard_map/broadcast_in_dim | solution.py:323
  26.0 0.8 slice.34
  26.7 1.1 collective-permute-start.3
  27.9 2.2 %collective-permute-start.4 = (bf16[64,3072]{1,0:T(8,128)(2,1)S(1)}, bf16[64,3072]{1,0:T(8,128)(2,1)S(1)}, u32[]{:S(2)}, u32[]{:S(2)}) collective-permute-start(bf16[64,3072]{1,0:T(8,128)(2,1)S(1)} %slice.35), channel_id=1, source_target_pairs={{0,48},{16,0},{32,16},{48,32},{64,112},{80,64},{96,80},{112,96},{1... | collective-permute-start | bytes 1179656 | tf_op jit(solution)/shard_map/ppermute | solution.py:65
  30.1 4.7 %all-to-all-start = ((bf16[4,256,1536]{2,1,0:T(8,128)(2,1)}), bf16[4,256,1536]{2,1,0:T(8,128)(2,1)}, u32[]{:S(2)}, u32[]{:S(2)}) async-start(bf16[4,256,1536]{2,1,0:T(8,128)(2,1)} %broadcast_in_dim.3), calls=%async_computation | async-start | bytes 6291456 | tf_op jit(solution)/shard_map/all_to_all | solution.py:327
  34.7 1.3 collective-permute-done.5.refs_3_
  36.1 2.4 %collective-permute-done.3.refs_0_ = bf16[64,3072]{1,0:T(8,128)(2,1)S(1)} collective-permute-done((bf16[64,3072]{1,0:T(8,128)(2,1)}, bf16[64,3072]{1,0:T(8,128)(2,1)S(1)}, u32[]{:S(2)}, u32[]{:S(2)}) %collective-permute-start.3) | collective-permute-done | bytes 393248 | tf_op jit(solution)/shard_map/ppermute | solution.py:65
  38.5 1.0 constant_dynamic-update-slice_fusion.1
  39.4 1.0 constant_dynamic-update-slice_fusion
  40.4 0.7 collective-permute-start.7
  41.1 2.6 %collective-permute-start.8 = (bf16[256,3072]{1,0:T(8,128)(2,1)}, bf16[256,3072]{1,0:T(8,128)(2,1)}, u32[]{:S(2)}, u32[]{:S(2)}) collective-permute-start(bf16[256,3072]{1,0:T(8,128)(2,1)} %constant_dynamic-update-slice_fusion), channel_id=1, source_target_pairs={{0,48},{16,0},{32,16},{48,32},{64,112},{80,64},{96,80},{112,96},{1... | collective-permute-start | bytes 4718600 | tf_op jit(solution)/shard_map/ppermute | solution.py:65
  43.7 1.0 pad_maximum_fusion.3
  44.7 3.0 %collective-permute-start.6 = (bf16[128,3072]{1,0:T(8,128)(2,1)}, bf16[128,3072]{1,0:T(8,128)(2,1)}, u32[]{:S(2)}, u32[]{:S(2)}) collective-permute-start(bf16[128,3072]{1,0:T(8,128)(2,1)} %pad_maximum_fusion.3), channel_id=1, source_target_pairs={{0,64},{16,80},{32,96},{48,112},{64,0},{80,16},{96,32},{112,48},{1... | collective-permute-start | bytes 2359304 | tf_op jit(solution)/shard_map/ppermute | solution.py:65
  48.3 1.1 copy-done.1
  49.4 1.1 copy-done.5
  50.6 1.1 copy-done.7
  51.7 10.1 %units.4 = (f32[256,1536]{1,0:T(8,128)S(1)}, f32[256,1536]{1,0:T(8,128)}, bf16[512,3072]{1,0:T(8,128)(2,1)}) custom-call(s32[3]{0:T(128)S(1)} %pad_add_fusion.place, bf16[128,3072]{1,0:T(8,128)(2,1)S(1)} %pad_maximum_fusion.refs_0_, bf16[128,3072]{1,0:T(8,128)(2,1)S(1)} %copy-done.5, bf16[128,3072]{1,0:T(8,128)(2,1)S(1)} %copy-done.7, ...), custom_call_target="tpu_custom_call" | custom-call | flops 4831838208 | bytes 18874368 | tf_op jit(solution)/shard_map/units/pallas_call | solution.py:135
  61.8 5.1 %collective-permute-done.6.refs_4_ = bf16[128,3072]{1,0:T(8,128)(2,1)} collective-permute-done((bf16[128,3072]{1,0:T(8,128)(2,1)}, bf16[128,3072]{1,0:T(8,128)(2,1)}, u32[]{:S(2)}, u32[]{:S(2)}) %collective-permute-start.6) | collective-permute-done | bytes 786464 | tf_op jit(solution)/shard_map/ppermute | solution.py:65
  67.0 13.6 %collective-permute-done.9.refs_3_ = bf16[128,3072]{1,0:T(8,128)(2,1)} collective-permute-done((bf16[128,3072]{1,0:T(8,128)(2,1)S(1)}, bf16[128,3072]{1,0:T(8,128)(2,1)}, u32[]{:S(2)}, u32[]{:S(2)}) %collective-permute-start.9) | collective-permute-done | bytes 786464 | tf_op jit(solution)/shard_map/ppermute | solution.py:65
  80.6 1.0 slice.36
  81.7 1.0 slice.37
  82.8 3.3 %collective-permute-start.12 = (bf16[64,3072]{1,0:T(8,128)(2,1)S(1)}, bf16[64,3072]{1,0:T(8,128)(2,1)S(1)}, u32[]{:S(2)}, u32[]{:S(2)}) collective-permute-start(bf16[64,3072]{1,0:T(8,128)(2,1)S(1)} %slice.37), channel_id=1, source_target_pairs={{0,48},{16,0},{32,16},{48,32},{64,112},{80,64},{96,80},{112,96},{1... | collective-permute-start | bytes 1179656 | tf_op jit(solution)/shard_map/ppermute | solution.py:65
  86.0 9.9 %units.5 = (f32[256,1536]{1,0:T(8,128)S(1)}, f32[256,1536]{1,0:T(8,128)S(1)}, bf16[512,3072]{1,0:T(8,128)(2,1)}) custom-call(s32[3]{0:T(128)S(1)} %pad_add_fusion.place, bf16[64,3072]{1,0:T(8,128)(2,1)S(1)} %collective-permute-done.3.refs_0_, bf16[64,3072]{1,0:T(8,128)(2,1)S(1)} %copy-done.3, bf16[256,3072]{1,0:T(8,128)(2,1)} %collective-permute-done.7.refs_2_.refs_1_, ...), custom_call_target="tpu_custom_call" | custom-call | flops 4831838208 | bytes 18874368 | tf_op jit(solution)/shard_map/units/pallas_call | solution.py:135
  96.0 0.7 copy-done.9
  96.7 0.8 copy-done.11
  98.0 3.2 %collective-permute-start.16 = (bf16[128,3072]{1,0:T(8,128)(2,1)}, bf16[128,3072]{1,0:T(8,128)(2,1)}, u32[]{:S(2)}, u32[]{:S(2)}) collective-permute-start(bf16[128,3072]{1,0:T(8,128)(2,1)} %collective-permute-done.9.refs_3_), channel_id=1, source_target_pairs={{0,48},{16,0},{32,16},{48,32},{64,112},{80,64},{96,80},{112,96},{1... | collective-permute-start | bytes 2359304 | tf_op jit(solution)/shard_map/ppermute | solution.py:65
  101.2 2.3 %chips.2 = f32[8,64,1536]{2,1,0:T(8,128)} custom-call(s32[3]{0:T(128)S(1)} %pad_add_fusion.place, f32[4,64,1536]{2,1,0:T(8,128)S(1)} %bitcast.12, f32[4,64,1536]{2,1,0:T(8,128)S(1)} %collective-permute-done.10.near_got, f32[4,64,1536]{2,1,0:T(8,128)S(1)} %bitcast.14, f32[4,64,1536]{2,1,0:T(8,128)S(1)} %collective-permute-done.13.far_got), custom_call_target="tpu_custom_call" | custom-call | flops 786432 | bytes 9437184 | tf_op jit(solution)/shard_map/chips/pallas_call | solution.py:263
  103.6 5.4 %all-to-all-start.1 = ((f32[8,64,1536]{2,1,0:T(8,128)}), f32[8,64,1536]{2,1,0:T(8,128)}, u32[]{:S(2)}, u32[]{:S(2)}) async-start(f32[8,64,1536]{2,1,0:T(8,128)} %chips.2), calls=%async_computation.1 | async-start | bytes 6291456 | tf_op jit(solution)/shard_map/all_to_all | solution.py:284
  109.0 9.9 %collective-permute-done.15.refs_2_ = bf16[128,3072]{1,0:T(8,128)(2,1)S(1)} collective-permute-done((bf16[128,3072]{1,0:T(8,128)(2,1)}, bf16[128,3072]{1,0:T(8,128)(2,1)S(1)}, u32[]{:S(2)}, u32[]{:S(2)}) %collective-permute-start.15) | collective-permute-done | bytes 786464 | tf_op jit(solution)/shard_map/ppermute | solution.py:65
  119.0 1.0 slice.41
  120.0 3.5 %collective-permute-start.18 = (bf16[64,3072]{1,0:T(8,128)(2,1)S(1)}, bf16[64,3072]{1,0:T(8,128)(2,1)S(1)}, u32[]{:S(2)}, u32[]{:S(2)}) collective-permute-start(bf16[64,3072]{1,0:T(8,128)(2,1)S(1)} %slice.41), channel_id=1, source_target_pairs={{0,48},{16,0},{32,16},{48,32},{64,112},{80,64},{96,80},{112,96},{1... | collective-permute-start | bytes 1179656 | tf_op jit(solution)/shard_map/ppermute | solution.py:65
  123.5 9.9 %units.6 = (f32[256,1536]{1,0:T(8,128)S(1)}, f32[256,1536]{1,0:T(8,128)S(1)}, bf16[512,3072]{1,0:T(8,128)(2,1)}) custom-call(s32[3]{0:T(128)S(1)} %pad_add_fusion.place, bf16[128,3072]{1,0:T(8,128)(2,1)S(1)} %pad_maximum_fusion.2.refs_0_, bf16[256,3072]{1,0:T(8,128)(2,1)} %collective-permute-done.7.refs_2_.refs_1_, ...), custom_call_target="tpu_custom_call" | custom-call | flops 4831838208 | bytes 18874368 | tf_op jit(solution)/shard_map/units/pallas_call | solution.py:135
  133.5 10.7 %units.7 = (f32[256,1536]{1,0:T(8,128)S(1)}, f32[256,1536]{1,0:T(8,128)}, bf16[512,3072]{1,0:T(8,128)(2,1)}) custom-call(s32[3]{0:T(128)S(1)} %pad_add_fusion.place, bf16[64,3072]{1,0:T(8,128)(2,1)S(1)} %copy-done.10, bf16[64,3072]{1,0:T(8,128)(2,1)S(1)} %copy-done.12, bf16[128,3072]{1,0:T(8,128)(2,1)S(1)} %collective-permute-done.15.refs_2_, ...), custom_call_target="tpu_custom_call" | custom-call | flops 4831838208 | bytes 18874368 | tf_op jit(solution)/shard_map/units/pallas_call | solution.py:135
  144.2 0.6 collective-permute-start.19
  144.8 3.2 %collective-permute-done.19.far_got = f32[4,64,1536]{2,1,0:T(8,128)S(1)} collective-permute-done((f32[4,64,1536]{2,1,0:T(8,128)}, f32[4,64,1536]{2,1,0:T(8,128)S(1)}, u32[]{:S(2)}, u32[]{:S(2)}) %collective-permute-start.19) | collective-permute-done | bytes 1572896 | tf_op jit(solution)/shard_map/ppermute | solution.py:261
  148.1 2.4 %chips.3 = f32[8,64,1536]{2,1,0:T(8,128)} custom-call(s32[3]{0:T(128)S(1)} %pad_add_fusion.place, f32[4,64,1536]{2,1,0:T(8,128)S(1)} %bitcast.13, f32[4,64,1536]{2,1,0:T(8,128)S(1)} %collective-permute-done.14.near_got, f32[4,64,1536]{2,1,0:T(8,128)S(1)} %bitcast.15, f32[4,64,1536]{2,1,0:T(8,128)S(1)} %collective-permute-done.19.far_got), custom_call_target="tpu_custom_call" | custom-call | flops 786432 | bytes 9437184 | tf_op jit(solution)/shard_map/chips/pallas_call | solution.py:263
  150.4 5.4 %all-to-all-start.2 = ((f32[8,64,1536]{2,1,0:T(8,128)}), f32[8,64,1536]{2,1,0:T(8,128)S(1)}, u32[]{:S(2)}, u32[]{:S(2)}) async-start(f32[8,64,1536]{2,1,0:T(8,128)} %chips.3), calls=%async_computation.2 | async-start | bytes 6291456 | tf_op jit(solution)/shard_map/all_to_all | solution.py:284
  155.9 28.3 %tokens.1 = bf16[1536,3072]{1,0:T(8,128)(2,1)} custom-call(s32[3]{0:T(128)} %copy-done.8, bf16[512,3072]{1,0:T(8,128)(2,1)} %get-tuple-element.70.refs_0_, bf16[512,3072]{1,0:T(8,128)(2,1)} %get-tuple-element.71.refs_1_, bf16[512,3072]{1,0:T(8,128)(2,1)} %get-tuple-element.72.refs_2_, bf16[512,3072]{1,0:T(8,128)(2,1)} %get-tuple-element.73.refs_3_, ...), custom_call_target="tpu_custom_call" | custom-call | flops 19327352832 | bytes 28311552 | tf_op jit(solution)/shard_map/tokens/pallas_call | solution.py:222
  184.2 2.1 %reduce_sum.18 = bf16[64,1536]{1,0:T(8,128)(2,1)S(1)} reduce(f32[8,64,1536]{2,1,0:T(8,128)} %all-to-all-done.1, f32[]{:T(128)} %constant.38.clone.1), dimensions={0}, to_apply=%region_0.1 | reduce | flops 688128 | bytes 3342340 | tf_op jit(solution)/shard_map/reduce_sum | solution.py:285
  186.3 8.3 %all-to-all-done.2 = f32[8,64,1536]{2,1,0:T(8,128)S(1)} async-done(((f32[8,64,1536]{2,1,0:T(8,128)}), f32[8,64,1536]{2,1,0:T(8,128)S(1)}, u32[]{:S(2)}, u32[]{:S(2)}) %all-to-all-start.2) | async-done | bytes 3145760 | tf_op jit(solution)/shard_map/all_to_all | solution.py:284
  194.8 0.8 pad_maximum_fusion.4
  (53 shorter events, 1.9 us)
Async XLA Ops:
  2.1 4.3 %copy-start.13 = (bf16[128,1536]{1,0:T(8,128)(2,1)S(1)}, bf16[128,1536]{1,0:T(8,128)(2,1)}, u32[]{:S(2)}) copy-start(bf16[128,1536]{1,0:T(8,128)(2,1)} %param.3) | copy-start | bytes 1179652
  2.2 21.7 %collective-permute-start = (bf16[128,3072]{1,0:T(8,128)(2,1)S(1)}, bf16[128,3072]{1,0:T(8,128)(2,1)S(1)}, u32[]{:S(2)}, u32[]{:S(2)}) collective-permute-start(bf16[128,3072]{1,0:T(8,128)(2,1)S(1)} %pad_maximum_fusion.refs_0_), channel_id=1, source_target_pairs={{0,16},{16,32},{32,48},{48,0},{64,80},{80,96},{96,112},{112,64},{1... | collective-permute-start | bytes 2359304 | tf_op jit(solution)/shard_map/ppermute | solution.py:65
  4.2 19.7 %collective-permute-start.1 = (bf16[128,3072]{1,0:T(8,128)(2,1)S(1)}, bf16[128,3072]{1,0:T(8,128)(2,1)S(1)}, u32[]{:S(2)}, u32[]{:S(2)}) collective-permute-start(bf16[128,3072]{1,0:T(8,128)(2,1)S(1)} %pad_maximum_fusion.refs_0_), channel_id=1, source_target_pairs={{0,48},{16,0},{32,16},{48,32},{64,112},{80,64},{96,80},{112,96},{1... | collective-permute-start | bytes 2359304 | tf_op jit(solution)/shard_map/ppermute | solution.py:65
  6.4 12.0 %collective-permute-start.2 = (bf16[128,1536]{1,0:T(8,128)(2,1)S(1)}, bf16[128,1536]{1,0:T(8,128)(2,1)S(1)}, u32[]{:S(2)}, u32[]{:S(2)}) collective-permute-start(bf16[128,1536]{1,0:T(8,128)(2,1)S(1)} %copy-done.13), channel_id=1, source_target_pairs={{0,2},{1,3},{2,0},{3,1},{4,6},{5,7},{6,4},{7,5},{8,10},{9,11},{10,... | collective-permute-start | bytes 1179656 | tf_op jit(solution)/shard_map/ppermute | solution.py:307
  7.9 28.1 %collective-permute-start.5 = (bf16[128,3072]{1,0:T(8,128)(2,1)S(1)}, bf16[128,3072]{1,0:T(8,128)(2,1)S(1)}, u32[]{:S(2)}, u32[]{:S(2)}) collective-permute-start(bf16[128,3072]{1,0:T(8,128)(2,1)S(1)} %pad_maximum_fusion.refs_0_), channel_id=1, source_target_pairs={{0,64},{16,80},{32,96},{48,112},{64,0},{80,16},{96,32},{112,48},{1... | collective-permute-start | bytes 2359304 | tf_op jit(solution)/shard_map/ppermute | solution.py:65
  23.9 2.1 %copy-start.4 = (bf16[128,3072]{1,0:T(8,128)(2,1)}, bf16[128,3072]{1,0:T(8,128)(2,1)S(1)}, u32[]{:S(2)}) copy-start(bf16[128,3072]{1,0:T(8,128)(2,1)S(1)} %collective-permute-done.refs_1_) | copy-start | bytes 2359300
  23.9 4.0 %copy-start.6 = (bf16[128,3072]{1,0:T(8,128)(2,1)}, bf16[128,3072]{1,0:T(8,128)(2,1)S(1)}, u32[]{:S(2)}) copy-start(bf16[128,3072]{1,0:T(8,128)(2,1)S(1)} %collective-permute-done.1.refs_2_) | copy-start | bytes 2359300
  26.7 11.7 %collective-permute-start.3 = (bf16[64,3072]{1,0:T(8,128)(2,1)}, bf16[64,3072]{1,0:T(8,128)(2,1)S(1)}, u32[]{:S(2)}, u32[]{:S(2)}) collective-permute-start(bf16[64,3072]{1,0:T(8,128)(2,1)} %slice.34), channel_id=1, source_target_pairs={{0,16},{16,32},{32,48},{48,0},{64,80},{80,96},{96,112},{112,64},{1... | collective-permute-start | bytes 1179656 | tf_op jit(solution)/shard_map/ppermute | solution.py:65
  27.9 10.6 %collective-permute-start.4 = (bf16[64,3072]{1,0:T(8,128)(2,1)S(1)}, bf16[64,3072]{1,0:T(8,128)(2,1)S(1)}, u32[]{:S(2)}, u32[]{:S(2)}) collective-permute-start(bf16[64,3072]{1,0:T(8,128)(2,1)S(1)} %slice.35), channel_id=1, source_target_pairs={{0,48},{16,0},{32,16},{48,32},{64,112},{80,64},{96,80},{112,96},{1... | collective-permute-start | bytes 1179656 | tf_op jit(solution)/shard_map/ppermute | solution.py:65
  30.1 50.5 %all-to-all-start = ((bf16[4,256,1536]{2,1,0:T(8,128)(2,1)}), bf16[4,256,1536]{2,1,0:T(8,128)(2,1)}, u32[]{:S(2)}, u32[]{:S(2)}) async-start(bf16[4,256,1536]{2,1,0:T(8,128)(2,1)} %broadcast_in_dim.3), calls=%async_computation | async-start | bytes 6291456 | tf_op jit(solution)/shard_map/all_to_all | solution.py:327
  36.1 4.4 %copy-start = (bf16[128,3072]{1,0:T(8,128)(2,1)}, bf16[128,3072]{1,0:T(8,128)(2,1)S(1)}, u32[]{:S(2)}) copy-start(bf16[128,3072]{1,0:T(8,128)(2,1)S(1)} %collective-permute-done.5.refs_3_) | copy-start | bytes 2359300
  38.5 5.2 %copy-start.2 = (bf16[64,3072]{1,0:T(8,128)(2,1)}, bf16[64,3072]{1,0:T(8,128)(2,1)S(1)}, u32[]{:S(2)}) copy-start(bf16[64,3072]{1,0:T(8,128)(2,1)S(1)} %collective-permute-done.4.refs_1_) | copy-start | bytes 1179652
  40.4 40.2 %collective-permute-start.7 = (bf16[256,3072]{1,0:T(8,128)(2,1)}, bf16[256,3072]{1,0:T(8,128)(2,1)}, u32[]{:S(2)}, u32[]{:S(2)}) collective-permute-start(bf16[256,3072]{1,0:T(8,128)(2,1)} %constant_dynamic-update-slice_fusion), channel_id=1, source_target_pairs={{0,16},{16,32},{32,48},{48,0},{64,80},{80,96},{96,112},{112,64},{1... | collective-permute-start | bytes 4718600 | tf_op jit(solution)/shard_map/ppermute | solution.py:65
  41.1 39.5 %collective-permute-start.8 = (bf16[256,3072]{1,0:T(8,128)(2,1)}, bf16[256,3072]{1,0:T(8,128)(2,1)}, u32[]{:S(2)}, u32[]{:S(2)}) collective-permute-start(bf16[256,3072]{1,0:T(8,128)(2,1)} %constant_dynamic-update-slice_fusion), channel_id=1, source_target_pairs={{0,48},{16,0},{32,16},{48,32},{64,112},{80,64},{96,80},{112,96},{1... | collective-permute-start | bytes 4718600 | tf_op jit(solution)/shard_map/ppermute | solution.py:65
  44.7 22.3 %collective-permute-start.6 = (bf16[128,3072]{1,0:T(8,128)(2,1)}, bf16[128,3072]{1,0:T(8,128)(2,1)}, u32[]{:S(2)}, u32[]{:S(2)}) collective-permute-start(bf16[128,3072]{1,0:T(8,128)(2,1)} %pad_maximum_fusion.3), channel_id=1, source_target_pairs={{0,64},{16,80},{32,96},{48,112},{64,0},{80,16},{96,32},{112,48},{1... | collective-permute-start | bytes 2359304 | tf_op jit(solution)/shard_map/ppermute | solution.py:65
  47.7 32.9 %collective-permute-start.9 = (bf16[128,3072]{1,0:T(8,128)(2,1)S(1)}, bf16[128,3072]{1,0:T(8,128)(2,1)}, u32[]{:S(2)}, u32[]{:S(2)}) collective-permute-start(bf16[128,3072]{1,0:T(8,128)(2,1)S(1)} %pad_maximum_fusion.2.refs_0_), channel_id=1, source_target_pairs={{0,64},{16,80},{32,96},{48,112},{64,0},{80,16},{96,32},{112,48},{1... | collective-permute-start | bytes 2359304 | tf_op jit(solution)/shard_map/ppermute | solution.py:65
  48.3 1.1 copy-start.1
  49.4 1.1 copy-start.5
  50.6 1.1 copy-start.7
  51.7 96.4 %copy-start.8 = (s32[3]{0:T(128)}, s32[3]{0:T(128)S(1)}, u32[]{:S(2)}) copy-start(s32[3]{0:T(128)S(1)} %pad_add_fusion.place) | copy-start | bytes 40
  61.8 24.2 %copy-start.3 = (bf16[64,3072]{1,0:T(8,128)(2,1)S(1)}, bf16[64,3072]{1,0:T(8,128)(2,1)}, u32[]{:S(2)}) copy-start(bf16[64,3072]{1,0:T(8,128)(2,1)} %copy-done.2) | copy-start | bytes 1179652
  81.6 14.3 %collective-permute-start.11 = (bf16[64,3072]{1,0:T(8,128)(2,1)S(1)}, bf16[64,3072]{1,0:T(8,128)(2,1)S(1)}, u32[]{:S(2)}, u32[]{:S(2)}) collective-permute-start(bf16[64,3072]{1,0:T(8,128)(2,1)S(1)} %slice.36), channel_id=1, source_target_pairs={{0,16},{16,32},{32,48},{48,0},{64,80},{80,96},{96,112},{112,64},{1... | collective-permute-start | bytes 1179656 | tf_op jit(solution)/shard_map/ppermute | solution.py:65
  82.8 14.0 %collective-permute-start.12 = (bf16[64,3072]{1,0:T(8,128)(2,1)S(1)}, bf16[64,3072]{1,0:T(8,128)(2,1)S(1)}, u32[]{:S(2)}, u32[]{:S(2)}) collective-permute-start(bf16[64,3072]{1,0:T(8,128)(2,1)S(1)} %slice.37), channel_id=1, source_target_pairs={{0,48},{16,0},{32,16},{48,32},{64,112},{80,64},{96,80},{112,96},{1... | collective-permute-start | bytes 1179656 | tf_op jit(solution)/shard_map/ppermute | solution.py:65
  86.0 15.2 %collective-permute-start.10 = (f32[4,64,1536]{2,1,0:T(8,128)}, f32[4,64,1536]{2,1,0:T(8,128)S(1)}, u32[]{:S(2)}, u32[]{:S(2)}) collective-permute-start(f32[4,64,1536]{2,1,0:T(8,128)} %bitcast.18), channel_id=1, source_target_pairs={{0,1},{1,0},{2,3},{3,2},{4,5},{5,4},{6,7},{7,6},{8,9},{9,8},{10,11... | collective-permute-start | bytes 4718600 | tf_op jit(solution)/shard_map/ppermute | solution.py:261
  96.0 0.7 copy-start.9
  96.7 0.8 copy-start.11
  97.5 3.8 %collective-permute-start.13 = (f32[4,64,1536]{2,1,0:T(8,128)S(1)}, f32[4,64,1536]{2,1,0:T(8,128)S(1)}, u32[]{:S(2)}, u32[]{:S(2)}) collective-permute-start(f32[4,64,1536]{2,1,0:T(8,128)S(1)} %bitcast.16), channel_id=1, source_target_pairs={{0,1},{1,0},{2,3},{3,2},{4,5},{5,4},{6,7},{7,6},{8,9},{9,8},{10,11... | collective-permute-start | bytes 4718600 | tf_op jit(solution)/shard_map/ppermute | solution.py:261
  98.0 20.9 %collective-permute-start.15 = (bf16[128,3072]{1,0:T(8,128)(2,1)}, bf16[128,3072]{1,0:T(8,128)(2,1)S(1)}, u32[]{:S(2)}, u32[]{:S(2)}) collective-permute-start(bf16[128,3072]{1,0:T(8,128)(2,1)} %collective-permute-done.9.refs_3_), channel_id=1, source_target_pairs={{0,16},{16,32},{32,48},{48,0},{64,80},{80,96},{96,112},{112,64},{1... | collective-permute-start | bytes 2359304 | tf_op jit(solution)/shard_map/ppermute | solution.py:65
  98.0 21.0 %collective-permute-start.16 = (bf16[128,3072]{1,0:T(8,128)(2,1)}, bf16[128,3072]{1,0:T(8,128)(2,1)}, u32[]{:S(2)}, u32[]{:S(2)}) collective-permute-start(bf16[128,3072]{1,0:T(8,128)(2,1)} %collective-permute-done.9.refs_3_), channel_id=1, source_target_pairs={{0,48},{16,0},{32,16},{48,32},{64,112},{80,64},{96,80},{112,96},{1... | collective-permute-start | bytes 2359304 | tf_op jit(solution)/shard_map/ppermute | solution.py:65
  101.2 49.2 %collective-permute-start.20 = (bf16[1024,1536]{1,0:T(8,128)(2,1)}, bf16[1024,1536]{1,0:T(8,128)(2,1)}, u32[]{:S(2)}, u32[]{:S(2)}) collective-permute-start(bf16[1024,1536]{1,0:T(8,128)(2,1)} %bitcast.5.refs_4_), channel_id=1, source_target_pairs={{0,1},{1,0},{2,3},{3,2},{4,5},{5,4},{6,7},{7,6},{8,9},{9,8},{10,11... | collective-permute-start | bytes 9437192 | tf_op jit(solution)/shard_map/ppermute | solution.py:375
  103.6 46.9 %all-to-all-start.1 = ((f32[8,64,1536]{2,1,0:T(8,128)}), f32[8,64,1536]{2,1,0:T(8,128)}, u32[]{:S(2)}, u32[]{:S(2)}) async-start(f32[8,64,1536]{2,1,0:T(8,128)} %chips.2), calls=%async_computation.1 | async-start | bytes 6291456 | tf_op jit(solution)/shard_map/all_to_all | solution.py:284
  118.9 14.6 %collective-permute-start.17 = (bf16[64,3072]{1,0:T(8,128)(2,1)S(1)}, bf16[64,3072]{1,0:T(8,128)(2,1)S(1)}, u32[]{:S(2)}, u32[]{:S(2)}) collective-permute-start(bf16[64,3072]{1,0:T(8,128)(2,1)S(1)} %slice.40), channel_id=1, source_target_pairs={{0,16},{16,32},{32,48},{48,0},{64,80},{80,96},{96,112},{112,64},{1... | collective-permute-start | bytes 1179656 | tf_op jit(solution)/shard_map/ppermute | solution.py:65
  120.0 13.5 %copy-start.10 = (bf16[64,3072]{1,0:T(8,128)(2,1)S(1)}, bf16[64,3072]{1,0:T(8,128)(2,1)}, u32[]{:S(2)}) copy-start(bf16[64,3072]{1,0:T(8,128)(2,1)} %copy-done.9) | copy-start | bytes 1179652
  120.0 13.5 %copy-start.12 = (bf16[64,3072]{1,0:T(8,128)(2,1)S(1)}, bf16[64,3072]{1,0:T(8,128)(2,1)}, u32[]{:S(2)}) copy-start(bf16[64,3072]{1,0:T(8,128)(2,1)} %copy-done.11) | copy-start | bytes 1179652
  120.0 13.5 %collective-permute-start.18 = (bf16[64,3072]{1,0:T(8,128)(2,1)S(1)}, bf16[64,3072]{1,0:T(8,128)(2,1)S(1)}, u32[]{:S(2)}, u32[]{:S(2)}) collective-permute-start(bf16[64,3072]{1,0:T(8,128)(2,1)S(1)} %slice.41), channel_id=1, source_target_pairs={{0,48},{16,0},{32,16},{48,32},{64,112},{80,64},{96,80},{112,96},{1... | collective-permute-start | bytes 1179656 | tf_op jit(solution)/shard_map/ppermute | solution.py:65
  133.4 11.4 %collective-permute-start.14 = (f32[4,64,1536]{2,1,0:T(8,128)S(1)}, f32[4,64,1536]{2,1,0:T(8,128)S(1)}, u32[]{:S(2)}, u32[]{:S(2)}) collective-permute-start(f32[4,64,1536]{2,1,0:T(8,128)S(1)} %bitcast.17), channel_id=1, source_target_pairs={{0,1},{1,0},{2,3},{3,2},{4,5},{5,4},{6,7},{7,6},{8,9},{9,8},{10,11... | collective-permute-start | bytes 4718600 | tf_op jit(solution)/shard_map/ppermute | solution.py:261
  144.2 3.8 %collective-permute-start.19 = (f32[4,64,1536]{2,1,0:T(8,128)}, f32[4,64,1536]{2,1,0:T(8,128)S(1)}, u32[]{:S(2)}, u32[]{:S(2)}) collective-permute-start(f32[4,64,1536]{2,1,0:T(8,128)} %bitcast.19), channel_id=1, source_target_pairs={{0,1},{1,0},{2,3},{3,2},{4,5},{5,4},{6,7},{7,6},{8,9},{9,8},{10,11... | collective-permute-start | bytes 4718600 | tf_op jit(solution)/shard_map/ppermute | solution.py:261
  150.4 44.2 %all-to-all-start.2 = ((f32[8,64,1536]{2,1,0:T(8,128)}), f32[8,64,1536]{2,1,0:T(8,128)S(1)}, u32[]{:S(2)}, u32[]{:S(2)}) async-start(f32[8,64,1536]{2,1,0:T(8,128)} %chips.3), calls=%async_computation.2 | async-start | bytes 6291456 | tf_op jit(solution)/shard_map/all_to_all | solution.py:284

commit v4 on v3

--- a/solution.py
+++ b/solution.py
@@ -339,9 +339,10 @@
         if k > 1:
             made = multiply((k - 2, FAR))
         last = min(k, count - 1)
-        ready, made, arrays["across", k - 1], arrays["own", last] = fence(
-            ready, made, arrays["across", k - 1], arrays["own", last]
-        )
+        if k < count:
+            ready, arrays["across", k - 1], arrays["own", last] = fence(
+                ready, arrays["across", k - 1], arrays["own", last]
+            )
         if made:
             far[k - 2] = made[0]
             made = [chip_sums(place, near[k - 2], far[k - 2])]

time: 197 us -> 193 us (0.980)
  waiting for transfers between devices: 57 us -> 54 us
    ppermute x15, waiting for transfers between devices: 37.7 us -> 34.6 us  [send(): return lax.ppermute(value, 'row', move)]
    unnamed x29 -> x21, local copies, waits for them, and re-layouts: 5.93 us -> 5.43 us
  transfers between devices with their start and end apart: 24 -> 24, of which waited for: 9 -> 10; matrix products, arithmetic and copies ran while one was open for 5% -> 6% of each run, Pallas kernels for 38% -> 38%
where the time goes in v4:
time: 193 us; the launch traced here: 192 us
  Pallas kernels  73.6 us (38%)
  waiting for transfers between devices  54 us (28%)
  starting transfers between devices  45 us (23%)
  local copies, waits for them, and re-layouts  13.8 us (7%)
  other arithmetic  4.36 us (2%)
    pallas_call x4, Pallas kernels, contract_units(): pl.pallas_call(functools.partial(units_kernel, parts), grid=(features //...  40.6 us
    ppermute x15, waiting for transfers between devices, send(): return lax.ppermute(value, 'row', move)  34.6 us
    pallas_call x1, Pallas kernels, contract_tokens(): pl.pallas_call(functools.partial(tokens_kernel, groups), grid=(units // t...  28.3 us
    ppermute x15, starting transfers between devices, send(): return lax.ppermute(value, 'row', move)  27.2 us
    all_to_all x2, starting transfers between devices, sum_direct(): lax.all_to_all(chip, 'col', 0, 0, axis_index_groups=CHIP_GROUPS, tiled=True)  10.8 us
    all_to_all x2, waiting for transfers between devices, sum_direct(): lax.all_to_all(chip, 'col', 0, 0, axis_index_groups=CHIP_GROUPS, tiled=True)  8.05 us
    ppermute x1, waiting for transfers between devices, local(): beside = lax.ppermute(inputs, 'col', BESIDE)  7.76 us
    unnamed x21, local copies, waits for them, and re-layouts  5.43 us
  transfers between devices with their start and end apart: 24, of which 10 were waited for; matrix products, arithmetic and copies ran while one was open for 6% of the time, Pallas kernels for 38%

profile of v4, /device:TPU:0, one launch (start us, length us, event | category | flops | bytes accessed | tf_op | source)
XLA Modules:
  0.0 191.7 jit_solution(8888169440322927124)
XLA Ops:
  0.6 1.5 fusion
  2.2 2.1 %collective-permute-start = (bf16[128,3072]{1,0:T(8,128)(2,1)S(1)}, bf16[128,3072]{1,0:T(8,128)(2,1)S(1)}, u32[]{:S(2)}, u32[]{:S(2)}) collective-permute-start(bf16[128,3072]{1,0:T(8,128)(2,1)S(1)} %pad_maximum_fusion.refs_0_), channel_id=1, source_target_pairs={{0,16},{16,32},{32,48},{48,0},{64,80},{80,96},{96,112},{112,64},{1... | collective-permute-start | bytes 2359304 | tf_op jit(solution)/shard_map/ppermute | solution.py:65
  4.2 2.2 %collective-permute-start.1 = (bf16[128,3072]{1,0:T(8,128)(2,1)S(1)}, bf16[128,3072]{1,0:T(8,128)(2,1)S(1)}, u32[]{:S(2)}, u32[]{:S(2)}) collective-permute-start(bf16[128,3072]{1,0:T(8,128)(2,1)S(1)} %pad_maximum_fusion.refs_0_), channel_id=1, source_target_pairs={{0,48},{16,0},{32,16},{48,32},{64,112},{80,64},{96,80},{112,96},{1... | collective-permute-start | bytes 2359304 | tf_op jit(solution)/shard_map/ppermute | solution.py:65
  6.4 1.5 collective-permute-start.2
  7.9 2.7 %collective-permute-start.5 = (bf16[128,3072]{1,0:T(8,128)(2,1)S(1)}, bf16[128,3072]{1,0:T(8,128)(2,1)S(1)}, u32[]{:S(2)}, u32[]{:S(2)}) collective-permute-start(bf16[128,3072]{1,0:T(8,128)(2,1)S(1)} %pad_maximum_fusion.refs_0_), channel_id=1, source_target_pairs={{0,64},{16,80},{32,96},{48,112},{64,0},{80,16},{96,32},{112,48},{1... | collective-permute-start | bytes 2359304 | tf_op jit(solution)/shard_map/ppermute | solution.py:65
  10.7 7.8 %collective-permute-done.2 = bf16[128,1536]{1,0:T(8,128)(2,1)S(1)} collective-permute-done((bf16[128,1536]{1,0:T(8,128)(2,1)S(1)}, bf16[128,1536]{1,0:T(8,128)(2,1)S(1)}, u32[]{:S(2)}, u32[]{:S(2)}) %collective-permute-start.2) | collective-permute-done | bytes 393248 | tf_op jit(solution)/shard_map/ppermute | solution.py:307
  18.5 5.4 %collective-permute-done.refs_1_ = bf16[128,3072]{1,0:T(8,128)(2,1)S(1)} collective-permute-done((bf16[128,3072]{1,0:T(8,128)(2,1)S(1)}, bf16[128,3072]{1,0:T(8,128)(2,1)S(1)}, u32[]{:S(2)}, u32[]{:S(2)}) %collective-permute-start) | collective-permute-done | bytes 786464 | tf_op jit(solution)/shard_map/ppermute | solution.py:65
  23.9 2.1 %broadcast_in_dim.3 = bf16[4,256,1536]{2,1,0:T(8,128)(2,1)} broadcast(bf16[256,1536]{1,0:T(8,128)(2,1)S(1)} %pad_maximum_fusion.1), dimensions={1,2} | broadcast | bytes 3932160 | tf_op jit(solution)/shard_map/broadcast_in_dim | solution.py:323
  26.0 0.8 slice.34
  26.7 1.1 collective-permute-start.3
  27.9 2.2 %collective-permute-start.4 = (bf16[64,3072]{1,0:T(8,128)(2,1)S(1)}, bf16[64,3072]{1,0:T(8,128)(2,1)S(1)}, u32[]{:S(2)}, u32[]{:S(2)}) collective-permute-start(bf16[64,3072]{1,0:T(8,128)(2,1)S(1)} %slice.35), channel_id=1, source_target_pairs={{0,48},{16,0},{32,16},{48,32},{64,112},{80,64},{96,80},{112,96},{1... | collective-permute-start | bytes 1179656 | tf_op jit(solution)/shard_map/ppermute | solution.py:65
  30.1 4.6 %all-to-all-start = ((bf16[4,256,1536]{2,1,0:T(8,128)(2,1)}), bf16[4,256,1536]{2,1,0:T(8,128)(2,1)}, u32[]{:S(2)}, u32[]{:S(2)}) async-start(bf16[4,256,1536]{2,1,0:T(8,128)(2,1)} %broadcast_in_dim.3), calls=%async_computation | async-start | bytes 6291456 | tf_op jit(solution)/shard_map/all_to_all | solution.py:327
  34.7 1.3 collective-permute-done.5.refs_3_
  36.1 2.4 %collective-permute-done.3.refs_0_ = bf16[64,3072]{1,0:T(8,128)(2,1)S(1)} collective-permute-done((bf16[64,3072]{1,0:T(8,128)(2,1)}, bf16[64,3072]{1,0:T(8,128)(2,1)S(1)}, u32[]{:S(2)}, u32[]{:S(2)}) %collective-permute-start.3) | collective-permute-done | bytes 393248 | tf_op jit(solution)/shard_map/ppermute | solution.py:65
  38.5 1.0 constant_dynamic-update-slice_fusion.1
  39.5 1.0 constant_dynamic-update-slice_fusion
  40.4 0.7 collective-permute-start.7
  41.1 2.6 %collective-permute-start.8 = (bf16[256,3072]{1,0:T(8,128)(2,1)}, bf16[256,3072]{1,0:T(8,128)(2,1)}, u32[]{:S(2)}, u32[]{:S(2)}) collective-permute-start(bf16[256,3072]{1,0:T(8,128)(2,1)} %constant_dynamic-update-slice_fusion), channel_id=1, source_target_pairs={{0,48},{16,0},{32,16},{48,32},{64,112},{80,64},{96,80},{112,96},{1... | collective-permute-start | bytes 4718600 | tf_op jit(solution)/shard_map/ppermute | solution.py:65
  43.7 1.0 pad_maximum_fusion.3
  44.7 3.0 %collective-permute-start.6 = (bf16[128,3072]{1,0:T(8,128)(2,1)}, bf16[128,3072]{1,0:T(8,128)(2,1)}, u32[]{:S(2)}, u32[]{:S(2)}) collective-permute-start(bf16[128,3072]{1,0:T(8,128)(2,1)} %pad_maximum_fusion.3), channel_id=1, source_target_pairs={{0,64},{16,80},{32,96},{48,112},{64,0},{80,16},{96,32},{112,48},{1... | collective-permute-start | bytes 2359304 | tf_op jit(solution)/shard_map/ppermute | solution.py:65
  48.3 1.1 copy-done.1
  49.4 1.1 copy-done.5
  50.6 1.1 copy-done.7
  51.7 10.2 %units.4 = (f32[256,1536]{1,0:T(8,128)S(1)}, f32[256,1536]{1,0:T(8,128)}, bf16[512,3072]{1,0:T(8,128)(2,1)}) custom-call(s32[3]{0:T(128)S(1)} %pad_add_fusion.place, bf16[128,3072]{1,0:T(8,128)(2,1)S(1)} %pad_maximum_fusion.refs_0_, bf16[128,3072]{1,0:T(8,128)(2,1)S(1)} %copy-done.5, bf16[128,3072]{1,0:T(8,128)(2,1)S(1)} %copy-done.7, ...), custom_call_target="tpu_custom_call" | custom-call | flops 4831838208 | bytes 18874368 | tf_op jit(solution)/shard_map/units/pallas_call | solution.py:135
  61.9 5.1 %collective-permute-done.6.refs_4_ = bf16[128,3072]{1,0:T(8,128)(2,1)} collective-permute-done((bf16[128,3072]{1,0:T(8,128)(2,1)}, bf16[128,3072]{1,0:T(8,128)(2,1)}, u32[]{:S(2)}, u32[]{:S(2)}) %collective-permute-start.6) | collective-permute-done | bytes 786464 | tf_op jit(solution)/shard_map/ppermute | solution.py:65
  67.0 13.6 %collective-permute-done.9.refs_3_ = bf16[128,3072]{1,0:T(8,128)(2,1)} collective-permute-done((bf16[128,3072]{1,0:T(8,128)(2,1)S(1)}, bf16[128,3072]{1,0:T(8,128)(2,1)}, u32[]{:S(2)}, u32[]{:S(2)}) %collective-permute-start.9) | collective-permute-done | bytes 786464 | tf_op jit(solution)/shard_map/ppermute | solution.py:65
  80.7 1.0 copy-done.3
  81.7 9.9 %units.5 = (f32[256,1536]{1,0:T(8,128)S(1)}, f32[256,1536]{1,0:T(8,128)S(1)}, bf16[512,3072]{1,0:T(8,128)(2,1)}) custom-call(s32[3]{0:T(128)S(1)} %pad_add_fusion.place, bf16[64,3072]{1,0:T(8,128)(2,1)S(1)} %collective-permute-done.3.refs_0_, bf16[64,3072]{1,0:T(8,128)(2,1)S(1)} %copy-done.3, bf16[256,3072]{1,0:T(8,128)(2,1)} %collective-permute-done.7.refs_2_.refs_1_, ...), custom_call_target="tpu_custom_call" | custom-call | flops 4831838208 | bytes 18874368 | tf_op jit(solution)/shard_map/units/pallas_call | solution.py:135
  91.6 0.6 collective-permute-start.11
  92.2 3.2 %collective-permute-start.16 = (bf16[128,3072]{1,0:T(8,128)(2,1)}, bf16[128,3072]{1,0:T(8,128)(2,1)}, u32[]{:S(2)}, u32[]{:S(2)}) collective-permute-start(bf16[128,3072]{1,0:T(8,128)(2,1)} %collective-permute-done.9.refs_3_), channel_id=1, source_target_pairs={{0,48},{16,0},{32,16},{48,32},{64,112},{80,64},{96,80},{112,96},{1... | collective-permute-start | bytes 2359304 | tf_op jit(solution)/shard_map/ppermute | solution.py:65
  95.4 2.3 %chips.2 = f32[8,64,1536]{2,1,0:T(8,128)} custom-call(s32[3]{0:T(128)S(1)} %pad_add_fusion.place, f32[4,64,1536]{2,1,0:T(8,128)S(1)} %bitcast.12, f32[4,64,1536]{2,1,0:T(8,128)S(1)} %collective-permute-done.10.near_got, f32[4,64,1536]{2,1,0:T(8,128)S(1)} %bitcast.14, f32[4,64,1536]{2,1,0:T(8,128)S(1)} %collective-permute-done.11.far_got), custom_call_target="tpu_custom_call" | custom-call | flops 786432 | bytes 9437184 | tf_op jit(solution)/shard_map/chips/pallas_call | solution.py:263
  97.7 5.4 %all-to-all-start.1 = ((f32[8,64,1536]{2,1,0:T(8,128)}), f32[8,64,1536]{2,1,0:T(8,128)}, u32[]{:S(2)}, u32[]{:S(2)}) async-start(f32[8,64,1536]{2,1,0:T(8,128)} %chips.2), calls=%async_computation.1 | async-start | bytes 6291456 | tf_op jit(solution)/shard_map/all_to_all | solution.py:284
  103.2 1.0 slice.36
  104.2 1.0 slice.37
  105.3 3.2 %collective-permute-start.14 = (bf16[64,3072]{1,0:T(8,128)(2,1)S(1)}, bf16[64,3072]{1,0:T(8,128)(2,1)S(1)}, u32[]{:S(2)}, u32[]{:S(2)}) collective-permute-start(bf16[64,3072]{1,0:T(8,128)(2,1)S(1)} %slice.37), channel_id=1, source_target_pairs={{0,48},{16,0},{32,16},{48,32},{64,112},{80,64},{96,80},{112,96},{1... | collective-permute-start | bytes 1179656 | tf_op jit(solution)/shard_map/ppermute | solution.py:65
  108.5 5.5 %collective-permute-done.15.refs_2_ = bf16[128,3072]{1,0:T(8,128)(2,1)S(1)} collective-permute-done((bf16[128,3072]{1,0:T(8,128)(2,1)}, bf16[128,3072]{1,0:T(8,128)(2,1)S(1)}, u32[]{:S(2)}, u32[]{:S(2)}) %collective-permute-start.15) | collective-permute-done | bytes 786464 | tf_op jit(solution)/shard_map/ppermute | solution.py:65
  114.1 1.0 slice.41
  115.1 3.5 %collective-permute-start.18 = (bf16[64,3072]{1,0:T(8,128)(2,1)S(1)}, bf16[64,3072]{1,0:T(8,128)(2,1)S(1)}, u32[]{:S(2)}, u32[]{:S(2)}) collective-permute-start(bf16[64,3072]{1,0:T(8,128)(2,1)S(1)} %slice.41), channel_id=1, source_target_pairs={{0,48},{16,0},{32,16},{48,32},{64,112},{80,64},{96,80},{112,96},{1... | collective-permute-start | bytes 1179656 | tf_op jit(solution)/shard_map/ppermute | solution.py:65
  118.6 9.9 %units.6 = (f32[256,1536]{1,0:T(8,128)S(1)}, f32[256,1536]{1,0:T(8,128)S(1)}, bf16[512,3072]{1,0:T(8,128)(2,1)}) custom-call(s32[3]{0:T(128)S(1)} %pad_add_fusion.place, bf16[128,3072]{1,0:T(8,128)(2,1)S(1)} %pad_maximum_fusion.2.refs_0_, bf16[256,3072]{1,0:T(8,128)(2,1)} %collective-permute-done.7.refs_2_.refs_1_, ...), custom_call_target="tpu_custom_call" | custom-call | flops 4831838208 | bytes 18874368 | tf_op jit(solution)/shard_map/units/pallas_call | solution.py:135
  128.7 1.3 collective-permute-done.17.refs_4_
  130.0 10.6 %units.7 = (f32[256,1536]{1,0:T(8,128)S(1)}, f32[256,1536]{1,0:T(8,128)}, bf16[512,3072]{1,0:T(8,128)(2,1)}) custom-call(s32[3]{0:T(128)S(1)} %pad_add_fusion.place, bf16[64,3072]{1,0:T(8,128)(2,1)S(1)} %collective-permute-done.13.refs_0_, bf16[64,3072]{1,0:T(8,128)(2,1)S(1)} %collective-permute-done.14.refs_1_, ...), custom_call_target="tpu_custom_call" | custom-call | flops 4831838208 | bytes 18874368 | tf_op jit(solution)/shard_map/units/pallas_call | solution.py:135
  140.7 3.6 %collective-permute-done.19.far_got = f32[4,64,1536]{2,1,0:T(8,128)S(1)} collective-permute-done((f32[4,64,1536]{2,1,0:T(8,128)}, f32[4,64,1536]{2,1,0:T(8,128)S(1)}, u32[]{:S(2)}, u32[]{:S(2)}) %collective-permute-start.19) | collective-permute-done | bytes 1572896 | tf_op jit(solution)/shard_map/ppermute | solution.py:261
  144.3 2.4 %chips.3 = f32[8,64,1536]{2,1,0:T(8,128)} custom-call(s32[3]{0:T(128)S(1)} %pad_add_fusion.place, f32[4,64,1536]{2,1,0:T(8,128)S(1)} %bitcast.13, f32[4,64,1536]{2,1,0:T(8,128)S(1)} %collective-permute-done.12.near_got, f32[4,64,1536]{2,1,0:T(8,128)S(1)} %bitcast.15, f32[4,64,1536]{2,1,0:T(8,128)S(1)} %collective-permute-done.19.far_got), custom_call_target="tpu_custom_call" | custom-call | flops 786432 | bytes 9437184 | tf_op jit(solution)/shard_map/chips/pallas_call | solution.py:263
  146.7 5.4 %all-to-all-start.2 = ((f32[8,64,1536]{2,1,0:T(8,128)}), f32[8,64,1536]{2,1,0:T(8,128)S(1)}, u32[]{:S(2)}, u32[]{:S(2)}) async-start(f32[8,64,1536]{2,1,0:T(8,128)} %chips.3), calls=%async_computation.2 | async-start | bytes 6291456 | tf_op jit(solution)/shard_map/all_to_all | solution.py:284
  152.2 28.3 %tokens.1 = bf16[1536,3072]{1,0:T(8,128)(2,1)} custom-call(s32[3]{0:T(128)} %copy-done.8, bf16[512,3072]{1,0:T(8,128)(2,1)} %get-tuple-element.58.refs_0_, bf16[512,3072]{1,0:T(8,128)(2,1)} %get-tuple-element.59.refs_1_, bf16[512,3072]{1,0:T(8,128)(2,1)} %get-tuple-element.60.refs_2_, bf16[512,3072]{1,0:T(8,128)(2,1)} %get-tuple-element.61.refs_3_, ...), custom_call_target="tpu_custom_call" | custom-call | flops 19327352832 | bytes 28311552 | tf_op jit(solution)/shard_map/tokens/pallas_call | solution.py:222
  180.5 2.1 %reduce_sum.18 = bf16[64,1536]{1,0:T(8,128)(2,1)S(1)} reduce(f32[8,64,1536]{2,1,0:T(8,128)} %all-to-all-done.1, f32[]{:T(128)} %constant.38.clone.1), dimensions={0}, to_apply=%region_0.1 | reduce | flops 688128 | bytes 3342340 | tf_op jit(solution)/shard_map/reduce_sum | solution.py:285
  182.6 8.0 %all-to-all-done.2 = f32[8,64,1536]{2,1,0:T(8,128)S(1)} async-done(((f32[8,64,1536]{2,1,0:T(8,128)}), f32[8,64,1536]{2,1,0:T(8,128)S(1)}, u32[]{:S(2)}, u32[]{:S(2)}) %all-to-all-start.2) | async-done | bytes 3145760 | tf_op jit(solution)/shard_map/all_to_all | solution.py:284
  190.9 0.8 pad_maximum_fusion.4
  (45 shorter events, 1.5 us)
Async XLA Ops:
  2.1 4.3 %copy-start.9 = (bf16[128,1536]{1,0:T(8,128)(2,1)S(1)}, bf16[128,1536]{1,0:T(8,128)(2,1)}, u32[]{:S(2)}) copy-start(bf16[128,1536]{1,0:T(8,128)(2,1)} %param.3) | copy-start | bytes 1179652
  2.2 21.7 %collective-permute-start = (bf16[128,3072]{1,0:T(8,128)(2,1)S(1)}, bf16[128,3072]{1,0:T(8,128)(2,1)S(1)}, u32[]{:S(2)}, u32[]{:S(2)}) collective-permute-start(bf16[128,3072]{1,0:T(8,128)(2,1)S(1)} %pad_maximum_fusion.refs_0_), channel_id=1, source_target_pairs={{0,16},{16,32},{32,48},{48,0},{64,80},{80,96},{96,112},{112,64},{1... | collective-permute-start | bytes 2359304 | tf_op jit(solution)/shard_map/ppermute | solution.py:65
  4.2 19.7 %collective-permute-start.1 = (bf16[128,3072]{1,0:T(8,128)(2,1)S(1)}, bf16[128,3072]{1,0:T(8,128)(2,1)S(1)}, u32[]{:S(2)}, u32[]{:S(2)}) collective-permute-start(bf16[128,3072]{1,0:T(8,128)(2,1)S(1)} %pad_maximum_fusion.refs_0_), channel_id=1, source_target_pairs={{0,48},{16,0},{32,16},{48,32},{64,112},{80,64},{96,80},{112,96},{1... | collective-permute-start | bytes 2359304 | tf_op jit(solution)/shard_map/ppermute | solution.py:65
  6.4 12.0 %collective-permute-start.2 = (bf16[128,1536]{1,0:T(8,128)(2,1)S(1)}, bf16[128,1536]{1,0:T(8,128)(2,1)S(1)}, u32[]{:S(2)}, u32[]{:S(2)}) collective-permute-start(bf16[128,1536]{1,0:T(8,128)(2,1)S(1)} %copy-done.9), channel_id=1, source_target_pairs={{0,2},{1,3},{2,0},{3,1},{4,6},{5,7},{6,4},{7,5},{8,10},{9,11},{10,... | collective-permute-start | bytes 1179656 | tf_op jit(solution)/shard_map/ppermute | solution.py:307
  7.9 28.1 %collective-permute-start.5 = (bf16[128,3072]{1,0:T(8,128)(2,1)S(1)}, bf16[128,3072]{1,0:T(8,128)(2,1)S(1)}, u32[]{:S(2)}, u32[]{:S(2)}) collective-permute-start(bf16[128,3072]{1,0:T(8,128)(2,1)S(1)} %pad_maximum_fusion.refs_0_), channel_id=1, source_target_pairs={{0,64},{16,80},{32,96},{48,112},{64,0},{80,16},{96,32},{112,48},{1... | collective-permute-start | bytes 2359304 | tf_op jit(solution)/shard_map/ppermute | solution.py:65
  23.9 2.1 %copy-start.4 = (bf16[128,3072]{1,0:T(8,128)(2,1)}, bf16[128,3072]{1,0:T(8,128)(2,1)S(1)}, u32[]{:S(2)}) copy-start(bf16[128,3072]{1,0:T(8,128)(2,1)S(1)} %collective-permute-done.refs_1_) | copy-start | bytes 2359300
  23.9 4.0 %copy-start.6 = (bf16[128,3072]{1,0:T(8,128)(2,1)}, bf16[128,3072]{1,0:T(8,128)(2,1)S(1)}, u32[]{:S(2)}) copy-start(bf16[128,3072]{1,0:T(8,128)(2,1)S(1)} %collective-permute-done.1.refs_2_) | copy-start | bytes 2359300
  26.7 11.7 %collective-permute-start.3 = (bf16[64,3072]{1,0:T(8,128)(2,1)}, bf16[64,3072]{1,0:T(8,128)(2,1)S(1)}, u32[]{:S(2)}, u32[]{:S(2)}) collective-permute-start(bf16[64,3072]{1,0:T(8,128)(2,1)} %slice.34), channel_id=1, source_target_pairs={{0,16},{16,32},{32,48},{48,0},{64,80},{80,96},{96,112},{112,64},{1... | collective-permute-start | bytes 1179656 | tf_op jit(solution)/shard_map/ppermute | solution.py:65
  27.9 10.6 %collective-permute-start.4 = (bf16[64,3072]{1,0:T(8,128)(2,1)S(1)}, bf16[64,3072]{1,0:T(8,128)(2,1)S(1)}, u32[]{:S(2)}, u32[]{:S(2)}) collective-permute-start(bf16[64,3072]{1,0:T(8,128)(2,1)S(1)} %slice.35), channel_id=1, source_target_pairs={{0,48},{16,0},{32,16},{48,32},{64,112},{80,64},{96,80},{112,96},{1... | collective-permute-start | bytes 1179656 | tf_op jit(solution)/shard_map/ppermute | solution.py:65
  30.1 50.5 %all-to-all-start = ((bf16[4,256,1536]{2,1,0:T(8,128)(2,1)}), bf16[4,256,1536]{2,1,0:T(8,128)(2,1)}, u32[]{:S(2)}, u32[]{:S(2)}) async-start(bf16[4,256,1536]{2,1,0:T(8,128)(2,1)} %broadcast_in_dim.3), calls=%async_computation | async-start | bytes 6291456 | tf_op jit(solution)/shard_map/all_to_all | solution.py:327
  36.1 4.4 %copy-start = (bf16[128,3072]{1,0:T(8,128)(2,1)}, bf16[128,3072]{1,0:T(8,128)(2,1)S(1)}, u32[]{:S(2)}) copy-start(bf16[128,3072]{1,0:T(8,128)(2,1)S(1)} %collective-permute-done.5.refs_3_) | copy-start | bytes 2359300
  38.5 5.2 %copy-start.2 = (bf16[64,3072]{1,0:T(8,128)(2,1)}, bf16[64,3072]{1,0:T(8,128)(2,1)S(1)}, u32[]{:S(2)}) copy-start(bf16[64,3072]{1,0:T(8,128)(2,1)S(1)} %collective-permute-done.4.refs_1_) | copy-start | bytes 1179652
  40.4 40.1 %collective-permute-start.7 = (bf16[256,3072]{1,0:T(8,128)(2,1)}, bf16[256,3072]{1,0:T(8,128)(2,1)}, u32[]{:S(2)}, u32[]{:S(2)}) collective-permute-start(bf16[256,3072]{1,0:T(8,128)(2,1)} %constant_dynamic-update-slice_fusion), channel_id=1, source_target_pairs={{0,16},{16,32},{32,48},{48,0},{64,80},{80,96},{96,112},{112,64},{1... | collective-permute-start | bytes 4718600 | tf_op jit(solution)/shard_map/ppermute | solution.py:65
  41.1 39.5 %collective-permute-start.8 = (bf16[256,3072]{1,0:T(8,128)(2,1)}, bf16[256,3072]{1,0:T(8,128)(2,1)}, u32[]{:S(2)}, u32[]{:S(2)}) collective-permute-start(bf16[256,3072]{1,0:T(8,128)(2,1)} %constant_dynamic-update-slice_fusion), channel_id=1, source_target_pairs={{0,48},{16,0},{32,16},{48,32},{64,112},{80,64},{96,80},{112,96},{1... | collective-permute-start | bytes 4718600 | tf_op jit(solution)/shard_map/ppermute | solution.py:65
  44.7 22.3 %collective-permute-start.6 = (bf16[128,3072]{1,0:T(8,128)(2,1)}, bf16[128,3072]{1,0:T(8,128)(2,1)}, u32[]{:S(2)}, u32[]{:S(2)}) collective-permute-start(bf16[128,3072]{1,0:T(8,128)(2,1)} %pad_maximum_fusion.3), channel_id=1, source_target_pairs={{0,64},{16,80},{32,96},{48,112},{64,0},{80,16},{96,32},{112,48},{1... | collective-permute-start | bytes 2359304 | tf_op jit(solution)/shard_map/ppermute | solution.py:65
  47.7 32.9 %collective-permute-start.9 = (bf16[128,3072]{1,0:T(8,128)(2,1)S(1)}, bf16[128,3072]{1,0:T(8,128)(2,1)}, u32[]{:S(2)}, u32[]{:S(2)}) collective-permute-start(bf16[128,3072]{1,0:T(8,128)(2,1)S(1)} %pad_maximum_fusion.2.refs_0_), channel_id=1, source_target_pairs={{0,64},{16,80},{32,96},{48,112},{64,0},{80,16},{96,32},{112,48},{1... | collective-permute-start | bytes 2359304 | tf_op jit(solution)/shard_map/ppermute | solution.py:65
  48.3 1.1 copy-start.1
  49.4 1.1 copy-start.5
  50.6 1.1 copy-start.7
  51.7 92.7 %copy-start.8 = (s32[3]{0:T(128)}, s32[3]{0:T(128)S(1)}, u32[]{:S(2)}) copy-start(s32[3]{0:T(128)S(1)} %pad_add_fusion.place) | copy-start | bytes 40
  80.6 14.8 %collective-permute-start.10 = (f32[4,64,1536]{2,1,0:T(8,128)}, f32[4,64,1536]{2,1,0:T(8,128)S(1)}, u32[]{:S(2)}, u32[]{:S(2)}) collective-permute-start(f32[4,64,1536]{2,1,0:T(8,128)} %bitcast.18), channel_id=1, source_target_pairs={{0,1},{1,0},{2,3},{3,2},{4,5},{5,4},{6,7},{7,6},{8,9},{9,8},{10,11... | collective-permute-start | bytes 4718600 | tf_op jit(solution)/shard_map/ppermute | solution.py:261
  80.7 1.0 copy-start.3
  91.6 3.8 %collective-permute-start.11 = (f32[4,64,1536]{2,1,0:T(8,128)S(1)}, f32[4,64,1536]{2,1,0:T(8,128)S(1)}, u32[]{:S(2)}, u32[]{:S(2)}) collective-permute-start(f32[4,64,1536]{2,1,0:T(8,128)S(1)} %bitcast.17), channel_id=1, source_target_pairs={{0,1},{1,0},{2,3},{3,2},{4,5},{5,4},{6,7},{7,6},{8,9},{9,8},{10,11... | collective-permute-start | bytes 4718600 | tf_op jit(solution)/shard_map/ppermute | solution.py:261
  92.2 21.8 %collective-permute-start.15 = (bf16[128,3072]{1,0:T(8,128)(2,1)}, bf16[128,3072]{1,0:T(8,128)(2,1)S(1)}, u32[]{:S(2)}, u32[]{:S(2)}) collective-permute-start(bf16[128,3072]{1,0:T(8,128)(2,1)} %collective-permute-done.9.refs_3_), channel_id=1, source_target_pairs={{0,16},{16,32},{32,48},{48,0},{64,80},{80,96},{96,112},{112,64},{1... | collective-permute-start | bytes 2359304 | tf_op jit(solution)/shard_map/ppermute | solution.py:65
  92.2 21.9 %collective-permute-start.16 = (bf16[128,3072]{1,0:T(8,128)(2,1)}, bf16[128,3072]{1,0:T(8,128)(2,1)}, u32[]{:S(2)}, u32[]{:S(2)}) collective-permute-start(bf16[128,3072]{1,0:T(8,128)(2,1)} %collective-permute-done.9.refs_3_), channel_id=1, source_target_pairs={{0,48},{16,0},{32,16},{48,32},{64,112},{80,64},{96,80},{112,96},{1... | collective-permute-start | bytes 2359304 | tf_op jit(solution)/shard_map/ppermute | solution.py:65
  95.4 51.3 %collective-permute-start.20 = (bf16[1024,1536]{1,0:T(8,128)(2,1)}, bf16[1024,1536]{1,0:T(8,128)(2,1)}, u32[]{:S(2)}, u32[]{:S(2)}) collective-permute-start(bf16[1024,1536]{1,0:T(8,128)(2,1)} %bitcast.5.refs_4_), channel_id=1, source_target_pairs={{0,1},{1,0},{2,3},{3,2},{4,5},{5,4},{6,7},{7,6},{8,9},{9,8},{10,11... | collective-permute-start | bytes 9437192 | tf_op jit(solution)/shard_map/ppermute | solution.py:376
  97.7 49.0 %all-to-all-start.1 = ((f32[8,64,1536]{2,1,0:T(8,128)}), f32[8,64,1536]{2,1,0:T(8,128)}, u32[]{:S(2)}, u32[]{:S(2)}) async-start(f32[8,64,1536]{2,1,0:T(8,128)} %chips.2), calls=%async_computation.1 | async-start | bytes 6291456 | tf_op jit(solution)/shard_map/all_to_all | solution.py:284
  105.2 23.3 %collective-permute-start.13 = (bf16[64,3072]{1,0:T(8,128)(2,1)S(1)}, bf16[64,3072]{1,0:T(8,128)(2,1)S(1)}, u32[]{:S(2)}, u32[]{:S(2)}) collective-permute-start(bf16[64,3072]{1,0:T(8,128)(2,1)S(1)} %slice.36), channel_id=1, source_target_pairs={{0,16},{16,32},{32,48},{48,0},{64,80},{80,96},{96,112},{112,64},{1... | collective-permute-start | bytes 1179656 | tf_op jit(solution)/shard_map/ppermute | solution.py:65
  105.3 23.4 %collective-permute-start.14 = (bf16[64,3072]{1,0:T(8,128)(2,1)S(1)}, bf16[64,3072]{1,0:T(8,128)(2,1)S(1)}, u32[]{:S(2)}, u32[]{:S(2)}) collective-permute-start(bf16[64,3072]{1,0:T(8,128)(2,1)S(1)} %slice.37), channel_id=1, source_target_pairs={{0,48},{16,0},{32,16},{48,32},{64,112},{80,64},{96,80},{112,96},{1... | collective-permute-start | bytes 1179656 | tf_op jit(solution)/shard_map/ppermute | solution.py:65
  114.0 16.0 %collective-permute-start.17 = (bf16[64,3072]{1,0:T(8,128)(2,1)S(1)}, bf16[64,3072]{1,0:T(8,128)(2,1)S(1)}, u32[]{:S(2)}, u32[]{:S(2)}) collective-permute-start(bf16[64,3072]{1,0:T(8,128)(2,1)S(1)} %slice.40), channel_id=1, source_target_pairs={{0,16},{16,32},{32,48},{48,0},{64,80},{80,96},{96,112},{112,64},{1... | collective-permute-start | bytes 1179656 | tf_op jit(solution)/shard_map/ppermute | solution.py:65
  115.1 14.8 %collective-permute-start.18 = (bf16[64,3072]{1,0:T(8,128)(2,1)S(1)}, bf16[64,3072]{1,0:T(8,128)(2,1)S(1)}, u32[]{:S(2)}, u32[]{:S(2)}) collective-permute-start(bf16[64,3072]{1,0:T(8,128)(2,1)S(1)} %slice.41), channel_id=1, source_target_pairs={{0,48},{16,0},{32,16},{48,32},{64,112},{80,64},{96,80},{112,96},{1... | collective-permute-start | bytes 1179656 | tf_op jit(solution)/shard_map/ppermute | solution.py:65
  128.6 12.2 %collective-permute-start.12 = (f32[4,64,1536]{2,1,0:T(8,128)S(1)}, f32[4,64,1536]{2,1,0:T(8,128)S(1)}, u32[]{:S(2)}, u32[]{:S(2)}) collective-permute-start(f32[4,64,1536]{2,1,0:T(8,128)S(1)} %bitcast.16), channel_id=1, source_target_pairs={{0,1},{1,0},{2,3},{3,2},{4,5},{5,4},{6,7},{7,6},{8,9},{9,8},{10,11... | collective-permute-start | bytes 4718600 | tf_op jit(solution)/shard_map/ppermute | solution.py:261
  140.6 3.7 %collective-permute-start.19 = (f32[4,64,1536]{2,1,0:T(8,128)}, f32[4,64,1536]{2,1,0:T(8,128)S(1)}, u32[]{:S(2)}, u32[]{:S(2)}) collective-permute-start(f32[4,64,1536]{2,1,0:T(8,128)} %bitcast.19), channel_id=1, source_target_pairs={{0,1},{1,0},{2,3},{3,2},{4,5},{5,4},{6,7},{7,6},{8,9},{9,8},{10,11... | collective-permute-start | bytes 4718600 | tf_op jit(solution)/shard_map/ppermute | solution.py:261
  146.7 43.9 %all-to-all-start.2 = ((f32[8,64,1536]{2,1,0:T(8,128)}), f32[8,64,1536]{2,1,0:T(8,128)S(1)}, u32[]{:S(2)}, u32[]{:S(2)}) async-start(f32[8,64,1536]{2,1,0:T(8,128)} %chips.3), calls=%async_computation.2 | async-start | bytes 6291456 | tf_op jit(solution)/shard_map/all_to_all | solution.py:284

commit v5 on v4

--- a/solution.py
+++ b/solution.py
@@ -357,7 +357,8 @@
             near[0] = multiply((0, NEAR))[0]
         if k < count:
             exchange()
-            arrays["across", k] = send(arrays["own", k], CROSS)
+            own_k, near[0] = fence(arrays["own", k], near[0])
+            arrays["across", k] = send(own_k, CROSS)
             started.append(("across", k))
         if k == count:
             started = []

time: 193 us -> 194 us (level)
  local copies, waits for them, and re-layouts: 13.8 us -> 11.8 us
    unnamed x21 -> x27, local copies, waits for them, and re-layouts: 5.43 us -> 4.32 us
  transfers between devices with their start and end apart: 24 -> 24, of which waited for: 10 -> 11; matrix products, arithmetic and copies ran while one was open for 6% -> 4% of each run, Pallas kernels for 38% -> 38%
where the time goes in v5:
time: 194 us; the launch traced here: 193 us
  Pallas kernels  73.3 us (38%)
  waiting for transfers between devices  55.8 us (29%)
  starting transfers between devices  45.6 us (24%)
  local copies, waits for them, and re-layouts  11.8 us (6%)
  other arithmetic  5.36 us (3%)
    pallas_call x4, Pallas kernels, contract_units(): pl.pallas_call(functools.partial(units_kernel, parts), grid=(features //...  40.4 us
    ppermute x15, waiting for transfers between devices, send(): return lax.ppermute(value, 'row', move)  36.3 us
    pallas_call x1, Pallas kernels, contract_tokens(): pl.pallas_call(functools.partial(tokens_kernel, groups), grid=(units // t...  28.3 us
    ppermute x15, starting transfers between devices, send(): return lax.ppermute(value, 'row', move)  27.9 us
    all_to_all x2, starting transfers between devices, sum_direct(): lax.all_to_all(chip, 'col', 0, 0, axis_index_groups=CHIP_GROUPS, tiled=True)  10.8 us
    all_to_all x2, waiting for transfers between devices, sum_direct(): lax.all_to_all(chip, 'col', 0, 0, axis_index_groups=CHIP_GROUPS, tiled=True)  8.14 us
    ppermute x1, waiting for transfers between devices, local(): beside = lax.ppermute(inputs, 'col', BESIDE)  7.76 us
    all_to_all x1, starting transfers between devices, local(): lax.all_to_all(copies, 'col', 0, 0, axis_index_groups=Y_GROUPS, tiled=True)  4.64 us
  transfers between devices with their start and end apart: 24, of which 11 were waited for; matrix products, arithmetic and copies ran while one was open for 4% of the time, Pallas kernels for 38%

profile of v5, /device:TPU:0, one launch (start us, length us, event | category | flops | bytes accessed | tf_op | source)
XLA Modules:
  0.0 192.7 jit_solution(9280395245546297936)
XLA Ops:
  0.6 1.5 fusion
  2.2 2.1 %collective-permute-start = (bf16[128,3072]{1,0:T(8,128)(2,1)S(1)}, bf16[128,3072]{1,0:T(8,128)(2,1)S(1)}, u32[]{:S(2)}, u32[]{:S(2)}) collective-permute-start(bf16[128,3072]{1,0:T(8,128)(2,1)S(1)} %pad_maximum_fusion.refs_0_), channel_id=1, source_target_pairs={{0,16},{16,32},{32,48},{48,0},{64,80},{80,96},{96,112},{112,64},{1... | collective-permute-start | bytes 2359304 | tf_op jit(solution)/shard_map/ppermute | solution.py:65
  4.2 2.2 %collective-permute-start.1 = (bf16[128,3072]{1,0:T(8,128)(2,1)S(1)}, bf16[128,3072]{1,0:T(8,128)(2,1)S(1)}, u32[]{:S(2)}, u32[]{:S(2)}) collective-permute-start(bf16[128,3072]{1,0:T(8,128)(2,1)S(1)} %pad_maximum_fusion.refs_0_), channel_id=1, source_target_pairs={{0,48},{16,0},{32,16},{48,32},{64,112},{80,64},{96,80},{112,96},{1... | collective-permute-start | bytes 2359304 | tf_op jit(solution)/shard_map/ppermute | solution.py:65
  6.4 1.5 collective-permute-start.2
  7.9 2.7 %collective-permute-start.5 = (bf16[128,3072]{1,0:T(8,128)(2,1)S(1)}, bf16[128,3072]{1,0:T(8,128)(2,1)S(1)}, u32[]{:S(2)}, u32[]{:S(2)}) collective-permute-start(bf16[128,3072]{1,0:T(8,128)(2,1)S(1)} %pad_maximum_fusion.refs_0_), channel_id=1, source_target_pairs={{0,64},{16,80},{32,96},{48,112},{64,0},{80,16},{96,32},{112,48},{1... | collective-permute-start | bytes 2359304 | tf_op jit(solution)/shard_map/ppermute | solution.py:65
  10.7 7.8 %collective-permute-done.2 = bf16[128,1536]{1,0:T(8,128)(2,1)S(1)} collective-permute-done((bf16[128,1536]{1,0:T(8,128)(2,1)S(1)}, bf16[128,1536]{1,0:T(8,128)(2,1)S(1)}, u32[]{:S(2)}, u32[]{:S(2)}) %collective-permute-start.2) | collective-permute-done | bytes 393248 | tf_op jit(solution)/shard_map/ppermute | solution.py:307
  18.5 5.4 %collective-permute-done.refs_1_ = bf16[128,3072]{1,0:T(8,128)(2,1)S(1)} collective-permute-done((bf16[128,3072]{1,0:T(8,128)(2,1)S(1)}, bf16[128,3072]{1,0:T(8,128)(2,1)S(1)}, u32[]{:S(2)}, u32[]{:S(2)}) %collective-permute-start) | collective-permute-done | bytes 786464 | tf_op jit(solution)/shard_map/ppermute | solution.py:65
  23.9 2.1 %broadcast_in_dim.3 = bf16[4,256,1536]{2,1,0:T(8,128)(2,1)} broadcast(bf16[256,1536]{1,0:T(8,128)(2,1)S(1)} %pad_maximum_fusion.1), dimensions={1,2} | broadcast | bytes 3932160 | tf_op jit(solution)/shard_map/broadcast_in_dim | solution.py:323
  26.0 1.2 collective-permute-start.3
  27.2 0.8 slice.35
  27.9 2.1 %collective-permute-start.4 = (bf16[64,3072]{1,0:T(8,128)(2,1)}, bf16[64,3072]{1,0:T(8,128)(2,1)S(1)}, u32[]{:S(2)}, u32[]{:S(2)}) collective-permute-start(bf16[64,3072]{1,0:T(8,128)(2,1)} %slice.35), channel_id=1, source_target_pairs={{0,48},{16,0},{32,16},{48,32},{64,112},{80,64},{96,80},{112,96},{1... | collective-permute-start | bytes 1179656 | tf_op jit(solution)/shard_map/ppermute | solution.py:65
  30.1 4.6 %all-to-all-start = ((bf16[4,256,1536]{2,1,0:T(8,128)(2,1)}), bf16[4,256,1536]{2,1,0:T(8,128)(2,1)}, u32[]{:S(2)}, u32[]{:S(2)}) async-start(bf16[4,256,1536]{2,1,0:T(8,128)(2,1)} %broadcast_in_dim.3), calls=%async_computation | async-start | bytes 6291456 | tf_op jit(solution)/shard_map/all_to_all | solution.py:327
  34.8 1.3 collective-permute-done.5.refs_3_
  36.1 1.5 collective-permute-done.3.refs_0_
  37.6 0.4 collective-permute-done.4.refs_1_
  38.1 1.5 collective-permute-start.7
  39.5 2.3 %collective-permute-start.8 = (bf16[256,3072]{1,0:T(8,128)(2,1)S(1)}, bf16[256,3072]{1,0:T(8,128)(2,1)}, u32[]{:S(2)}, u32[]{:S(2)}) collective-permute-start(bf16[256,3072]{1,0:T(8,128)(2,1)S(1)} %constant_dynamic-update-slice_fusion), channel_id=1, source_target_pairs={{0,48},{16,0},{32,16},{48,32},{64,112},{80,64},{96,80},{112,96},{1... | collective-permute-start | bytes 4718600 | tf_op jit(solution)/shard_map/ppermute | solution.py:65
  41.9 3.1 %collective-permute-start.6 = (bf16[128,3072]{1,0:T(8,128)(2,1)S(1)}, bf16[128,3072]{1,0:T(8,128)(2,1)S(1)}, u32[]{:S(2)}, u32[]{:S(2)}) collective-permute-start(bf16[128,3072]{1,0:T(8,128)(2,1)S(1)} %pad_maximum_fusion.3), channel_id=1, source_target_pairs={{0,64},{16,80},{32,96},{48,112},{64,0},{80,16},{96,32},{112,48},{1... | collective-permute-start | bytes 2359304 | tf_op jit(solution)/shard_map/ppermute | solution.py:65
  45.0 10.2 %units.4 = (f32[256,1536]{1,0:T(8,128)S(1)}, f32[256,1536]{1,0:T(8,128)}, bf16[512,3072]{1,0:T(8,128)(2,1)}) custom-call(s32[3]{0:T(128)S(1)} %pad_add_fusion.place, bf16[128,3072]{1,0:T(8,128)(2,1)S(1)} %pad_maximum_fusion.refs_0_, bf16[128,3072]{1,0:T(8,128)(2,1)S(1)} %copy-done.5, bf16[128,3072]{1,0:T(8,128)(2,1)S(1)} %copy-done.7, ...), custom_call_target="tpu_custom_call" | custom-call | flops 4831838208 | bytes 18874368 | tf_op jit(solution)/shard_map/units/pallas_call | solution.py:135
  55.2 0.6 collective-permute-start.9
  55.8 8.2 %collective-permute-done.6.refs_4_ = bf16[128,3072]{1,0:T(8,128)(2,1)S(1)} collective-permute-done((bf16[128,3072]{1,0:T(8,128)(2,1)S(1)}, bf16[128,3072]{1,0:T(8,128)(2,1)S(1)}, u32[]{:S(2)}, u32[]{:S(2)}) %collective-permute-start.6) | collective-permute-done | bytes 786464 | tf_op jit(solution)/shard_map/ppermute | solution.py:65
  64.0 0.9 copy-done.9
  64.9 12.8 %collective-permute-done.9.refs_3_ = bf16[128,3072]{1,0:T(8,128)(2,1)} collective-permute-done((bf16[128,3072]{1,0:T(8,128)(2,1)S(1)}, bf16[128,3072]{1,0:T(8,128)(2,1)}, u32[]{:S(2)}, u32[]{:S(2)}) %collective-permute-start.9) | collective-permute-done | bytes 786464 | tf_op jit(solution)/shard_map/ppermute | solution.py:65
  77.7 1.2 copy-done.12
  78.9 1.0 copy-done.3
  79.9 1.1 copy-done.10
  81.0 9.7 %units.5 = (f32[256,1536]{1,0:T(8,128)S(1)}, f32[256,1536]{1,0:T(8,128)S(1)}, bf16[512,3072]{1,0:T(8,128)(2,1)}) custom-call(s32[3]{0:T(128)S(1)} %pad_add_fusion.place, bf16[64,3072]{1,0:T(8,128)(2,1)S(1)} %collective-permute-done.3.refs_0_, bf16[64,3072]{1,0:T(8,128)(2,1)S(1)} %copy-done.3, bf16[256,3072]{1,0:T(8,128)(2,1)} %copy-done.12, ...), custom_call_target="tpu_custom_call" | custom-call | flops 4831838208 | bytes 18874368 | tf_op jit(solution)/shard_map/units/pallas_call | solution.py:135
  90.7 0.6 collective-permute-start.11
  91.3 3.2 %collective-permute-start.16 = (bf16[128,3072]{1,0:T(8,128)(2,1)}, bf16[128,3072]{1,0:T(8,128)(2,1)}, u32[]{:S(2)}, u32[]{:S(2)}) collective-permute-start(bf16[128,3072]{1,0:T(8,128)(2,1)} %collective-permute-done.9.refs_3_), channel_id=1, source_target_pairs={{0,48},{16,0},{32,16},{48,32},{64,112},{80,64},{96,80},{112,96},{1... | collective-permute-start | bytes 2359304 | tf_op jit(solution)/shard_map/ppermute | solution.py:65
  94.5 2.3 %chips.2 = f32[8,64,1536]{2,1,0:T(8,128)} custom-call(s32[3]{0:T(128)S(1)} %pad_add_fusion.place, f32[4,64,1536]{2,1,0:T(8,128)S(1)} %bitcast.12, f32[4,64,1536]{2,1,0:T(8,128)S(1)} %collective-permute-done.10.near_got, f32[4,64,1536]{2,1,0:T(8,128)S(1)} %bitcast.14, f32[4,64,1536]{2,1,0:T(8,128)S(1)} %collective-permute-done.11.far_got), custom_call_target="tpu_custom_call" | custom-call | flops 786432 | bytes 9437184 | tf_op jit(solution)/shard_map/chips/pallas_call | solution.py:263
  96.8 5.4 %all-to-all-start.1 = ((f32[8,64,1536]{2,1,0:T(8,128)}), f32[8,64,1536]{2,1,0:T(8,128)}, u32[]{:S(2)}, u32[]{:S(2)}) async-start(f32[8,64,1536]{2,1,0:T(8,128)} %chips.2), calls=%async_computation.1 | async-start | bytes 6291456 | tf_op jit(solution)/shard_map/all_to_all | solution.py:284
  102.2 1.0 slice.36
  103.2 1.0 slice.37
  104.4 3.2 %collective-permute-start.14 = (bf16[64,3072]{1,0:T(8,128)(2,1)S(1)}, bf16[64,3072]{1,0:T(8,128)(2,1)S(1)}, u32[]{:S(2)}, u32[]{:S(2)}) collective-permute-start(bf16[64,3072]{1,0:T(8,128)(2,1)S(1)} %slice.37), channel_id=1, source_target_pairs={{0,48},{16,0},{32,16},{48,32},{64,112},{80,64},{96,80},{112,96},{1... | collective-permute-start | bytes 1179656 | tf_op jit(solution)/shard_map/ppermute | solution.py:65
  107.6 5.5 %collective-permute-done.15.refs_2_ = bf16[128,3072]{1,0:T(8,128)(2,1)S(1)} collective-permute-done((bf16[128,3072]{1,0:T(8,128)(2,1)}, bf16[128,3072]{1,0:T(8,128)(2,1)S(1)}, u32[]{:S(2)}, u32[]{:S(2)}) %collective-permute-start.15) | collective-permute-done | bytes 786464 | tf_op jit(solution)/shard_map/ppermute | solution.py:65
  113.2 1.0 slice.41
  114.2 3.5 %collective-permute-start.18 = (bf16[64,3072]{1,0:T(8,128)(2,1)S(1)}, bf16[64,3072]{1,0:T(8,128)(2,1)S(1)}, u32[]{:S(2)}, u32[]{:S(2)}) collective-permute-start(bf16[64,3072]{1,0:T(8,128)(2,1)S(1)} %slice.41), channel_id=1, source_target_pairs={{0,48},{16,0},{32,16},{48,32},{64,112},{80,64},{96,80},{112,96},{1... | collective-permute-start | bytes 1179656 | tf_op jit(solution)/shard_map/ppermute | solution.py:65
  117.7 9.9 %units.6 = (f32[256,1536]{1,0:T(8,128)S(1)}, f32[256,1536]{1,0:T(8,128)S(1)}, bf16[512,3072]{1,0:T(8,128)(2,1)}) custom-call(s32[3]{0:T(128)S(1)} %pad_add_fusion.place, bf16[128,3072]{1,0:T(8,128)(2,1)S(1)} %pad_maximum_fusion.2.refs_0_, bf16[256,3072]{1,0:T(8,128)(2,1)} %copy-done.12, bf16[256,3072]{1,0:T(8,128)(2,1)} %collective-permute-done.8.refs_3_.refs_2_, ...), custom_call_target="tpu_custom_call" | custom-call | flops 4831838208 | bytes 18874368 | tf_op jit(solution)/shard_map/units/pallas_call | solution.py:135
  127.7 1.3 collective-permute-done.17.refs_4_
  129.1 10.7 %units.7 = (f32[256,1536]{1,0:T(8,128)S(1)}, f32[256,1536]{1,0:T(8,128)}, bf16[512,3072]{1,0:T(8,128)(2,1)}) custom-call(s32[3]{0:T(128)S(1)} %pad_add_fusion.place, bf16[64,3072]{1,0:T(8,128)(2,1)S(1)} %collective-permute-done.13.refs_0_, bf16[64,3072]{1,0:T(8,128)(2,1)S(1)} %collective-permute-done.14.refs_1_, ...), custom_call_target="tpu_custom_call" | custom-call | flops 4831838208 | bytes 18874368 | tf_op jit(solution)/shard_map/units/pallas_call | solution.py:135
  139.8 3.6 %collective-permute-done.19.far_got = f32[4,64,1536]{2,1,0:T(8,128)S(1)} collective-permute-done((f32[4,64,1536]{2,1,0:T(8,128)}, f32[4,64,1536]{2,1,0:T(8,128)S(1)}, u32[]{:S(2)}, u32[]{:S(2)}) %collective-permute-start.19) | collective-permute-done | bytes 1572896 | tf_op jit(solution)/shard_map/ppermute | solution.py:261
  143.4 2.3 %chips.3 = f32[8,64,1536]{2,1,0:T(8,128)} custom-call(s32[3]{0:T(128)S(1)} %pad_add_fusion.place, f32[4,64,1536]{2,1,0:T(8,128)S(1)} %bitcast.13, f32[4,64,1536]{2,1,0:T(8,128)S(1)} %collective-permute-done.12.near_got, f32[4,64,1536]{2,1,0:T(8,128)S(1)} %bitcast.15, f32[4,64,1536]{2,1,0:T(8,128)S(1)} %collective-permute-done.19.far_got), custom_call_target="tpu_custom_call" | custom-call | flops 786432 | bytes 9437184 | tf_op jit(solution)/shard_map/chips/pallas_call | solution.py:263
  145.7 5.4 %all-to-all-start.2 = ((f32[8,64,1536]{2,1,0:T(8,128)}), f32[8,64,1536]{2,1,0:T(8,128)}, u32[]{:S(2)}, u32[]{:S(2)}) async-start(f32[8,64,1536]{2,1,0:T(8,128)} %chips.3), calls=%async_computation.2 | async-start | bytes 6291456 | tf_op jit(solution)/shard_map/all_to_all | solution.py:284
  151.1 28.3 %tokens.1 = bf16[1536,3072]{1,0:T(8,128)(2,1)} custom-call(s32[3]{0:T(128)} %copy-done.8, bf16[512,3072]{1,0:T(8,128)(2,1)} %get-tuple-element.64.refs_0_, bf16[512,3072]{1,0:T(8,128)(2,1)} %get-tuple-element.65.refs_1_, bf16[512,3072]{1,0:T(8,128)(2,1)} %get-tuple-element.66.refs_2_, bf16[512,3072]{1,0:T(8,128)(2,1)} %get-tuple-element.67.refs_3_, ...), custom_call_target="tpu_custom_call" | custom-call | flops 19327352832 | bytes 28311552 | tf_op jit(solution)/shard_map/tokens/pallas_call | solution.py:222
  179.5 2.1 %reduce_sum.18 = bf16[64,1536]{1,0:T(8,128)(2,1)S(1)} reduce(f32[8,64,1536]{2,1,0:T(8,128)} %all-to-all-done.1, f32[]{:T(128)} %constant.38.clone.1), dimensions={0}, to_apply=%region_0.1 | reduce | flops 688128 | bytes 3342340 | tf_op jit(solution)/shard_map/reduce_sum | solution.py:285
  181.6 8.1 %all-to-all-done.2 = f32[8,64,1536]{2,1,0:T(8,128)} async-done(((f32[8,64,1536]{2,1,0:T(8,128)}), f32[8,64,1536]{2,1,0:T(8,128)}, u32[]{:S(2)}, u32[]{:S(2)}) %all-to-all-start.2) | async-done | bytes 3145760 | tf_op jit(solution)/shard_map/all_to_all | solution.py:284
  189.8 2.1 %reduce_sum.19 = bf16[64,1536]{1,0:T(8,128)(2,1)S(1)} reduce(f32[8,64,1536]{2,1,0:T(8,128)} %all-to-all-done.2, f32[]{:T(128)} %constant.38.clone.1), dimensions={0}, to_apply=%region_1.2 | reduce | flops 688128 | bytes 3342340 | tf_op jit(solution)/shard_map/reduce_sum | solution.py:285
  191.9 0.8 pad_maximum_fusion.4
  (51 shorter events, 0.9 us)
Async XLA Ops:
  2.1 4.3 %copy-start.11 = (bf16[128,1536]{1,0:T(8,128)(2,1)S(1)}, bf16[128,1536]{1,0:T(8,128)(2,1)}, u32[]{:S(2)}) copy-start(bf16[128,1536]{1,0:T(8,128)(2,1)} %param.3) | copy-start | bytes 1179652
  2.2 21.7 %collective-permute-start = (bf16[128,3072]{1,0:T(8,128)(2,1)S(1)}, bf16[128,3072]{1,0:T(8,128)(2,1)S(1)}, u32[]{:S(2)}, u32[]{:S(2)}) collective-permute-start(bf16[128,3072]{1,0:T(8,128)(2,1)S(1)} %pad_maximum_fusion.refs_0_), channel_id=1, source_target_pairs={{0,16},{16,32},{32,48},{48,0},{64,80},{80,96},{96,112},{112,64},{1... | collective-permute-start | bytes 2359304 | tf_op jit(solution)/shard_map/ppermute | solution.py:65
  4.2 19.7 %collective-permute-start.1 = (bf16[128,3072]{1,0:T(8,128)(2,1)S(1)}, bf16[128,3072]{1,0:T(8,128)(2,1)S(1)}, u32[]{:S(2)}, u32[]{:S(2)}) collective-permute-start(bf16[128,3072]{1,0:T(8,128)(2,1)S(1)} %pad_maximum_fusion.refs_0_), channel_id=1, source_target_pairs={{0,48},{16,0},{32,16},{48,32},{64,112},{80,64},{96,80},{112,96},{1... | collective-permute-start | bytes 2359304 | tf_op jit(solution)/shard_map/ppermute | solution.py:65
  6.4 12.0 %collective-permute-start.2 = (bf16[128,1536]{1,0:T(8,128)(2,1)S(1)}, bf16[128,1536]{1,0:T(8,128)(2,1)S(1)}, u32[]{:S(2)}, u32[]{:S(2)}) collective-permute-start(bf16[128,1536]{1,0:T(8,128)(2,1)S(1)} %copy-done.11), channel_id=1, source_target_pairs={{0,2},{1,3},{2,0},{3,1},{4,6},{5,7},{6,4},{7,5},{8,10},{9,11},{10,... | collective-permute-start | bytes 1179656 | tf_op jit(solution)/shard_map/ppermute | solution.py:307
  7.9 28.1 %collective-permute-start.5 = (bf16[128,3072]{1,0:T(8,128)(2,1)S(1)}, bf16[128,3072]{1,0:T(8,128)(2,1)S(1)}, u32[]{:S(2)}, u32[]{:S(2)}) collective-permute-start(bf16[128,3072]{1,0:T(8,128)(2,1)S(1)} %pad_maximum_fusion.refs_0_), channel_id=1, source_target_pairs={{0,64},{16,80},{32,96},{48,112},{64,0},{80,16},{96,32},{112,48},{1... | collective-permute-start | bytes 2359304 | tf_op jit(solution)/shard_map/ppermute | solution.py:65
  23.9 2.1 %copy-start.4 = (bf16[128,3072]{1,0:T(8,128)(2,1)}, bf16[128,3072]{1,0:T(8,128)(2,1)S(1)}, u32[]{:S(2)}) copy-start(bf16[128,3072]{1,0:T(8,128)(2,1)S(1)} %collective-permute-done.refs_1_) | copy-start | bytes 2359300
  23.9 3.3 %copy-start.6 = (bf16[128,3072]{1,0:T(8,128)(2,1)}, bf16[128,3072]{1,0:T(8,128)(2,1)S(1)}, u32[]{:S(2)}) copy-start(bf16[128,3072]{1,0:T(8,128)(2,1)S(1)} %collective-permute-done.1.refs_2_) | copy-start | bytes 2359300
  26.0 11.6 %collective-permute-start.3 = (bf16[64,3072]{1,0:T(8,128)(2,1)S(1)}, bf16[64,3072]{1,0:T(8,128)(2,1)S(1)}, u32[]{:S(2)}, u32[]{:S(2)}) collective-permute-start(bf16[64,3072]{1,0:T(8,128)(2,1)S(1)} %slice.34), channel_id=1, source_target_pairs={{0,16},{16,32},{32,48},{48,0},{64,80},{80,96},{96,112},{112,64},{1... | collective-permute-start | bytes 1179656 | tf_op jit(solution)/shard_map/ppermute | solution.py:65
  27.9 10.0 %collective-permute-start.4 = (bf16[64,3072]{1,0:T(8,128)(2,1)}, bf16[64,3072]{1,0:T(8,128)(2,1)S(1)}, u32[]{:S(2)}, u32[]{:S(2)}) collective-permute-start(bf16[64,3072]{1,0:T(8,128)(2,1)} %slice.35), channel_id=1, source_target_pairs={{0,48},{16,0},{32,16},{48,32},{64,112},{80,64},{96,80},{112,96},{1... | collective-permute-start | bytes 1179656 | tf_op jit(solution)/shard_map/ppermute | solution.py:65
  30.1 48.8 %all-to-all-start = ((bf16[4,256,1536]{2,1,0:T(8,128)(2,1)}), bf16[4,256,1536]{2,1,0:T(8,128)(2,1)}, u32[]{:S(2)}, u32[]{:S(2)}) async-start(bf16[4,256,1536]{2,1,0:T(8,128)(2,1)} %broadcast_in_dim.3), calls=%async_computation | async-start | bytes 6291456 | tf_op jit(solution)/shard_map/all_to_all | solution.py:327
  34.8 108.6 %copy-start.8 = (s32[3]{0:T(128)}, s32[3]{0:T(128)S(1)}, u32[]{:S(2)}) copy-start(s32[3]{0:T(128)S(1)} %pad_add_fusion.place) | copy-start | bytes 40
  36.1 2.0 %copy-start = (bf16[128,3072]{1,0:T(8,128)(2,1)}, bf16[128,3072]{1,0:T(8,128)(2,1)S(1)}, u32[]{:S(2)}) copy-start(bf16[128,3072]{1,0:T(8,128)(2,1)S(1)} %collective-permute-done.5.refs_3_) | copy-start | bytes 2359300
  37.9 3.9 %copy-start.2 = (bf16[64,3072]{1,0:T(8,128)(2,1)}, bf16[64,3072]{1,0:T(8,128)(2,1)S(1)}, u32[]{:S(2)}) copy-start(bf16[64,3072]{1,0:T(8,128)(2,1)S(1)} %collective-permute-done.4.refs_1_) | copy-start | bytes 1179652
  38.0 7.0 %copy-start.5 = (bf16[128,3072]{1,0:T(8,128)(2,1)S(1)}, bf16[128,3072]{1,0:T(8,128)(2,1)}, u32[]{:S(2)}) copy-start(bf16[128,3072]{1,0:T(8,128)(2,1)} %copy-done.4) | copy-start | bytes 2359300
  38.0 7.0 %copy-start.7 = (bf16[128,3072]{1,0:T(8,128)(2,1)S(1)}, bf16[128,3072]{1,0:T(8,128)(2,1)}, u32[]{:S(2)}) copy-start(bf16[128,3072]{1,0:T(8,128)(2,1)} %copy-done.6) | copy-start | bytes 2359300
  38.1 39.6 %collective-permute-start.7 = (bf16[256,3072]{1,0:T(8,128)(2,1)S(1)}, bf16[256,3072]{1,0:T(8,128)(2,1)S(1)}, u32[]{:S(2)}, u32[]{:S(2)}) collective-permute-start(bf16[256,3072]{1,0:T(8,128)(2,1)S(1)} %constant_dynamic-update-slice_fusion), channel_id=1, source_target_pairs={{0,16},{16,32},{32,48},{48,0},{64,80},{80,96},{96,112},{112,64},{1... | collective-permute-start | bytes 4718600 | tf_op jit(solution)/shard_map/ppermute | solution.py:65
  39.5 5.5 %copy-start.1 = (bf16[128,3072]{1,0:T(8,128)(2,1)S(1)}, bf16[128,3072]{1,0:T(8,128)(2,1)}, u32[]{:S(2)}) copy-start(bf16[128,3072]{1,0:T(8,128)(2,1)} %copy-done) | copy-start | bytes 2359300
  39.5 39.3 %collective-permute-start.8 = (bf16[256,3072]{1,0:T(8,128)(2,1)S(1)}, bf16[256,3072]{1,0:T(8,128)(2,1)}, u32[]{:S(2)}, u32[]{:S(2)}) collective-permute-start(bf16[256,3072]{1,0:T(8,128)(2,1)S(1)} %constant_dynamic-update-slice_fusion), channel_id=1, source_target_pairs={{0,48},{16,0},{32,16},{48,32},{64,112},{80,64},{96,80},{112,96},{1... | collective-permute-start | bytes 4718600 | tf_op jit(solution)/shard_map/ppermute | solution.py:65
  41.9 22.1 %collective-permute-start.6 = (bf16[128,3072]{1,0:T(8,128)(2,1)S(1)}, bf16[128,3072]{1,0:T(8,128)(2,1)S(1)}, u32[]{:S(2)}, u32[]{:S(2)}) collective-permute-start(bf16[128,3072]{1,0:T(8,128)(2,1)S(1)} %pad_maximum_fusion.3), channel_id=1, source_target_pairs={{0,64},{16,80},{32,96},{48,112},{64,0},{80,16},{96,32},{112,48},{1... | collective-permute-start | bytes 2359304 | tf_op jit(solution)/shard_map/ppermute | solution.py:65
  55.2 22.5 %collective-permute-start.9 = (bf16[128,3072]{1,0:T(8,128)(2,1)S(1)}, bf16[128,3072]{1,0:T(8,128)(2,1)}, u32[]{:S(2)}, u32[]{:S(2)}) collective-permute-start(bf16[128,3072]{1,0:T(8,128)(2,1)S(1)} %pad_maximum_fusion.2.refs_0_), channel_id=1, source_target_pairs={{0,64},{16,80},{32,96},{48,112},{64,0},{80,16},{96,32},{112,48},{1... | collective-permute-start | bytes 2359304 | tf_op jit(solution)/shard_map/ppermute | solution.py:65
  63.9 0.9 copy-start.9
  77.7 1.2 copy-start.12
  78.9 15.6 %collective-permute-start.10 = (f32[4,64,1536]{2,1,0:T(8,128)}, f32[4,64,1536]{2,1,0:T(8,128)S(1)}, u32[]{:S(2)}, u32[]{:S(2)}) collective-permute-start(f32[4,64,1536]{2,1,0:T(8,128)} %bitcast.18), channel_id=1, source_target_pairs={{0,1},{1,0},{2,3},{3,2},{4,5},{5,4},{6,7},{7,6},{8,9},{9,8},{10,11... | collective-permute-start | bytes 4718600 | tf_op jit(solution)/shard_map/ppermute | solution.py:261
  78.9 1.0 copy-start.3
  79.9 1.1 copy-start.10
  90.7 3.8 %collective-permute-start.11 = (f32[4,64,1536]{2,1,0:T(8,128)S(1)}, f32[4,64,1536]{2,1,0:T(8,128)S(1)}, u32[]{:S(2)}, u32[]{:S(2)}) collective-permute-start(f32[4,64,1536]{2,1,0:T(8,128)S(1)} %bitcast.17), channel_id=1, source_target_pairs={{0,1},{1,0},{2,3},{3,2},{4,5},{5,4},{6,7},{7,6},{8,9},{9,8},{10,11... | collective-permute-start | bytes 4718600 | tf_op jit(solution)/shard_map/ppermute | solution.py:261
  91.3 21.8 %collective-permute-start.15 = (bf16[128,3072]{1,0:T(8,128)(2,1)}, bf16[128,3072]{1,0:T(8,128)(2,1)S(1)}, u32[]{:S(2)}, u32[]{:S(2)}) collective-permute-start(bf16[128,3072]{1,0:T(8,128)(2,1)} %collective-permute-done.9.refs_3_), channel_id=1, source_target_pairs={{0,16},{16,32},{32,48},{48,0},{64,80},{80,96},{96,112},{112,64},{1... | collective-permute-start | bytes 2359304 | tf_op jit(solution)/shard_map/ppermute | solution.py:65
  91.3 21.9 %collective-permute-start.16 = (bf16[128,3072]{1,0:T(8,128)(2,1)}, bf16[128,3072]{1,0:T(8,128)(2,1)}, u32[]{:S(2)}, u32[]{:S(2)}) collective-permute-start(bf16[128,3072]{1,0:T(8,128)(2,1)} %collective-permute-done.9.refs_3_), channel_id=1, source_target_pairs={{0,48},{16,0},{32,16},{48,32},{64,112},{80,64},{96,80},{112,96},{1... | collective-permute-start | bytes 2359304 | tf_op jit(solution)/shard_map/ppermute | solution.py:65
  94.5 51.2 %collective-permute-start.20 = (bf16[1024,1536]{1,0:T(8,128)(2,1)}, bf16[1024,1536]{1,0:T(8,128)(2,1)}, u32[]{:S(2)}, u32[]{:S(2)}) collective-permute-start(bf16[1024,1536]{1,0:T(8,128)(2,1)} %bitcast.5.refs_4_), channel_id=1, source_target_pairs={{0,1},{1,0},{2,3},{3,2},{4,5},{5,4},{6,7},{7,6},{8,9},{9,8},{10,11... | collective-permute-start | bytes 9437192 | tf_op jit(solution)/shard_map/ppermute | solution.py:377
  96.8 48.9 %all-to-all-start.1 = ((f32[8,64,1536]{2,1,0:T(8,128)}), f32[8,64,1536]{2,1,0:T(8,128)}, u32[]{:S(2)}, u32[]{:S(2)}) async-start(f32[8,64,1536]{2,1,0:T(8,128)} %chips.2), calls=%async_computation.1 | async-start | bytes 6291456 | tf_op jit(solution)/shard_map/all_to_all | solution.py:284
  104.3 23.4 %collective-permute-start.13 = (bf16[64,3072]{1,0:T(8,128)(2,1)S(1)}, bf16[64,3072]{1,0:T(8,128)(2,1)S(1)}, u32[]{:S(2)}, u32[]{:S(2)}) collective-permute-start(bf16[64,3072]{1,0:T(8,128)(2,1)S(1)} %slice.36), channel_id=1, source_target_pairs={{0,16},{16,32},{32,48},{48,0},{64,80},{80,96},{96,112},{112,64},{1... | collective-permute-start | bytes 1179656 | tf_op jit(solution)/shard_map/ppermute | solution.py:65
  104.4 23.4 %collective-permute-start.14 = (bf16[64,3072]{1,0:T(8,128)(2,1)S(1)}, bf16[64,3072]{1,0:T(8,128)(2,1)S(1)}, u32[]{:S(2)}, u32[]{:S(2)}) collective-permute-start(bf16[64,3072]{1,0:T(8,128)(2,1)S(1)} %slice.37), channel_id=1, source_target_pairs={{0,48},{16,0},{32,16},{48,32},{64,112},{80,64},{96,80},{112,96},{1... | collective-permute-start | bytes 1179656 | tf_op jit(solution)/shard_map/ppermute | solution.py:65
  113.1 16.0 %collective-permute-start.17 = (bf16[64,3072]{1,0:T(8,128)(2,1)S(1)}, bf16[64,3072]{1,0:T(8,128)(2,1)S(1)}, u32[]{:S(2)}, u32[]{:S(2)}) collective-permute-start(bf16[64,3072]{1,0:T(8,128)(2,1)S(1)} %slice.40), channel_id=1, source_target_pairs={{0,16},{16,32},{32,48},{48,0},{64,80},{80,96},{96,112},{112,64},{1... | collective-permute-start | bytes 1179656 | tf_op jit(solution)/shard_map/ppermute | solution.py:65
  114.2 14.8 %collective-permute-start.18 = (bf16[64,3072]{1,0:T(8,128)(2,1)S(1)}, bf16[64,3072]{1,0:T(8,128)(2,1)S(1)}, u32[]{:S(2)}, u32[]{:S(2)}) collective-permute-start(bf16[64,3072]{1,0:T(8,128)(2,1)S(1)} %slice.41), channel_id=1, source_target_pairs={{0,48},{16,0},{32,16},{48,32},{64,112},{80,64},{96,80},{112,96},{1... | collective-permute-start | bytes 1179656 | tf_op jit(solution)/shard_map/ppermute | solution.py:65
  127.6 12.2 %collective-permute-start.12 = (f32[4,64,1536]{2,1,0:T(8,128)S(1)}, f32[4,64,1536]{2,1,0:T(8,128)S(1)}, u32[]{:S(2)}, u32[]{:S(2)}) collective-permute-start(f32[4,64,1536]{2,1,0:T(8,128)S(1)} %bitcast.16), channel_id=1, source_target_pairs={{0,1},{1,0},{2,3},{3,2},{4,5},{5,4},{6,7},{7,6},{8,9},{9,8},{10,11... | collective-permute-start | bytes 4718600 | tf_op jit(solution)/shard_map/ppermute | solution.py:261
  139.7 3.7 %collective-permute-start.19 = (f32[4,64,1536]{2,1,0:T(8,128)}, f32[4,64,1536]{2,1,0:T(8,128)S(1)}, u32[]{:S(2)}, u32[]{:S(2)}) collective-permute-start(f32[4,64,1536]{2,1,0:T(8,128)} %bitcast.19), channel_id=1, source_target_pairs={{0,1},{1,0},{2,3},{3,2},{4,5},{5,4},{6,7},{7,6},{8,9},{9,8},{10,11... | collective-permute-start | bytes 4718600 | tf_op jit(solution)/shard_map/ppermute | solution.py:261
  145.7 44.0 %all-to-all-start.2 = ((f32[8,64,1536]{2,1,0:T(8,128)}), f32[8,64,1536]{2,1,0:T(8,128)}, u32[]{:S(2)}, u32[]{:S(2)}) async-start(f32[8,64,1536]{2,1,0:T(8,128)} %chips.3), calls=%async_computation.2 | async-start | bytes 6291456 | tf_op jit(solution)/shard_map/all_to_all | solution.py:284
